TPU v7x, 32 devices: a whole 2x2x4 slice. The times are simulated.
32 devices in a mesh: batch: 4 (over y, x), head: 8 (over z, core).
Axes of the slice: x: 2, y: 2, z: 4, core: 2. Of those that a mesh axis runs over, the one named last changes fastest.
Arguments:
- tokens: bfloat16 [8, 1024, 2048], P('batch', 'head'), may hold values from -6 to 6
- segment_ids: int32 [8, 1024], P('batch'), may hold values from 0 to 3, as said below
- position_ids: int32 [8, 1024], P('batch'), may hold values from 0 to 1023, as said below
- w_query: bfloat16 [2048, 2048], P('batch', 'head'), may hold values from -0.125 to 0.125
- w_key: bfloat16 [2048, 2048], P('batch', 'head'), may hold values from -0.125 to 0.125
- w_value: bfloat16 [2048, 2048], P('batch', 'head'), may hold values from -0.125 to 0.125
- w_output: bfloat16 [2048, 2048], P('batch', 'head'), may hold values from -0.75 to 0.75
- w_gate: bfloat16 [2048, 8192], P('batch', 'head'), may hold values from -0.125 to 0.125
- w_up: bfloat16 [2048, 8192], P('batch', 'head'), may hold values from -0.125 to 0.125
- w_down: bfloat16 [2048, 8192], P('batch', 'head'), may hold values from -0.0625 to 0.0625
- attn_gain: bfloat16 [2048], P('batch'), may hold values from 0.099609375 to 1.8984375
- mlp_gain: bfloat16 [2048], P('batch'), may hold values from 0.099609375 to 1.8984375
- cotangent: bfloat16 [8, 1024, 2048], P('batch', 'head'), may hold values from -6 to 6
Outputs:
- layer_out: bfloat16 [8, 1024, 2048], P('batch', 'head')
- grad_input: float32 [8, 1024, 2048], P('batch', 'head')
- grad_query: float32 [2048, 2048], P('batch', 'head')
- grad_key: float32 [2048, 2048], P('batch', 'head')
- grad_value: float32 [2048, 2048], P('batch', 'head')
- grad_output: float32 [2048, 2048], P('batch', 'head')
- grad_gate: float32 [2048, 8192], P('batch', 'head')
- grad_up: float32 [2048, 8192], P('batch', 'head')
- grad_down: float32 [2048, 8192], P('batch', 'head')
- grad_attn_gain: float32 [2048], P('batch')
- grad_mlp_gain: float32 [2048], P('batch')
Inputs may be any that keep to these rules, and one draw needn't show every extreme that they name: `segment_ids`: within a row the ids start at 0, rise by one at each document's first token and never fall. In every aligned block of 2 rows, one row (which one is drawn from the seed) is a single document of all 1024 tokens, and the next row in the block (cyclically) is cut into documents of exactly 256 tokens; in all other rows documents have 256 to 512 tokens except the last of a row, which may be shorter. `position_ids`: the token's index counted from its document's first token.
All inputs are finite; a program needn't handle non-finite values.
Results may differ from a plain program's by a relative error of at most 0.02.
Values may be sent and summed in bfloat16 or wider, within the bound.
A program may use at most 184 MiB of HBM per device.

v0:
```python
import jax
import jax.numpy as jnp
from jax import lax
from jax.sharding import PartitionSpec as P

HEAD_DIM = 64


epsilon = 1e-05
rope_base = 130000.0
masked_value = -1000000000.0


def normed(values, gain):
    inv_root = lax.rsqrt(jnp.mean(values * values, axis=-1, keepdims=True) + epsilon)
    return values * inv_root * gain


def norm_back(values, gain, grad):
    inv_root = lax.rsqrt(jnp.mean(values * values, axis=-1, keepdims=True) + epsilon)
    unit = values * inv_root
    weighted = grad * gain
    grad_values = inv_root * (weighted - unit * jnp.mean(weighted * unit, axis=-1, keepdims=True))
    return (grad_values, grad * unit)


def rope_tables(positions):
    half_dim = HEAD_DIM // 2
    frequency = rope_base ** (-(jnp.arange(half_dim).astype(jnp.float32) * 2.0) / HEAD_DIM)
    angles = positions.astype(jnp.float32)[:, None] * frequency[None, :]
    return (jnp.cos(angles)[:, None, :], jnp.sin(angles)[:, None, :])


def rotate(values, cosine, sine):
    half_dim = values.shape[-1] // 2
    first_half = values[..., :half_dim]
    second = values[..., half_dim:]
    return jnp.concatenate(
        [first_half * cosine - second * sine, second * cosine + first_half * sine], axis=-1
    )


def contract_rows(left, right):
    return lax.dot_general(
        left, right, (((0,), (0,)), ((), ())), preferred_element_type=jnp.float32
    )


def contract_cols(left, right):
    return lax.dot_general(
        left, right, (((1,), (1,)), ((), ())), preferred_element_type=jnp.float32
    )


def fetch_weights(w_query, w_key, w_value, w_output, w_gate, w_up, w_down, attn_gain, mlp_gain):
    return (
        lax.all_gather(w_query, "batch", axis=0, tiled=True),
        lax.all_gather(w_key, "batch", axis=0, tiled=True),
        lax.all_gather(w_value, "batch", axis=0, tiled=True),
        lax.all_gather(w_output, "batch", axis=0, tiled=True),
        lax.all_gather(w_gate, "batch", axis=0, tiled=True),
        lax.all_gather(w_up, "batch", axis=0, tiled=True),
        lax.all_gather(w_down, "batch", axis=0, tiled=True),
        lax.all_gather(attn_gain, "batch", axis=0, tiled=True),
        lax.all_gather(mlp_gain, "batch", axis=0, tiled=True),
    )


def reduce_grads(grad_parts):
    gain_sums = lax.psum((grad_parts[7], grad_parts[8]), "head")
    return (
        lax.psum_scatter(
            grad_parts[0].astype(jnp.bfloat16), "batch", scatter_dimension=0, tiled=True
        ).astype(jnp.float32),
        lax.psum_scatter(
            grad_parts[1].astype(jnp.bfloat16), "batch", scatter_dimension=0, tiled=True
        ).astype(jnp.float32),
        lax.psum_scatter(
            grad_parts[2].astype(jnp.bfloat16), "batch", scatter_dimension=0, tiled=True
        ).astype(jnp.float32),
        lax.psum_scatter(
            grad_parts[3].astype(jnp.bfloat16), "batch", scatter_dimension=0, tiled=True
        ).astype(jnp.float32),
        lax.psum_scatter(
            grad_parts[4].astype(jnp.bfloat16), "batch", scatter_dimension=0, tiled=True
        ).astype(jnp.float32),
        lax.psum_scatter(
            grad_parts[5].astype(jnp.bfloat16), "batch", scatter_dimension=0, tiled=True
        ).astype(jnp.float32),
        lax.psum_scatter(
            grad_parts[6].astype(jnp.bfloat16), "batch", scatter_dimension=0, tiled=True
        ).astype(jnp.float32),
        lax.psum_scatter(
            gain_sums[0].astype(jnp.bfloat16), "batch", scatter_dimension=0, tiled=True
        ).astype(jnp.float32),
        lax.psum_scatter(
            gain_sums[1].astype(jnp.bfloat16), "batch", scatter_dimension=0, tiled=True
        ).astype(jnp.float32),
    )


def block_scores(query, key_rot, segments, block_start):
    block_len = query.shape[0]
    scores = jnp.einsum(
        "qhd,khd->hqk", query, key_rot, preferred_element_type=jnp.float32
    ) * HEAD_DIM ** (-0.5)
    query_index = block_start + jnp.arange(block_len)[:, None]
    key_index = jnp.arange(key_rot.shape[0])[None, :]
    same_doc = segments[block_start : block_start + block_len][:, None] == segments[None, :]
    return (scores, (same_doc & (key_index <= query_index))[None, :, :])


def attend_forward(query, key_rot, values, segments):
    length = query.shape[0]
    block_len = min(512, length)
    results = []
    log_sums = []
    for block_start in range(0, length, block_len):
        scores, allowed = block_scores(
            query[block_start : block_start + block_len], key_rot, segments, block_start
        )
        masked = jnp.where(allowed, scores, masked_value)
        row_max = jnp.max(masked, axis=-1, keepdims=True)
        weights_exp = jnp.exp(masked - row_max)
        row_total = jnp.sum(weights_exp, axis=-1, keepdims=True)
        probabilities = (weights_exp / row_total).astype(jnp.bfloat16)
        results.append(
            jnp.einsum("hqk,khd->qhd", probabilities, values, preferred_element_type=jnp.float32)
        )
        log_sums.append(row_max + jnp.log(row_total))
    return (jnp.concatenate(results, axis=0), log_sums)


def attend_backward(query, key_rot, values, segments, log_sums, grad_out):
    length = query.shape[0]
    block_len = min(512, length)
    inv_scale = HEAD_DIM ** (-0.5)
    query_grads = []
    key_grad = jnp.zeros(key_rot.shape, jnp.float32)
    value_grad = jnp.zeros(values.shape, jnp.float32)
    for block_number, block_start in enumerate(range(0, length, block_len)):
        query_block = query[block_start : block_start + block_len]
        scores, allowed = block_scores(query_block, key_rot, segments, block_start)
        probs_full = jnp.exp(jnp.where(allowed, scores, masked_value) - log_sums[block_number])
        grad_block = grad_out[block_start : block_start + block_len]
        grad_prob = jnp.einsum(
            "qhd,khd->hqk", grad_block, values, preferred_element_type=jnp.float32
        )
        row_delta = jnp.sum(probs_full * grad_prob, axis=-1, keepdims=True)
        grad_score = (probs_full * (grad_prob - row_delta)).astype(jnp.bfloat16)
        query_grads.append(
            jnp.einsum("hqk,khd->qhd", grad_score, key_rot, preferred_element_type=jnp.float32)
            * inv_scale
        )
        key_grad = (
            key_grad
            + jnp.einsum(
                "hqk,qhd->khd", grad_score, query_block, preferred_element_type=jnp.float32
            )
            * inv_scale
        )
        value_grad = value_grad + jnp.einsum(
            "hqk,qhd->khd",
            probs_full.astype(jnp.bfloat16),
            grad_block,
            preferred_element_type=jnp.float32,
        )
    return (jnp.concatenate(query_grads, axis=0), key_grad, value_grad)


def per_device(
    tokens,
    segment_ids,
    position_ids,
    w_query,
    w_key,
    w_value,
    w_output,
    w_gate,
    w_up,
    w_down,
    attn_gain,
    mlp_gain,
    cotangent,
):
    row_count = tokens.shape[0]
    local_len = tokens.shape[1]
    offset = lax.axis_index("head") * local_len
    accumulated = None
    outputs = []
    input_grads = []
    for row_index in range(row_count):
        gathered = fetch_weights(
            w_query, w_key, w_value, w_output, w_gate, w_up, w_down, attn_gain, mlp_gain
        )
        query_w, key_w, value_w, output_w, gate_w, up_w, down_w = gathered[:7]
        gain_one = gathered[7].astype(jnp.float32)
        gain_two = gathered[8].astype(jnp.float32)
        segments = segment_ids[row_index]
        cosine, sine = rope_tables(position_ids[row_index])
        inputs = tokens[row_index].astype(jnp.float32)
        attn_in = lax.all_gather(
            normed(inputs, gain_one).astype(jnp.bfloat16), "head", axis=0, tiled=True
        )
        length = attn_in.shape[0]
        heads_here = query_w.shape[1] // HEAD_DIM
        head_shape = (length, heads_here, HEAD_DIM)
        query_lin = jnp.dot(attn_in, query_w, preferred_element_type=jnp.float32).reshape(
            head_shape
        )
        key_lin = jnp.dot(attn_in, key_w, preferred_element_type=jnp.float32).reshape(head_shape)
        query = rotate(query_lin, cosine, sine).astype(jnp.bfloat16)
        key_rot = rotate(key_lin, cosine, sine).astype(jnp.bfloat16)
        values = (
            jnp.dot(attn_in, value_w, preferred_element_type=jnp.float32)
            .astype(jnp.bfloat16)
            .reshape(head_shape)
        )
        attended, log_sums = attend_forward(query, key_rot, values, segments)
        attended = attended.reshape(length, heads_here * HEAD_DIM).astype(jnp.bfloat16)
        attn_terms = contract_cols(attended, output_w)
        token_rows = jnp.arange(length)
        own_rows = (token_rows >= offset) & (token_rows < offset + local_len)
        placed = lax.dynamic_update_slice_in_dim(jnp.zeros_like(attn_terms), inputs, offset, 0)
        mixed_full = lax.psum(attn_terms + placed, "head")
        mixed = lax.dynamic_slice_in_dim(mixed_full, offset, local_len, 0)
        mlp_in = normed(mixed_full, gain_two).astype(jnp.bfloat16)
        gate_act = jnp.dot(mlp_in, gate_w, preferred_element_type=jnp.float32)
        up_act = jnp.dot(mlp_in, up_w, preferred_element_type=jnp.float32)
        hidden = (jax.nn.silu(gate_act) * up_act).astype(jnp.bfloat16)
        mlp_terms = contract_cols(hidden, down_w)
        result = mixed + lax.psum_scatter(
            mlp_terms.astype(jnp.bfloat16), "head", scatter_dimension=0, tiled=True
        ).astype(jnp.float32)
        outputs.append(result.astype(jnp.bfloat16))
        grad_row = cotangent[row_index]
        grad_full = lax.all_gather(grad_row, "head", axis=0, tiled=True)
        grad_down = contract_rows(grad_full, hidden)
        grad_hidden = jnp.dot(grad_full, down_w, preferred_element_type=jnp.float32)
        _, pull_swish = jax.vjp(
            lambda gate_in, up_in: jax.nn.silu(gate_in) * up_in, gate_act, up_act
        )
        grad_gate_act, grad_up_act = pull_swish(grad_hidden)
        grad_gate_act = grad_gate_act.astype(jnp.bfloat16)
        grad_up_act = grad_up_act.astype(jnp.bfloat16)
        grad_gate = contract_rows(mlp_in, grad_gate_act)
        grad_up = contract_rows(mlp_in, grad_up_act)
        mlp_in_terms = contract_cols(grad_gate_act, gate_w) + contract_cols(grad_up_act, up_w)
        grad_mlp_in = lax.psum(mlp_in_terms, "head")
        grad_from_norm, gain_terms = norm_back(mixed_full, gain_two, grad_mlp_in)
        gain_two_grad = jnp.sum(jnp.where(own_rows[:, None], gain_terms, 0.0), axis=0)
        grad_mixed_full = grad_full.astype(jnp.float32) + grad_from_norm
        grad_mixed = lax.dynamic_slice_in_dim(grad_mixed_full, offset, local_len, 0)
        grad_att = grad_mixed_full.astype(jnp.bfloat16)
        grad_output = contract_rows(grad_att, attended)
        grad_attended = (
            jnp.dot(grad_att, output_w, preferred_element_type=jnp.float32)
            .astype(jnp.bfloat16)
            .reshape(head_shape)
        )
        query_rot_grad, key_rot_grad, value_rot_grad = attend_backward(
            query, key_rot, values, segments, log_sums, grad_attended
        )
        _, pull_rope = jax.vjp(
            lambda query_in, key_in: (rotate(query_in, cosine, sine), rotate(key_in, cosine, sine)),
            query_lin,
            key_lin,
        )
        query_pre_grad, key_pre_grad = pull_rope((query_rot_grad, key_rot_grad))
        query_grad_b = query_pre_grad.reshape(length, heads_here * HEAD_DIM).astype(jnp.bfloat16)
        key_grad_b = key_pre_grad.reshape(length, heads_here * HEAD_DIM).astype(jnp.bfloat16)
        value_grad_b = value_rot_grad.reshape(length, heads_here * HEAD_DIM).astype(jnp.bfloat16)
        grad_query = contract_rows(attn_in, query_grad_b)
        grad_key = contract_rows(attn_in, key_grad_b)
        grad_value = contract_rows(attn_in, value_grad_b)
        attn_in_terms = (
            contract_cols(query_grad_b, query_w)
            + contract_cols(key_grad_b, key_w)
            + contract_cols(value_grad_b, value_w)
        )
        grad_attn_in = lax.psum_scatter(
            attn_in_terms.astype(jnp.bfloat16), "head", scatter_dimension=0, tiled=True
        ).astype(jnp.float32)
        grad_from_first, first_terms = norm_back(inputs, gain_one, grad_attn_in)
        input_grads.append(grad_mixed + grad_from_first)
        grad_parts = (
            grad_query,
            grad_key,
            grad_value,
            grad_output,
            grad_gate,
            grad_up,
            grad_down,
            jnp.sum(first_terms, axis=0),
            gain_two_grad,
        )
        if accumulated is None:
            accumulated = grad_parts
        else:
            accumulated = jax.tree.map(jnp.add, accumulated, grad_parts)
    reduced = reduce_grads(accumulated)
    return (
        jnp.stack(outputs),
        jnp.stack(input_grads),
        reduced[0],
        reduced[1],
        reduced[2],
        reduced[3],
        reduced[4],
        reduced[5],
        reduced[6],
        reduced[7],
        reduced[8],
    )


def solution(mesh):
    placed = (
        P("batch", "head", None),
        P("batch", None),
        P("batch", None),
        P("batch", "head"),
        P("batch", "head"),
        P("batch", "head"),
        P("batch", "head"),
        P("batch", "head"),
        P("batch", "head"),
        P("batch", "head"),
        P("batch"),
        P("batch"),
        P("batch", "head", None),
    )
    return jax.shard_map(
        per_device,
        mesh=mesh,
        in_specs=placed,
        out_specs=(
            P("batch", "head", None),
            P("batch", "head", None),
            P("batch", "head"),
            P("batch", "head"),
            P("batch", "head"),
            P("batch", "head"),
            P("batch", "head"),
            P("batch", "head"),
            P("batch", "head"),
            P("batch"),
            P("batch"),
        ),
        check_vma=False,
    )
```

profile of v0, /device:TPU:0, one launch (start us, length us, event | category | flops | bytes accessed | tf_op | source)
XLA Modules:
  0.0 1740.1 jit_solution(4648591317237889378)
XLA Ops:
  39.2 49.3 %all-gather.32.cloned.1.call-done = bf16[1024,2048]{1,0:T(8,128)(2,1)} async-done(((bf16[128,2048]{1,0:T(8,128)(2,1)}), bf16[1024,2048]{1,0:T(8,128)(2,1)}) %all-gather.32.cloned.1.call-update) | async-done | bytes 4194320 | tf_op jit(solution)/shard_map/all_gather | solution.py:202
  92.4 23.4 %all-gather.20.cloned.1.call-done = bf16[2048,256]{1,0:T(8,128)(2,1)} async-done(((bf16[512,256]{1,0:T(8,128)(2,1)}), bf16[2048,256]{1,0:T(8,128)(2,1)}) %all-gather.20.cloned.1.call-update) | async-done | bytes 1048592 | tf_op jit(solution)/shard_map/all_gather | solution.py:57
  129.6 14.5 all-gather.18.cloned.1.call-done
  157.5 35.8 %all-gather.16.cloned.1.call-done = bf16[1024,2048]{1,0:T(8,128)(2,1)} async-done(((bf16[128,2048]{1,0:T(8,128)(2,1)}), bf16[1024,2048]{1,0:T(8,128)(2,1)}) %all-gather.16.cloned.1.call-update) | async-done | bytes 4194320 | tf_op jit(solution)/shard_map/all_gather | solution.py:202
  246.3 321.9 %all-reduce.19.cloned.1.call-done = (f32[1024,2048]{1,0:T(8,128)}, f32[1024,2048]{1,0:T(8,128)}) async-done(((f32[1024,2048]{1,0:T(8,128)}, f32[1024,2048]{1,0:T(8,128)}), (f32[1024,2048]{1,0:T(8,128)}, f32[1024,2048]{1,0:T(8,128)})) %all-reduce.19.cloned.1.call-update) | async-done | bytes 16777232 | tf_op jit(solution)/shard_map/psum | solution.py:225
  581.0 41.9 %all-gather.28.cloned.1.call-done = bf16[2048,1024]{1,0:T(8,128)(2,1)} async-done(((bf16[512,1024]{1,0:T(8,128)(2,1)}), bf16[2048,1024]{1,0:T(8,128)(2,1)}) %all-gather.28.cloned.1.call-update) | async-done | bytes 4194320 | tf_op jit(solution)/shard_map/all_gather | solution.py:62
  632.8 44.7 %all-gather.26.cloned.1.call-done = bf16[2048,1024]{1,0:T(8,128)(2,1)} async-done(((bf16[512,1024]{1,0:T(8,128)(2,1)}), bf16[2048,1024]{1,0:T(8,128)(2,1)}) %all-gather.26.cloned.1.call-update) | async-done | bytes 4194320 | tf_op jit(solution)/shard_map/all_gather | solution.py:61
  687.5 44.4 %all-gather.30.cloned.1.call-done = bf16[2048,1024]{1,0:T(8,128)(2,1)} async-done(((bf16[512,1024]{1,0:T(8,128)(2,1)}), bf16[2048,1024]{1,0:T(8,128)(2,1)}) %all-gather.30.cloned.1.call-update) | async-done | bytes 4194320 | tf_op jit(solution)/shard_map/all_gather | solution.py:63
  731.9 49.4 %all-gather.36.cloned.1.call-done = bf16[1,1024,2048]{2,1,0:T(8,128)(2,1)} async-done(((bf16[1,128,2048]{2,1,0:T(8,128)(2,1)}), bf16[1,1024,2048]{2,1,0:T(8,128)(2,1)}) %all-gather.36.cloned.1.call-update) | async-done | bytes 4194320 | tf_op jit(solution)/shard_map/all_gather | solution.py:237
  781.3 13.2 multiply_convert_fusion.6
  813.9 15.3 all-gather.34.cloned.1.call-done
  829.2 13.2 multiply_convert_fusion.7
  922.2 273.4 %all-reduce.17.cloned.1.call-done = (f32[1024,2048]{1,0:T(8,128)}, f32[1024,2048]{1,0:T(8,128)}) async-done(((f32[1024,2048]{1,0:T(8,128)}, f32[1024,2048]{1,0:T(8,128)}), (f32[1024,2048]{1,0:T(8,128)}, f32[1024,2048]{1,0:T(8,128)})) %all-reduce.17.cloned.1.call-update) | async-done | bytes 16777232 | tf_op jit(solution)/shard_map/psum | solution.py:249
  1195.6 14.7 select_reduce_fusion.1
  1210.3 22.6 %multiply_add_fusion.1 = (f32[1024,2048]{1,0:T(8,128)}, f32[1024,2048]{1,0:T(8,128)}) fusion(f32[1024,2048]{1,0:T(8,128)} %get-tuple-element.50, f32[1024,2048]{1,0:T(8,128)} %get-tuple-element.52, bf16[1,1024,2048]{2,1,0:T(8,128)(2,1)} %all-gather.34.cloned.1.call-done, f32[1024]{0:T(1024)S(1)} %broadcast_multiply_fusion.1, f32[2048]{0:T(1024)S(1)} %bitcast.256, ...), kind=kLoop, calls=%fused_computation.21 | loop fusion | flops 29360128 | bytes 58744832 | tf_op jit(solution)/shard_map/add | solution.py:252
  1370.4 44.5 %reduce-scatter.12.cloned.1.call-done = bf16[128,2048]{1,0:T(8,128)(2,1)} async-done(((bf16[1024,2048]{1,0:T(8,128)(2,1)}), bf16[128,2048]{1,0:T(8,128)(2,1)}) %reduce-scatter.12.cloned.1.call-update) | async-done | bytes 524304 | tf_op jit(solution)/shard_map/reduce_scatter | solution.py:232
  1416.4 48.9 %reduce-scatter.14.cloned.1.call-done = bf16[128,2048]{1,0:T(8,128)(2,1)} async-done(((bf16[1024,2048]{1,0:T(8,128)(2,1)}), bf16[128,2048]{1,0:T(8,128)(2,1)}) %reduce-scatter.14.cloned.1.call-update) | async-done | bytes 524304 | tf_op jit(solution)/shard_map/reduce_scatter | solution.py:232
  1467.8 26.5 %reduce-scatter.26.cloned.1.call-done = bf16[512,256]{1,0:T(8,128)(2,1)} async-done(((bf16[2048,256]{1,0:T(8,128)(2,1)}), bf16[512,256]{1,0:T(8,128)(2,1)}) %reduce-scatter.26.cloned.1.call-update) | async-done | bytes 262160 | tf_op jit(solution)/shard_map/reduce_scatter | solution.py:81
  1496.1 28.7 %reduce-scatter.24.cloned.1.call-done = bf16[512,256]{1,0:T(8,128)(2,1)} async-done(((bf16[2048,256]{1,0:T(8,128)(2,1)}), bf16[512,256]{1,0:T(8,128)(2,1)}) %reduce-scatter.24.cloned.1.call-update) | async-done | bytes 262160 | tf_op jit(solution)/shard_map/reduce_scatter | solution.py:78
  1526.6 29.2 %reduce-scatter.22.cloned.1.call-done = bf16[512,256]{1,0:T(8,128)(2,1)} async-done(((bf16[2048,256]{1,0:T(8,128)(2,1)}), bf16[512,256]{1,0:T(8,128)(2,1)}) %reduce-scatter.22.cloned.1.call-update) | async-done | bytes 262160 | tf_op jit(solution)/shard_map/reduce_scatter | solution.py:75
  1557.5 29.4 %reduce-scatter.20.cloned.1.call-done = bf16[512,256]{1,0:T(8,128)(2,1)} async-done(((bf16[2048,256]{1,0:T(8,128)(2,1)}), bf16[512,256]{1,0:T(8,128)(2,1)}) %reduce-scatter.20.cloned.1.call-update) | async-done | bytes 262160 | tf_op jit(solution)/shard_map/reduce_scatter | solution.py:72
  1588.7 50.7 %reduce-scatter.18.cloned.1.call-done = bf16[128,2048]{1,0:T(8,128)(2,1)} async-done(((bf16[1024,2048]{1,0:T(8,128)(2,1)}), bf16[128,2048]{1,0:T(8,128)(2,1)}) %reduce-scatter.18.cloned.1.call-update) | async-done | bytes 524304 | tf_op jit(solution)/shard_map/reduce_scatter | solution.py:281
  1639.4 50.4 %reduce-scatter.16.cloned.1.call-done = bf16[128,2048]{1,0:T(8,128)(2,1)} async-done(((bf16[1024,2048]{1,0:T(8,128)(2,1)}), bf16[128,2048]{1,0:T(8,128)(2,1)}) %reduce-scatter.16.cloned.1.call-update) | async-done | bytes 524304 | tf_op jit(solution)/shard_map/reduce_scatter | solution.py:281
  1691.8 25.9 %all-reduce.10 = (bf16[2048]{0:T(1024)(128)(2,1)S(1)}, bf16[2048]{0:T(1024)(128)(2,1)S(1)}) all-reduce(f32[2048]{0:T(1024)S(1)} %add.306, f32[2048]{0:T(1024)S(1)} %add.308), channel_id=1, replica_groups=mesh['batch'=4,'head'=8] {'head'}, use_global_device_ids=true, to_apply=%region_37.38 | all-reduce | flops 4096 | bytes 24576 | tf_op jit(solution)/shard_map/psum | solution.py:70
  (487 shorter events, 410.9 us)
Async XLA Ops:
  7.2 32.0 %all-gather.22.cloned.1.call-start = ((), (), s32[]{:S(2)}) async-start(), calls=%async_computation.14 | async-start | bytes 1310720 | tf_op jit(solution)/shard_map/all_gather | solution.py:58
  7.9 80.7 %all-gather.32.cloned.1.call-start = ((), (), s32[]{:S(2)}) async-start(), calls=%async_computation.20 | async-start | bytes 4718592 | tf_op jit(solution)/shard_map/all_gather | solution.py:202
  22.3 93.5 %all-gather.20.cloned.1.call-start = ((), (), s32[]{:S(2)}) async-start(), calls=%async_computation.13 | async-start | bytes 1310720 | tf_op jit(solution)/shard_map/all_gather | solution.py:57
  23.0 121.1 %all-gather.18.cloned.1.call-start = ((), (), s32[]{:S(2)}) async-start(), calls=%async_computation.12 | async-start | bytes 1310720 | tf_op jit(solution)/shard_map/all_gather | solution.py:59
  23.6 169.7 %all-gather.16.cloned.1.call-start = ((), (), s32[]{:S(2)}) async-start(), calls=%async_computation.11 | async-start | bytes 4718592 | tf_op jit(solution)/shard_map/all_gather | solution.py:202
  24.2 196.5 %all-gather.24.cloned.1.call-start = ((), (), s32[]{:S(2)}) async-start(), calls=%async_computation.15 | async-start | bytes 1310720 | tf_op jit(solution)/shard_map/all_gather | solution.py:60
  24.8 543.4 %all-reduce.19.cloned.1.call-start = ((), (), s32[]{:S(2)}) async-start(), calls=%async_computation.34 | async-start | bytes 33554432 | tf_op jit(solution)/shard_map/psum | solution.py:225
  234.5 388.4 %all-gather.28.cloned.1.call-start = ((), (), s32[]{:S(2)}) async-start(), calls=%async_computation.17 | async-start | bytes 5242880 | tf_op jit(solution)/shard_map/all_gather | solution.py:62
  235.2 442.2 %all-gather.26.cloned.1.call-start = ((), (), s32[]{:S(2)}) async-start(), calls=%async_computation.16 | async-start | bytes 5242880 | tf_op jit(solution)/shard_map/all_gather | solution.py:61
  236.0 495.9 %all-gather.30.cloned.1.call-start = ((), (), s32[]{:S(2)}) async-start(), calls=%async_computation.18 | async-start | bytes 5242880 | tf_op jit(solution)/shard_map/all_gather | solution.py:63
  236.5 544.7 %all-gather.36.cloned.1.call-start = ((), (), s32[]{:S(2)}) async-start(), calls=%async_computation.32 | async-start | bytes 4718592 | tf_op jit(solution)/shard_map/all_gather | solution.py:237
  237.7 591.5 %all-gather.34.cloned.1.call-start = ((), (), s32[]{:S(2)}) async-start(), calls=%async_computation.31 | async-start | bytes 4718592 | tf_op jit(solution)/shard_map/all_gather | solution.py:237
  238.2 957.3 %all-reduce.17.cloned.1.call-start = ((), (), s32[]{:S(2)}) async-start(), calls=%async_computation.33 | async-start | bytes 33554432 | tf_op jit(solution)/shard_map/psum | solution.py:249
  863.1 499.1 %reduce-scatter.32.cloned.1.call-start = ((), (), s32[]{:S(2)}) async-start(), calls=%async_computation.30 | async-start | bytes 5242880 | tf_op jit(solution)/shard_map/reduce_scatter | solution.py:90
  876.2 488.6 %reduce-scatter.30.cloned.1.call-start = ((), (), s32[]{:S(2)}) async-start(), calls=%async_computation.29 | async-start | bytes 5242880 | tf_op jit(solution)/shard_map/reduce_scatter | solution.py:87
  889.7 477.9 %reduce-scatter.28.cloned.1.call-start = ((), (), s32[]{:S(2)}) async-start(), calls=%async_computation.28 | async-start | bytes 5242880 | tf_op jit(solution)/shard_map/reduce_scatter | solution.py:84
  903.4 511.4 %reduce-scatter.12.cloned.1.call-start = ((), (), s32[]{:S(2)}) async-start(), calls=%async_computation.19 | async-start | bytes 4718592 | tf_op jit(solution)/shard_map/reduce_scatter | solution.py:232
  912.9 552.3 %reduce-scatter.14.cloned.1.call-start = ((), (), s32[]{:S(2)}) async-start(), calls=%async_computation.21 | async-start | bytes 4718592 | tf_op jit(solution)/shard_map/reduce_scatter | solution.py:232
  922.1 572.2 %reduce-scatter.26.cloned.1.call-start = ((), (), s32[]{:S(2)}) async-start(), calls=%async_computation.27 | async-start | bytes 1310720 | tf_op jit(solution)/shard_map/reduce_scatter | solution.py:81
  1303.7 221.1 %reduce-scatter.24.cloned.1.call-start = ((), (), s32[]{:S(2)}) async-start(), calls=%async_computation.26 | async-start | bytes 1310720 | tf_op jit(solution)/shard_map/reduce_scatter | solution.py:78
  1326.5 229.2 %reduce-scatter.22.cloned.1.call-start = ((), (), s32[]{:S(2)}) async-start(), calls=%async_computation.25 | async-start | bytes 1310720 | tf_op jit(solution)/shard_map/reduce_scatter | solution.py:75
  1339.5 247.5 %reduce-scatter.20.cloned.1.call-start = ((), (), s32[]{:S(2)}) async-start(), calls=%async_computation.24 | async-start | bytes 1310720 | tf_op jit(solution)/shard_map/reduce_scatter | solution.py:72
  1346.5 292.9 %reduce-scatter.18.cloned.1.call-start = ((), (), s32[]{:S(2)}) async-start(), calls=%async_computation.23 | async-start | bytes 4718592 | tf_op jit(solution)/shard_map/reduce_scatter | solution.py:281
  1352.8 337.0 %reduce-scatter.16.cloned.1.call-start = ((), (), s32[]{:S(2)}) async-start(), calls=%async_computation.22 | async-start | bytes 4718592 | tf_op jit(solution)/shard_map/reduce_scatter | solution.py:281
  (145 other events, 3517.4 us)
Sparse Core Ops, SparseCore 0:
  9.9 29.3 all-gather.21
  41.4 47.1 all-gather.31
  90.4 25.3 all-gather.19
  117.5 26.6 all-gather.17
  146.2 47.0 all-gather.15
  195.0 25.6 all-gather.23
  234.6 333.5 all-reduce.18
  570.0 52.7 all-gather.27
  624.7 52.6 all-gather.25
  679.1 52.6 all-gather.29
  734.1 47.1 all-gather.35
  783.3 45.8 all-gather.33
  863.2 332.2 all-reduce.16
  1198.4 52.7 reduce-scatter.31
  1254.3 52.6 reduce-scatter.29
  1309.8 52.6 reduce-scatter.27
  1364.8 49.9 reduce-scatter.11
  1417.1 48.1 reduce-scatter.13
  1468.4 25.8 reduce-scatter.25
  1497.1 27.6 reduce-scatter.23
  1528.0 27.7 reduce-scatter.21
  1559.2 27.6 reduce-scatter.19
  1589.4 49.9 reduce-scatter.17
  1641.6 48.1 reduce-scatter.15
where the time goes:
time: 1740 us
  waiting for transfers between devices  1250 us (72%)
  matrix products  281 us (16%)
  other arithmetic  114 us (7%)
  blocking collectives  53.4 us (3%)
  local copies, waits for them, and re-layouts  26.4 us (2%)
    psum x1, waiting for transfers between devices, per_device(): mixed_full = lax.psum(attn_terms + placed, 'head')  322 us
    psum x1, waiting for transfers between devices, per_device(): grad_mlp_in = lax.psum(mlp_in_terms, 'head')  273 us
    reduce_scatter x2, waiting for transfers between devices, per_device(): lax.psum_scatter(attn_in_terms.astype(jnp.bfloat16), 'head', scatter_dime...  101 us
    reduce_scatter x2, waiting for transfers between devices, per_device(): lax.psum_scatter(mlp_terms.astype(jnp.bfloat16), 'head', scatter_dimensio...  93.4 us
    all_gather x2, waiting for transfers between devices, per_device(): lax.all_gather(normed(inputs, gain_one).astype(jnp.bfloat16), 'head', axi...  85.1 us
    dot_general x14, matrix products, contract_cols(): lax.dot_general(left, right, (((1,), (1,)), ((), ())), preferred_element_...  69.3 us
    all_gather x2, waiting for transfers between devices, per_device(): grad_full = lax.all_gather(grad_row, 'head', axis=0, tiled=True)  64.6 us
    dot_general x14, matrix products, contract_rows(): lax.dot_general(left, right, (((0,), (0,)), ((), ())), preferred_element_...  57.6 us
  transfers between devices with their start and end apart: 24, of which 21 were waited for; matrix products, arithmetic and copies ran while one was open for 20% of the time, Pallas kernels for 0%

commit v1 on v0

v1 whole, which is shorter than its diff:
```python
import functools

import jax
import jax.numpy as jnp
from jax import lax
from jax.experimental import pallas as pl
from jax.experimental.pallas import tpu as pltpu
from jax.sharding import PartitionSpec as P

HEAD_DIM = 64
epsilon = 1e-05
rope_base = 130000.0
masked_value = -1000000000.0
MESH = pl.DeviceIdType.MESH
F32 = jnp.float32
BF16 = jnp.bfloat16
DMA = pltpu.SemaphoreType.DMA
ANY = pl.BlockSpec(memory_space=pl.ANY)
VMEM = pl.BlockSpec(memory_space=pltpu.VMEM)
VMEM_LIMIT = 60 * 2**20


class Place:
    def __init__(self, batch, head):
        self.n, self.H = batch, head
        self.L = head // 2
        self.b = lax.axis_index("batch")
        self.h = lax.axis_index("head")
        self.z = self.h // 2
        self.c = self.h % 2
        self.sib = self.z * 2 + (1 - self.c)
        self.up = self.h + 2
        self.down = self.h - 2
        self.x, self.y = self.b % 2, self.b // 2
        self.xn = self.y * 2 + (1 - self.x)
        self.yn = (1 - self.y) * 2 + self.x
        self.dg = (1 - self.y) * 2 + (1 - self.x)
        self.square = batch == 4

    def greet(self, line=True, batch=True, all_heads=False):
        barrier = pltpu.get_barrier_semaphore()
        me, L = self, self.L

        def hello(device):
            pl.semaphore_signal(barrier, inc=1, device_id=device, device_id_type=MESH)

        count = 0
        if all_heads:
            for off in range(1, self.H):
                hello({"head": (me.h + off) % self.H})
                count += 1
        elif line:
            hello({"head": me.sib})
            count += 1

            @pl.when(me.z > 0)
            def _():
                hello({"head": me.down})

            @pl.when(me.z < L - 1)
            def _():
                hello({"head": me.up})

        if batch:
            if self.square and not all_heads:
                hello({"batch": me.xn})
                hello({"batch": me.yn})
                count += 2
            else:
                for off in range(1, self.n):
                    hello({"batch": (me.b + off) % self.n})
                    count += 1
        if line and not all_heads:
            count = count + jnp.minimum(me.z, 1) + jnp.minimum(L - 1 - me.z, 1)
        pl.semaphore_wait(barrier, count)


def remote(src, dst, ssem, rsem, device):
    return pltpu.make_async_remote_copy(
        src_ref=src, dst_ref=dst, send_sem=ssem, recv_sem=rsem, device_id=device, device_id_type=MESH
    )


class Gather:
    def __init__(self, at, own, out, sems):
        self.at, self.own, self.out = at, own, out
        self.line_recv, self.sib_recv, self.up_send, self.down_send, self.sib_send, self.local = sems

    @staticmethod
    def sems(at_L):
        return [DMA((at_L,))] * 5 + [DMA]

    def _up(self, zb, src):
        at = self.at
        return remote(src, self.out.at[zb * 2 + at.c], self.up_send.at[zb], self.line_recv.at[zb], {"head": at.up})

    def _down(self, zb, src):
        at = self.at
        return remote(src, self.out.at[zb * 2 + at.c], self.down_send.at[zb], self.line_recv.at[zb], {"head": at.down})

    def _sib(self, zb, src):
        at = self.at
        return remote(src, self.out.at[zb * 2 + at.c], self.sib_send.at[zb], self.sib_recv.at[zb], {"head": at.sib})

    def _mine(self):
        return pltpu.make_async_copy(self.own, self.out.at[self.at.h], self.local)

    def start(self):
        at = self.at

        @pl.when(at.z < at.L - 1)
        def _():
            self._up(at.z, self.own).start()

        @pl.when(at.z > 0)
        def _():
            self._down(at.z, self.own).start()

        self._sib(at.z, self.own).start()
        self._mine().start()

    def step(self, k):
        at = self.at
        below, above = at.z - k, at.z + k

        @pl.when(below >= 0)
        def _():
            block = self.out.at[below * 2 + at.c]
            self._up(below, block).wait_recv()

            @pl.when(at.z < at.L - 1)
            def _():
                self._up(below, block).start()

            self._sib(below, block).start()

        @pl.when(above <= at.L - 1)
        def _():
            block = self.out.at[above * 2 + at.c]
            self._down(above, block).wait_recv()

            @pl.when(at.z > 0)
            def _():
                self._down(above, block).start()

            self._sib(above, block).start()

    def finish(self):
        at = self.at
        self._mine().wait()
        for zb in range(at.L):
            block = self.out.at[zb * 2 + at.c]
            self._sib(zb, block).wait_send()
            other = self.out.at[zb * 2 + 1 - at.c]
            remote(other, other, self.sib_send.at[zb], self.sib_recv.at[zb], {"head": at.sib}).wait_recv()

            @pl.when((zb <= at.z) & (at.z < at.L - 1))
            def _():
                self._up(zb, block).wait_send()

            @pl.when((zb >= at.z) & (at.z > 0))
            def _():
                self._down(zb, block).wait_send()


class Reduce:
    def __init__(self, at, src, own, sib, recv, sems):
        self.at, self.src, self.own, self.sib, self.recv = at, src, own, sib, recv
        self.load, self.sib_send, self.sib_recv, self.fwd_send, self.recv_sem = sems

    @staticmethod
    def sems(L):
        return [DMA((L,)), DMA((L,)), DMA((L,)), DMA((L,)), DMA((L + 1,))]

    @staticmethod
    def bufs(L, T, D):
        return [pltpu.VMEM((L, T, D), BF16), pltpu.VMEM((L, T, D), BF16), pltpu.VMEM((L + 1, T, D), BF16)]

    def _load(self, zd):
        return pltpu.make_async_copy(self.src.at[zd * 2 + self.at.c], self.own.at[zd], self.load.at[zd])

    def _sib(self, zd):
        at = self.at
        return remote(
            self.src.at[zd * 2 + 1 - at.c], self.sib.at[zd], self.sib_send.at[zd], self.sib_recv.at[zd], {"head": at.sib}
        )

    def _fwd(self, zd, slot, device):
        return remote(self.recv.at[zd], self.recv.at[slot], self.fwd_send.at[zd], self.recv_sem.at[slot], {"head": device})

    def start(self):
        at, L = self.at, self.at.L
        order = []
        for k in range((L + 1) // 2):
            order += [L - 1 - k] + ([k] if k != L - 1 - k else [])
        for zd in order:
            self._sib(zd).start()
            self._load(zd).start()

    def _chunks(self, fn):
        T = self.own.shape[1]
        step = 32 if T % 32 == 0 else T

        @pl.loop(0, T // step)
        def _(i):
            fn(pl.ds(pl.multiple_of(i * step, step), step))

    def _hop(self, zd, first, slot, device, which):
        @pl.when(first)
        def _():
            if which in ("first", "both"):
                self._load(zd).wait()
                self._sib(zd).wait_recv()

                def add(rows):
                    self.recv[zd, rows, :] = (self.own[zd, rows, :].astype(F32) + self.sib[zd, rows, :].astype(F32)).astype(
                        BF16
                    )

                self._chunks(add)
                self._fwd(zd, slot, device).start()

        @pl.when(jnp.logical_not(first))
        def _():
            if which in ("mid", "both"):
                self._load(zd).wait()
                self._sib(zd).wait_recv()
                self._fwd(zd, zd, device).wait_recv()

                def add(rows):
                    self.recv[zd, rows, :] = (
                        self.own[zd, rows, :].astype(F32)
                        + self.sib[zd, rows, :].astype(F32)
                        + self.recv[zd, rows, :].astype(F32)
                    ).astype(BF16)

                self._chunks(add)
                self._fwd(zd, slot, device).start()

    def hops(self, k, which="both"):
        at, L = self.at, self.at.L
        far, near = L - 1 - k, k

        @pl.when(far > at.z)
        def _():
            self._hop(far, at.z == 0, far, at.up, which)

        @pl.when(near < at.z)
        def _():
            self._hop(near, at.z == L - 1, jnp.where(at.z - 1 == near, L, near), at.down, which)

    def final(self, add):
        at, L = self.at, self.at.L
        z = at.z
        self._load(z).wait()
        self._sib(z).wait_recv()

        @pl.when(z > 0)
        def _():
            self._fwd(z, z, at.up).wait_recv()

        @pl.when(z < L - 1)
        def _():
            self._fwd(z, L, at.down).wait_recv()

        def base(rows):
            return self.own[z, rows, :].astype(F32) + self.sib[z, rows, :].astype(F32)

        @pl.when(z == 0)
        def _():
            self._chunks(lambda rows: add(rows, base(rows) + self.recv[L, rows, :].astype(F32)))

        @pl.when(z == L - 1)
        def _():
            self._chunks(lambda rows: add(rows, base(rows) + self.recv[z, rows, :].astype(F32)))

        @pl.when((z > 0) & (z < L - 1))
        def _():
            self._chunks(
                lambda rows: add(
                    rows, base(rows) + self.recv[z, rows, :].astype(F32) + self.recv[L, rows, :].astype(F32)
                )
            )

    def finish(self):
        at = self.at
        for zd in range(at.L):
            self._sib(zd).wait_send()

            @pl.when(zd != at.z)
            def _():
                self._fwd(zd, zd, at.up).wait_send()


class BatchGather:
    def __init__(self, at, own, out, sems):
        self.at, self.own, self.out = at, own, out
        self.send, self.recv, self.local = sems

    @staticmethod
    def sems(n):
        m = 4 if n == 4 else n
        return [DMA((m,)), DMA((m,)), DMA]

    def _half(self, b, i):
        half = self.own.shape[0] // 2
        return self.out(b, pl.ds(i * half, half))

    def _all(self, b):
        return self.out(b, pl.ds(0, self.own.shape[0]))

    def _direct(self, i, device):
        at = self.at
        return remote(self.own, self._all(at.b), self.send.at[i], self.recv.at[i], {"batch": device})

    def start(self):
        at = self.at
        pltpu.make_async_copy(self.own, self._all(at.b), self.local).start()
        if at.square:
            self._direct(0, at.xn).start()
            self._direct(1, at.yn).start()
        else:
            for off in range(1, at.n):
                remote(
                    self.own, self._all(at.b), self.send.at[off], self.recv.at[off], {"batch": (at.b + off) % at.n}
                ).start()

    def forward(self):
        at = self.at
        if at.square:
            block = self._all(at.xn)
            remote(block, block, self.send.at[0], self.recv.at[0], {"batch": at.xn}).wait_recv()
            half = self._half(at.xn, 0)
            remote(half, half, self.send.at[2], self.recv.at[2], {"batch": at.yn}).start()
            block = self._all(at.yn)
            remote(block, block, self.send.at[1], self.recv.at[1], {"batch": at.yn}).wait_recv()
            half = self._half(at.yn, 1)
            remote(half, half, self.send.at[3], self.recv.at[3], {"batch": at.xn}).start()

    def finish(self):
        at = self.at
        pltpu.make_async_copy(self.own, self._all(at.b), self.local).wait()
        if at.square:
            self._direct(0, at.xn).wait_send()
            self._direct(1, at.yn).wait_send()
            half = self._half(at.dg, 0)
            remote(half, half, self.send.at[2], self.recv.at[2], {"batch": at.yn}).wait()
            half = self._half(at.dg, 1)
            remote(half, half, self.send.at[3], self.recv.at[3], {"batch": at.xn}).wait()
        else:
            for off in range(1, at.n):
                block = self._all((at.b + at.n - off) % at.n)
                remote(block, block, self.send.at[off], self.recv.at[off], {"batch": (at.b + off) % at.n}).wait()


class BatchReduce:
    def __init__(self, at, src, bufs, sems, before=None):
        self.at, self.src, self.before = at, src, before
        if at.square:
            self.first, self.mine, self.second = bufs
        else:
            (self.slots,) = bufs
        self.send, self.recv, self.load = sems

    @staticmethod
    def sems(n):
        m = 6 if n == 4 else n
        return [DMA((m,)), DMA((m,)), DMA((4,))]

    @staticmethod
    def bufs(n, R, K):
        if n == 4:
            return [
                pltpu.VMEM((4, R // 2, K), BF16),
                pltpu.VMEM((4, R // 2, K), BF16),
                pltpu.VMEM((2, R // 2, K), BF16),
            ]
        return [pltpu.VMEM((n, R, K), BF16)]

    def _first(self, i):
        at, half = self.at, self.src.shape[1] // 2
        if i < 2:
            src = self.src.at[i * 2 + 1 - at.x, pl.ds(0, half), :]
            device = {"batch": at.xn}
        else:
            src = self.src.at[(1 - at.y) * 2 + i - 2, pl.ds(half, half), :]
            device = {"batch": at.yn}
        return remote(src, self.first.at[i], self.send.at[i], self.recv.at[i], device)

    def _taken(self, i):
        if self.before is None:
            return self._first(i)
        return pltpu.make_async_copy(self.before.at[i], self.first.at[i], self.recv.at[i])

    def _load(self, i):
        at, half = self.at, self.src.shape[1] // 2
        if i < 2:
            src = self.src.at[i * 2 + at.x, pl.ds(0, half), :]
        else:
            src = self.src.at[at.y * 2 + i - 2, pl.ds(half, half), :]
        return pltpu.make_async_copy(src, self.mine.at[i], self.load.at[i])

    def _second(self, j):
        at = self.at
        if j == 0:
            return remote(
                self.mine.at[1 - at.y], self.second.at[0], self.send.at[4], self.recv.at[4], {"batch": at.yn}
            )
        return remote(self.mine.at[3 - at.x], self.second.at[1], self.send.at[5], self.recv.at[5], {"batch": at.xn})

    def _direct(self, off):
        at = self.at
        to = (at.b + off) % at.n
        return remote(self.src.at[to], self.slots.at[off], self.send.at[off], self.recv.at[off], {"batch": to})

    def start(self):
        at = self.at
        if at.square:
            for i in (0, 2, 1, 3):
                self._taken(i).start()
                self._load(i).start()
        else:
            for off in range(1, at.n):
                self._direct(off).start()
            pltpu.make_async_copy(self.src.at[at.b], self.slots.at[0], self.load.at[0]).start()

    def _chunks(self, R, fn):
        step = 16

        @pl.loop(0, R // step)
        def _(i):
            fn(pl.multiple_of(i * step, step), step)

    def second_step(self):
        at = self.at
        if at.square:
            for i in range(4):
                self._load(i).wait()
                if self.before is None:
                    self._first(i).wait_recv()
                else:
                    self._taken(i).wait()
            for j, i in ((0, 1 - at.y), (1, 3 - at.x)):

                def add(r, step, i=i):
                    rows = pl.ds(r, step)
                    self.mine[i, rows, :] = (
                        self.mine[i, rows, :].astype(F32) + self.first[i, rows, :].astype(F32)
                    ).astype(BF16)

                self._chunks(self.mine.shape[1], add)
                self._second(j).start()

    def final(self, put):
        at = self.at
        if at.square:
            half = self.src.shape[1] // 2
            for j, i in ((0, at.y), (1, 2 + at.x)):
                self._second(j).wait_recv()

                def add(r, step, i=i, j=j):
                    rows = pl.ds(r, step)
                    put(
                        pl.ds(r + j * half, step),
                        self.mine[i, rows, :].astype(F32)
                        + self.first[i, rows, :].astype(F32)
                        + self.second[j, rows, :].astype(F32),
                    )

                self._chunks(half, add)
        else:
            pltpu.make_async_copy(self.src.at[at.b], self.slots.at[0], self.load.at[0]).wait()
            for off in range(1, at.n):
                self._direct(off).wait_recv()

            def add(r, step):
                rows = pl.ds(r, step)
                total = self.slots[0, rows, :].astype(F32)
                for off in range(1, at.n):
                    total = total + self.slots[off, rows, :].astype(F32)
                put(rows, total)

            self._chunks(self.src.shape[1], add)

    def finish(self):
        at = self.at
        if at.square:
            for i in range(4 if self.before is None else 0):
                self._first(i).wait_send()
            self._second(0).wait_send()
            self._second(1).wait_send()
        else:
            for off in range(1, at.n):
                self._direct(off).wait_send()


class Names:
    def __init__(self):
        self.shapes = []

    def add(self, shapes):
        start = len(self.shapes)
        self.shapes += list(shapes)
        return slice(start, len(self.shapes))


def chunk_loop(rows, step, fn):
    step = min(step, rows)

    @pl.loop(0, rows // step)
    def _(i):
        fn(pl.ds(pl.multiple_of(i * step, step), step))


def inv_root_of(values):
    return lax.rsqrt(jnp.mean(values * values, axis=-1, keepdims=True) + epsilon)


def gather_all(n, H, tokens, cotangent, gains, weights):
    rows, T, D = tokens.shape
    R = weights[0].shape[0]
    hw, ff = weights[0].shape[1], weights[4].shape[1]
    L = H // 2
    names = Names()
    normed_at = names.add([pltpu.VMEM((rows, T, D), BF16)])
    z_at = [names.add(Gather.sems(L)) for _ in range(2 * rows)]
    w_at = [names.add(BatchGather.sems(n)) for _ in range(7)]
    g_at = names.add([DMA((n,)), DMA((n,)), DMA])

    def kernel(tok, ct, gain, wq, wk, wv, wo, wg, wu, wd, attn_in, ct_full, w_qkv, w_o, w_gu, w_d, gains_full, *scratch):
        at = Place(n, H)
        (normed,) = scratch[normed_at]
        at.greet()
        gsend, grecv, glocal = scratch[g_at]

        def gain_dst(b):
            return gains_full.at[:, pl.ds(pl.multiple_of(b * R, R), R)]

        gain_jobs = []
        if at.square:
            first = remote(gain, gain_dst(at.b), gsend.at[0], grecv.at[0], {"batch": at.xn})
            own_y = remote(gain, gain_dst(at.b), gsend.at[1], grecv.at[1], {"batch": at.yn})
            first.start()
            own_y.start()
        else:
            for o in range(1, n):
                job = remote(gain, gain_dst(at.b), gsend.at[o], grecv.at[o], {"batch": (at.b + o) % n})
                job.start()
                gain_jobs.append(job)
        mine = pltpu.make_async_copy(gain, gain_dst(at.b), glocal)
        mine.start()

        ct_jobs = [Gather(at, ct.at[r], ct_full.at[r], scratch[z_at[rows + r]]) for r in range(rows)]
        in_jobs = [Gather(at, normed.at[r], attn_in.at[r], scratch[z_at[r]]) for r in range(rows)]
        outs = []
        for src, dst, col, width in (
            (wq, w_qkv, 0, hw),
            (wk, w_qkv, hw, hw),
            (wv, w_qkv, 2 * hw, hw),
            (wo, w_o, 0, hw),
            (wg, w_gu, 0, ff),
            (wu, w_gu, ff, ff),
            (wd, w_d, 0, ff),
        ):
            outs.append((src, lambda b, rr, dst=dst, col=col, width=width: dst.at[b, rr, pl.ds(col, width)]))
        w_jobs = [BatchGather(at, src, out, scratch[w_at[i]]) for i, (src, out) in enumerate(outs)]
        ct_jobs[0].start()
        mine.wait()
        if at.square:
            got = gain_dst(at.xn)
            remote(got, got, gsend.at[0], grecv.at[0], {"batch": at.xn}).wait_recv()
            fwd = remote(got, got, gsend.at[2], grecv.at[2], {"batch": at.yn})
            fwd.start()
            got = gain_dst(at.yn)
            remote(got, got, gsend.at[1], grecv.at[1], {"batch": at.yn}).wait_recv()
            got = gain_dst(at.dg)
            remote(got, got, gsend.at[2], grecv.at[2], {"batch": at.yn}).wait_recv()
            first.wait_send()
            own_y.wait_send()
            fwd.wait_send()
        else:
            for o in range(1, n):
                got = gain_dst((at.b + n - o) % n)
                remote(got, got, gsend.at[o], grecv.at[o], {"batch": (at.b + o) % n}).wait_recv()
                gain_jobs[o - 1].wait_send()

        for job in w_jobs:
            job.start()
        for r in range(rows):

            def norm(part, r=r):
                values = tok[r, part, :].astype(F32)
                normed[r, part, :] = (values * inv_root_of(values) * gains_full[0:1, :]).astype(BF16)

            chunk_loop(T, 32, norm)
            in_jobs[r].start()
        for job in ct_jobs[1:]:
            job.start()
        order = [ct_jobs[0]] + in_jobs + ct_jobs[1:]
        for k in range(1, L):
            for job in order:
                job.step(k)
            for job in {1: w_jobs[:4], 2: w_jobs[4:]}.get(k, ()):
                job.forward()
        for job in order + w_jobs:
            job.finish()

    return pl.pallas_call(
        kernel,
        out_shape=(
            jax.ShapeDtypeStruct((rows, H, T, D), BF16),
            jax.ShapeDtypeStruct((rows, H, T, D), BF16),
            jax.ShapeDtypeStruct((n, R, 3 * hw), BF16),
            jax.ShapeDtypeStruct((n, R, hw), BF16),
            jax.ShapeDtypeStruct((n, R, 2 * ff), BF16),
            jax.ShapeDtypeStruct((n, R, ff), BF16),
            jax.ShapeDtypeStruct((8, D), F32),
        ),
        in_specs=[VMEM, ANY, VMEM] + [ANY] * 7,
        out_specs=(ANY,) * 6 + (VMEM,),
        scratch_shapes=names.shapes,
        compiler_params=pltpu.CompilerParams(collective_id=1, has_side_effects=True, vmem_limit_bytes=VMEM_LIMIT),
        name="gather_all",
    )(tokens, cotangent, gains, *weights)


def far_first(L, z):
    return sorted(range(L), key=lambda zd: (-abs(zd - z), -zd))


class Plan:
    def __init__(self, L, rank, reduces, early, follow, begin, tasks):
        self.L = L
        order = [far_first(L, z) for z in range(L)]
        never = 10**6
        jobs = list(rank)
        ready = {j: [[never] * L for _ in range(L)] for j in reduces}
        own = {j: begin.get(j, never) for j in jobs if j not in reduces}
        arrive = {j: {} for j in jobs}
        sent = {j: set() for j in jobs}
        for j, when in early.items():
            for z in range(L):
                for i in range(L):
                    ready[j][z][order[z][i]] = when[i]
        self.final, self.complete, self.tasks, self.sends = {}, {}, {}, []
        todo = list(tasks)
        total = L * (L - 1) * 2
        last = {j: -1 for j in jobs}
        s = free = 0

        def close():
            for j in jobs:
                if len(sent[j]) == total:
                    if j in reduces and j not in self.final:
                        self.final[j] = max(last[j] + 1, max(ready[j][z][z] for z in range(L)) - 1, s - 1)
                        if j in follow:
                            own[follow[j]] = self.final[j] + 1
                    if j in own and j not in self.complete:
                        self.complete[j] = last[j] + 2

        while any(len(sent[j]) < total for j in jobs) or todo:
            close()
            now = {}
            for z in range(L):
                for way in (1, -1):
                    if not 0 <= z + way < L:
                        continue
                    for j in jobs:
                        best = []
                        for block in range(L):
                            for half in (0, 1):
                                if (z, way, block, half) in sent[j]:
                                    continue
                                came = arrive[j].get((z, way, block, half), never)
                                if j in reduces:
                                    first = not 0 <= z - way < L
                                    if (block - z) * way > 0 and ready[j][z][block] <= s and (first or came + 2 <= s):
                                        best.append((-abs(block - z), half, block))
                                elif (z - block) * way >= 0 and (own[j] <= s if block == z else came + 2 <= s):
                                    best.append((abs(block - z), half, block))
                        if best:
                            _, half, block = min(best)
                            now[(z, way)] = (j, block, half)
                            break
            for (z, way), (j, block, half) in now.items():
                sent[j].add((z, way, block, half))
                arrive[j][(z + way, way, block, half)] = s
                last[j] = s
            self.sends.append(now)
            if todo and s >= free:
                name, needs, makes, i, length = todo[0]
                if needs is None or self.complete.get(needs, never) <= s:
                    self.tasks[s] = todo.pop(0)
                    free = s + length
                    for j in makes:
                        for z in range(L):
                            ready[j][z][order[z][i]] = s + 2
            s += 1
        close()
        self.jobs, self.reduces, self.order = jobs, reduces, order
        self.ready, self.arrive, self.own = ready, arrive, own
        self.slots = 1 + max(list(self.final.values()) + list(self.complete.values()))

    def block(self, z, i):
        return pick(z, [self.order[q][i] for q in range(self.L)])


def run_plan(plan, at, jobs, task, after, finish):
    z, L = at.z, at.L
    for s in range(plan.slots):
        now = plan.sends[s] if s < len(plan.sends) else {}
        for q in range(L):
            mine = [(way, now[(q, way)]) for way in (1, -1) if (q, way) in now]
            if mine:

                @pl.when(z == q)
                def _():
                    for way, (j, block, half) in mine:
                        jobs[j].copy(q, way, block, half).start()

        if s in plan.tasks:
            task(plan.tasks[s][0])
        after(s)
        past = plan.sends[s - 1] if 0 <= s - 1 < len(plan.sends) else {}
        for q in range(L):
            came = [(way, past[(q - way, way)]) for way in (1, -1) if (q - way, way) in past]
            adds = []
            for j in plan.reduces:
                for (zq, way, block, half), when in plan.arrive[j].items():
                    if zq == q and block != q and max(when + 1, plan.ready[j][q][block] - 1) == s:
                        adds.append((j, block, half))
            if came or adds:

                @pl.when(z == q)
                def _():
                    for way, (j, block, half) in came:
                        jobs[j].landed(q, way, block, half).wait_recv()
                        if j not in plan.reduces:
                            jobs[j].share(block, half).start()
                    for j, block, half in adds:
                        jobs[j].add(block, half)

        for j, when in plan.final.items():
            if when == s:
                finish(j)


def pick(z, values):
    if len(set(values)) == 1:
        return values[0]
    out = jnp.int32(values[0])
    for i, v in enumerate(values[1:], 1):
        out = jnp.where(z == i, v, out)
    return out


class SlotReduce:
    def __init__(self, at, sib, recv, sems):
        self.at, self.sib, self.recv = at, sib, recv
        self.sib_send, self.sib_recv, self.fwd_send, self.recv_sem = sems
        self.half = sib.shape[1] // 2

    @staticmethod
    def sems(L):
        return [DMA((L,)), DMA((L,)), DMA((L, 2)), DMA((L + 1, 2))]

    @staticmethod
    def bufs(L, T, D):
        return [pltpu.VMEM((L, T, D), BF16), pltpu.VMEM((L + 1, T, D), BF16)]

    def part(self, half):
        return pl.ds(half * self.half, self.half)

    def slot(self, z, way, zd):
        return self.at.L if way < 0 and z == zd else zd

    def copy(self, z, way, zd, half):
        at, part = self.at, self.part(half)
        first = not 0 <= z - way < at.L
        src = (self.sib if first else self.recv).at[zd, part, :]
        slot = self.slot(z + way, way, zd)
        device = {"head": at.up if way > 0 else at.down}
        return remote(src, self.recv.at[slot, part, :], self.fwd_send.at[zd, half], self.recv_sem.at[slot, half], device)

    def landed(self, z, way, zd, half):
        at, part = self.at, self.part(half)
        slot = self.slot(z, way, zd)
        block = self.recv.at[slot, part, :]
        device = {"head": at.down if way > 0 else at.up}
        return remote(block, block, self.fwd_send.at[zd, half], self.recv_sem.at[slot, half], device)

    def exchange(self, zd, src):
        return remote(src, self.sib.at[zd], self.sib_send.at[zd], self.sib_recv.at[zd], {"head": self.at.sib})

    def combine(self, zd, mine):
        def add(rows):
            self.sib[zd, rows, :] = (self.sib[zd, rows, :].astype(F32) + mine[rows, :].astype(F32)).astype(BF16)

        chunk_loop(self.sib.shape[1], 32, add)

    def add(self, zd, half):
        def one(rows):
            self.recv[zd, rows, :] = (self.recv[zd, rows, :].astype(F32) + self.sib[zd, rows, :].astype(F32)).astype(BF16)

        step = min(32, self.half)

        @pl.loop(0, self.half // step)
        def _(i):
            one(pl.ds(pl.multiple_of(half * self.half + i * step, step), step))

    def final(self, put):
        at, z = self.at, self.at.z

        def run(extra):
            def part(rows):
                value = self.sib[z, rows, :].astype(F32)
                for slot in extra:
                    value = value + self.recv[slot, rows, :].astype(F32)
                put(rows, value)

            chunk_loop(self.sib.shape[1], 32, part)

        @pl.when(z == 0)
        def _():
            run((at.L,))

        @pl.when(z == at.L - 1)
        def _():
            run((z,))

        @pl.when((z > 0) & (z < at.L - 1))
        def _():
            run((z, at.L))

    def sent(self):
        at = self.at
        for zd in range(at.L):

            @pl.when(zd != at.z)
            def _():
                for half in (0, 1):
                    block = self.recv.at[zd, self.part(half), :]
                    remote(block, block, self.fwd_send.at[zd, half], self.recv_sem.at[zd, half], {"head": at.up}).wait_send()


class SlotGather:
    def __init__(self, at, own, out, sems):
        self.at, self.own, self.out = at, own, out
        self.line_recv, self.up_send, self.down_send, self.sib_send, self.sib_recv, self.local = sems
        self.half = own.shape[0] // 2

    @staticmethod
    def sems(L):
        return [DMA((L, 2))] * 5 + [DMA]

    def block(self, index, half):
        return self.out.at[index, pl.ds(half * self.half, self.half), :]

    def mine(self, half):
        return self.own.at[pl.ds(half * self.half, self.half), :]

    def copy(self, z, way, zb, half):
        at = self.at
        dst = self.block(zb * 2 + at.c, half)
        src = self.mine(half) if zb == z else dst
        send = (self.up_send if way > 0 else self.down_send).at[zb, half]
        return remote(src, dst, send, self.line_recv.at[zb, half], {"head": at.up if way > 0 else at.down})

    def landed(self, z, way, zb, half):
        at = self.at
        dst = self.block(zb * 2 + at.c, half)
        return remote(dst, dst, self.up_send.at[zb, half], self.line_recv.at[zb, half], {"head": at.down if way > 0 else at.up})

    def share(self, zb, half, src=None):
        at = self.at
        dst = self.block(zb * 2 + at.c, half)
        return remote(dst if src is None else src, dst, self.sib_send.at[zb, half], self.sib_recv.at[zb, half], {"head": at.sib})

    def keep(self):
        return pltpu.make_async_copy(self.own, self.out.at[self.at.h], self.local)

    def begin(self):
        for half in (0, 1):
            self.share(self.at.z, half, self.mine(half)).start()
        self.keep().start()

    def finish(self):
        at = self.at
        self.keep().wait()
        for zb in range(at.L):
            for half in (0, 1):
                self.share(zb, half).wait_send()
                other = self.block(zb * 2 + 1 - at.c, half)
                remote(other, other, self.sib_send.at[zb, half], self.sib_recv.at[zb, half], {"head": at.sib}).wait_recv()

            @pl.when((zb <= at.z) & (at.z < at.L - 1))
            def _():
                for half in (0, 1):
                    self.copy(-1, 1, zb, half).wait_send()

            @pl.when((zb >= at.z) & (at.z > 0))
            def _():
                for half in (0, 1):
                    self.copy(-1, -1, zb, half).wait_send()


def norm_back_part(values, gain, grad):
    inv_root = inv_root_of(values)
    unit = values * inv_root
    weighted = grad * gain
    back = inv_root * (weighted - unit * jnp.mean(weighted * unit, axis=-1, keepdims=True))
    return back, jnp.sum(grad * unit, axis=0, keepdims=True)


def feed_forward(n, H, terms, ct_full, tokens, cotangent, gains, w_gu, w_d):
    rows, T, D = tokens.shape
    L = H // 2
    ff = w_d.shape[1]
    S = H * T
    U = w_d.shape[0] // n // 2
    square = n == 4
    rank = []
    for kinds in (("mix", "in"), ("sum", "att"), ("out",)):
        rank += [(kind, r) for r in range(rows) for kind in kinds]
    tasks = []
    for r in range(rows):
        for i in range(L):
            tasks.append((("first", r, i), ("in", r), (), i, 1))
            tasks.append((("second", r, i), None, (("sum", r), ("out", r)), i, 1))
    tasks += [(("grad", k, 0), None, (), 0, 1) for k in range(2 * n)]
    plan = Plan(
        L,
        rank,
        [j for j in rank if j[0] in ("mix", "sum", "out")],
        {("mix", r): [r * L + i for i in range(L)] for r in range(rows)},
        {(a, r): (b, r) for a, b in (("mix", "in"), ("sum", "att")) for r in range(rows)},
        {},
        tasks,
    )
    names = Names()
    n_bufs = [names.add(SlotReduce.bufs(L, T, D)) for _ in range(2 * rows)]
    n_sems = [names.add(SlotReduce.sems(L)) for _ in range(2 * rows)]
    n_gsem = [names.add(SlotGather.sems(L)) for _ in range(rows)]
    rest = names.add(
        [
            pltpu.VMEM((rows, T, D), BF16),
            pltpu.VMEM((rows, T, D), BF16),
            pltpu.VMEM((rows, T, D), F32),
            pltpu.VMEM((2, 2, T, D), BF16),
            pltpu.VMEM((2, 2, T, D), BF16),
            pltpu.VMEM((max(D, rows * S), 2 * ff), BF16),
            pltpu.VMEM((max(D, rows * S), ff), BF16),
            pltpu.VMEM((2, 2, T, D), BF16),
            pltpu.VMEM((2, 2, T, D), BF16),
            pltpu.VMEM((2, max(2 * T, U), ff), BF16),
            pltpu.VMEM((2, max(2 * T, U), 2 * ff), BF16),
            pltpu.VMEM((2, rows, H, T, U), BF16),
            pltpu.VMEM((2, rows, H, T, U), BF16),
            DMA((4,)),
            DMA((2, 4)),
            DMA((2, 4)),
            DMA((2,)),
            DMA((rows, L)),
            DMA((2,)),
            DMA((2,)),
            DMA((2,)),
            DMA((2,)),
        ]
    )
    tile = min(256, ff)
    wide = min(512, D)

    def kernel(
        src,
        ctf,
        tok,
        ct,
        gain,
        wgu_hbm,
        wd_hbm,
        mlp_in,
        g_att,
        hid_hbm,
        ggu_hbm,
        grad_gu,
        grad_d,
        first_gu,
        first_d,
        g_mixed,
        layer_out,
        gain_sum,
        *scratch,
    ):
        at = Place(n, H)
        z = at.z
        (
            normed,
            att,
            mixed,
            stage_g,
            stage_o,
            wgu,
            wd,
            xb,
            cb,
            hb,
            gb,
            xt,
            ct_t,
            t_sem,
            gsend,
            grecv,
            w_sem,
            own_sem,
            x_sem,
            c_sem,
            h_sem,
            g_sem,
        ) = scratch[rest]
        loads = [
            pltpu.make_async_copy(wgu_hbm, wgu.at[pl.ds(0, D), :], w_sem.at[0]),
            pltpu.make_async_copy(wd_hbm, wd.at[pl.ds(0, D), :], w_sem.at[1]),
        ]
        red, gat = {}, {}
        for r in range(rows):
            for kind in ("mix", "sum"):
                red[(kind, r)] = SlotReduce(at, *scratch[n_bufs[r]], scratch[n_sems[r]])
            red[("out", r)] = SlotReduce(at, *scratch[n_bufs[rows + r]], scratch[n_sems[rows + r]])
            gat[("in", r)] = SlotGather(at, normed.at[r], mlp_in.at[r], scratch[n_gsem[r]])
            gat[("att", r)] = SlotGather(at, att.at[r], g_att.at[r], scratch[n_gsem[r]])
        both = {**red, **gat}
        at.greet(batch=square)

        def mine_of(r, zd):
            return red[("out", r)].recv.at[zd]

        def own_load(r, zd):
            return pltpu.make_async_copy(src.at[r, zd * 2 + at.c], mine_of(r, zd), own_sem.at[r, zd])

        def exchange(r, zd):
            return red[("mix", r)].exchange(zd, src.at[r, zd * 2 + 1 - at.c])

        for r in range(rows):
            for i in range(L):
                zd = plan.block(z, i)
                exchange(r, zd).start()
                own_load(r, zd).start()
        for job in loads:
            job.start()
        gain_sum[...] = jnp.zeros_like(gain_sum)

        def combine_mix(r, i):
            zd = plan.block(z, i)
            own_load(r, zd).wait()
            exchange(r, zd).wait()
            red[("mix", r)].combine(zd, mine_of(r, zd))

        def combine_terms(r, i):
            zd = plan.block(z, i)
            for kind, stage in (("sum", stage_g), ("out", stage_o)):
                job = red[(kind, r)]
                job.exchange(zd, stage.at[i % 2, 1 - at.c]).wait()
                job.combine(zd, stage.at[i % 2, at.c])

        def x_load(r, i):
            blk = plan.block(z, i)
            return (
                pltpu.make_async_copy(mlp_in.at[r, pl.ds(2 * blk, 2)], xb.at[i % 2], x_sem.at[i % 2]),
                pltpu.make_async_copy(ctf.at[r, pl.ds(2 * blk, 2)], cb.at[i % 2], c_sem.at[i % 2]),
            )

        def act_store(r, i):
            blk = plan.block(z, i)
            at_row = pl.ds(pl.multiple_of(r * S + blk * 2 * T, 2 * T), 2 * T)
            return (
                pltpu.make_async_copy(hb.at[i % 2, pl.ds(0, 2 * T), :], hid_hbm.at[at_row, :], h_sem.at[i % 2]),
                pltpu.make_async_copy(gb.at[i % 2, pl.ds(0, 2 * T), :], ggu_hbm.at[at_row, :], g_sem.at[i % 2]),
            )

        def first_part(r, i):
            if i == 0:
                gat[("in", r)].finish()
                for job in x_load(r, 0):
                    job.start()
                if r == 0:
                    for job in loads:
                        job.wait()
            for job in x_load(r, i):
                job.wait()
            if i + 1 < L:
                for job in x_load(r, i + 1):
                    job.start()
            if r * L + i >= 2:
                before = (r, i - 2) if i >= 2 else (r - 1, L + i - 2)
                for job in act_store(*before):
                    job.wait()
            k = i % 2

            @pl.loop(0, ff // tile)
            def _(j):
                cols = pl.ds(pl.multiple_of(j * tile, tile), tile)
                up_cols = pl.ds(pl.multiple_of(ff + j * tile, tile), tile)
                x = xb[k].reshape(2 * T, D)
                gate = jnp.dot(x, wgu[0:D, cols], preferred_element_type=F32)
                up = jnp.dot(x, wgu[0:D, up_cols], preferred_element_type=F32)
                back = jnp.dot(cb[k].reshape(2 * T, D), wd[0:D, cols], preferred_element_type=F32)
                sig = 1.0 / (1.0 + jnp.exp(-gate))
                silu = gate * sig
                hb[k, 0 : 2 * T, cols] = (silu * up).astype(BF16)
                gb[k, 0 : 2 * T, cols] = (back * up * (sig * (1.0 + gate * (1.0 - sig)))).astype(BF16)
                gb[k, 0 : 2 * T, up_cols] = (back * silu).astype(BF16)

            for job in act_store(r, i):
                job.start()

        def second_part(r, i):
            k = i % 2

            @pl.loop(0, D // wide)
            def _(j):
                cols = pl.ds(pl.multiple_of(j * wide, wide), wide)
                back = cols_dot(gb[k, 0 : 2 * T, :], wgu[cols, :]).astype(BF16)
                stage_g[k, 0, :, cols] = back[:T]
                stage_g[k, 1, :, cols] = back[T:]
                out = cols_dot(hb[k, 0 : 2 * T, :], wd[cols, :]).astype(BF16)
                stage_o[k, 0, :, cols] = out[:T]
                stage_o[k, 1, :, cols] = out[T:]

            zd = plan.block(z, i)
            for kind, stage in (("sum", stage_g), ("out", stage_o)):
                red[(kind, r)].exchange(zd, stage.at[k, 1 - at.c]).start()

        def finish_mix(r):
            def put(part, value):
                value = value + tok[r, part, :].astype(F32)
                mixed[r, part, :] = value
                normed[r, part, :] = (value * inv_root_of(value) * gain[1:2, :]).astype(BF16)

            red[("mix", r)].final(put)
            red[("mix", r)].sent()
            gat[("in", r)].begin()

        def finish_sum(r):
            def put(part, value):
                back, gain_part = norm_back_part(mixed[r, part, :], gain[1:2, :], value)
                total = ct[r, part, :].astype(F32) + back
                g_mixed[r, part, :] = total
                att[r, part, :] = total.astype(BF16)
                gain_sum[1:2, :] += gain_part

            red[("sum", r)].final(put)
            red[("sum", r)].sent()
            gat[("att", r)].begin()

        def finish_out(r):
            def put(part, value):
                layer_out[r, part, :] = (mixed[r, part, :] + value).astype(BF16)

            red[("out", r)].final(put)
            red[("out", r)].sent()

        if square:
            units = [
                ((1 - at.y) * 2 + 1 - at.x, 0, 1 - at.y, at.xn),
                ((1 - at.y) * 2 + 1 - at.x, 1, 3 - at.x, at.yn),
                (at.y * 2 + 1 - at.x, 0, at.y, at.xn),
                ((1 - at.y) * 2 + at.x, 1, 2 + at.x, at.yn),
                ((1 - at.y) * 2 + at.x, 0, None, None),
                (at.y * 2 + 1 - at.x, 1, None, None),
                (at.b, 0, None, None),
                (at.b, 1, None, None),
            ]
        else:
            units = [(k // 2, k % 2, None, None) for k in range(2 * n)]
        again = [
            pltpu.make_async_copy(ggu_hbm, wgu.at[pl.ds(0, rows * S), :], w_sem.at[0]),
            pltpu.make_async_copy(hid_hbm, wd.at[pl.ds(0, rows * S), :], w_sem.at[1]),
        ]

        def columns(k):
            cols = pl.ds(pl.multiple_of((units[k][0] * 2 + units[k][1]) * U, U), U)
            return [
                pltpu.make_async_copy(mlp_in.at[:, :, :, cols], xt.at[k % 2], t_sem.at[k % 2]),
                pltpu.make_async_copy(ctf.at[:, :, :, cols], ct_t.at[k % 2], t_sem.at[2 + k % 2]),
            ]

        def grad_store(k):
            b, half = units[k][:2]
            part = pl.ds(half * U, U)
            return [
                pltpu.make_async_copy(hb.at[k % 2, pl.ds(0, U), :], grad_d.at[b, part, :], h_sem.at[k % 2]),
                pltpu.make_async_copy(gb.at[k % 2, pl.ds(0, U), :], grad_gu.at[b, part, :], g_sem.at[k % 2]),
            ]

        def grad_sends(k):
            b, half, slot, to = units[k]
            part = pl.ds(half * U, U)
            return [
                remote(src.at[b, part, :], dst.at[slot], gsend.at[a, k], grecv.at[a, slot], {"batch": to})
                for a, (src, dst) in enumerate(((grad_d, first_d), (grad_gu, first_gu)))
            ]

        def prepare_grads():
            for i in (L - 2, L - 1):
                for job in act_store(rows - 1, i):
                    job.wait()
            for job in again + columns(0):
                job.start()

        def grad(k):
            if k == 0:
                for job in again:
                    job.wait()
            for job in columns(k):
                job.wait()
            if k + 1 < 2 * n:
                for job in columns(k + 1):
                    job.start()
            ring = k % 2

            @pl.loop(0, 2 * ff // tile)
            def _(j):
                cols = pl.ds(pl.multiple_of(j * tile, tile), tile)
                x = xt[ring].reshape(rows * S, U)
                gb[ring, 0:U, cols] = rows_dot(x, wgu[0 : rows * S, cols]).astype(BF16)

            @pl.loop(0, ff // tile)
            def _(j):
                cols = pl.ds(pl.multiple_of(j * tile, tile), tile)
                x = ct_t[ring].reshape(rows * S, U)
                hb[ring, 0:U, cols] = rows_dot(x, wd[0 : rows * S, cols]).astype(BF16)

            for job in grad_store(k):
                job.start()

        def task(name):
            kind, r, i = name
            if kind == "first":
                first_part(r, i)
            elif kind == "second":
                second_part(r, i)
                if (r, i) == (rows - 1, L - 1):
                    prepare_grads()
            else:
                grad(r)

        def after(s):
            if s + 1 < rows * L:
                combine_mix((s + 1) // L, (s + 1) % L)
            name = plan.tasks[s - 1][0] if s - 1 in plan.tasks else None
            if name and name[0] == "second":
                combine_terms(*name[1:])
            if name and name[0] == "grad":
                for job in grad_store(name[1]):
                    job.wait()
                if units[name[1]][3] is not None:
                    for job in grad_sends(name[1]):
                        job.start()

        def finish(j):
            {"mix": finish_mix, "sum": finish_sum, "out": finish_out}[j[0]](j[1])

        combine_mix(0, 0)
        run_plan(plan, at, both, task, after, finish)
        if square:
            for k in range(4):
                for job in grad_sends(k):
                    job.wait()
        for r in range(rows):
            gat[("att", r)].finish()

    return pl.pallas_call(
        kernel,
        out_shape=(
            jax.ShapeDtypeStruct((rows, H, T, D), BF16),
            jax.ShapeDtypeStruct((rows, H, T, D), BF16),
            jax.ShapeDtypeStruct((rows * S, ff), BF16),
            jax.ShapeDtypeStruct((rows * S, 2 * ff), BF16),
            jax.ShapeDtypeStruct((n, 2 * U, 2 * ff), BF16),
            jax.ShapeDtypeStruct((n, 2 * U, ff), BF16),
            jax.ShapeDtypeStruct((4, U, 2 * ff), BF16),
            jax.ShapeDtypeStruct((4, U, ff), BF16),
            jax.ShapeDtypeStruct((rows, T, D), F32),
            jax.ShapeDtypeStruct((rows, T, D), BF16),
            jax.ShapeDtypeStruct((8, D), F32),
        ),
        in_specs=[ANY, ANY, VMEM, VMEM, VMEM, ANY, ANY],
        out_specs=(ANY,) * 8 + (VMEM, VMEM, VMEM),
        scratch_shapes=names.shapes,
        compiler_params=pltpu.CompilerParams(collective_id=2, has_side_effects=True, vmem_limit_bytes=VMEM_LIMIT),
        name="feed_forward",
    )(terms, ct_full, tokens, cotangent, gains, w_gu, w_d)


def last_sums(n, H, terms, tokens, g_mixed, gains, gain_sum, g_qkv, g_o, g_gu, g_d, first_gu, first_d):
    rows, T, D = tokens.shape
    L = H // 2
    R, hw = g_o.shape[1], g_o.shape[2]
    ff = g_d.shape[2]
    names = Names()
    r_bufs = [names.add(Reduce.bufs(L, T, D)) for _ in range(rows)]
    r_sems = [names.add(Reduce.sems(L)) for _ in range(rows)]
    b_bufs = [names.add(BatchReduce.bufs(n, R, w)) for w in (ff, 2 * ff, hw, 3 * hw)]
    b_sems = [names.add(BatchReduce.sems(n)) for _ in range(4)]
    s_at = names.add(
        [pltpu.VMEM((8, D), F32), pltpu.VMEM((n, 8, R), F32), pltpu.VMEM((H, 8, R), F32)]
        + [DMA((n,)), DMA((n,)), DMA((H,)), DMA((H,)), DMA]
    )

    def kernel(src, tok, gmix, gain, gain_in, gqkv, go, ggu, gd, fgu, fd, grad_in, gq, gk, gv, gout, ggate, gup, gdown, gain_out, *scratch):
        at = Place(n, H)
        at.greet(all_heads=True)
        small, over_batch, over_head, bsend, brecv, hsend, hrecv, local = scratch[s_at]
        sums = [Reduce(at, src.at[r], *scratch[r_bufs[r]], scratch[r_sems[r]]) for r in range(rows)]
        weights = [
            BatchReduce(at, s, scratch[b_bufs[i]], scratch[b_sems[i]], first if at.square else None)
            for i, (s, first) in enumerate(((gd, fd), (ggu, fgu), (go, None), (gqkv, None)))
        ]
        for job in sums[:1] + weights + sums[1:]:
            job.start()
        for job in weights[:2]:
            job.second_step()
        small[...] = gain_in[...]

        def finish_sum(r):
            def put(part, value):
                back, gain_part = norm_back_part(tok[r, part, :].astype(F32), gain[0:1, :], value)
                grad_in[r, part, :] = gmix[r, part, :] + back
                small[0:1, :] += gain_part

            sums[r].final(put)

        for k in range(L - 1):
            sums[0].hops(k)
        for r in range(rows):
            if r + 1 < rows:
                for k in range(L - 1):
                    sums[r + 1].hops(k, "first")
            finish_sum(r)
            if r + 1 < rows:
                for k in range(L - 1):
                    sums[r + 1].hops(k, "mid")
        for job in weights[2:]:
            job.second_step()

        def slice_of(b):
            return small.at[:, pl.ds(pl.multiple_of(b * R, R), R)]

        def batch_job(off):
            to = (at.b + off) % n
            return remote(slice_of(to), over_batch.at[off], bsend.at[off], brecv.at[off], {"batch": to})

        for off in range(1, n):
            batch_job(off).start()
        mine = pltpu.make_async_copy(slice_of(at.b), over_batch.at[0], local)
        mine.start()

        def put_o(part, value):
            gout[part, :] = value

        def put_d(part, value):
            gdown[part, :] = value

        def put_gu(part, value):
            ggate[part, :] = value[:, :ff]
            gup[part, :] = value[:, ff:]

        weights[0].final(put_d)
        weights[1].final(put_gu)
        weights[2].final(put_o)
        mine.wait()
        total = over_batch[0]
        for off in range(1, n):
            batch_job(off).wait_recv()
            total = total + over_batch[off]
        over_head[at.h] = total

        def head_job(off, block):
            to = (at.h + off) % H
            return remote(over_head.at[block], over_head.at[block], hsend.at[off], hrecv.at[off], {"head": to})

        for off in range(1, H):
            head_job(off, at.h).start()

        def put_qkv(part, value):
            gq[part, :] = value[:, :hw]
            gk[part, :] = value[:, hw : 2 * hw]
            gv[part, :] = value[:, 2 * hw :]

        weights[3].final(put_qkv)
        for off in range(1, H):
            head_job(off, (at.h + H - off) % H).wait_recv()
        total = over_head[0]
        for h in range(1, H):
            total = total + over_head[h]
        gain_out[...] = total
        for off in range(1, n):
            batch_job(off).wait_send()
        for off in range(1, H):
            head_job(off, at.h).wait_send()
        for job in sums + weights:
            job.finish()

    return pl.pallas_call(
        kernel,
        out_shape=(
            jax.ShapeDtypeStruct((rows, T, D), F32),
            jax.ShapeDtypeStruct((R, hw), F32),
            jax.ShapeDtypeStruct((R, hw), F32),
            jax.ShapeDtypeStruct((R, hw), F32),
            jax.ShapeDtypeStruct((R, hw), F32),
            jax.ShapeDtypeStruct((R, ff), F32),
            jax.ShapeDtypeStruct((R, ff), F32),
            jax.ShapeDtypeStruct((R, ff), F32),
            jax.ShapeDtypeStruct((8, R), F32),
        ),
        in_specs=[ANY, VMEM, VMEM, VMEM, VMEM] + [ANY] * 6,
        out_specs=(VMEM,) * 9,
        scratch_shapes=names.shapes,
        compiler_params=pltpu.CompilerParams(collective_id=4, has_side_effects=True, vmem_limit_bytes=VMEM_LIMIT),
        name="last_sums",
    )(terms, tokens, g_mixed, gains, gain_sum, g_qkv, g_o, g_gu, g_d, first_gu, first_d)


def rows_dot(left, right):
    return lax.dot_general(left, right, (((0,), (0,)), ((), ())), preferred_element_type=F32)


def cols_dot(left, right):
    return lax.dot_general(left, right, (((1,), (1,)), ((), ())), preferred_element_type=F32)


QUERIES = 256


def rope_tables(positions):
    half_dim = HEAD_DIM // 2
    frequency = rope_base ** (-(jnp.arange(half_dim).astype(F32) * 2.0) / HEAD_DIM)
    angles = positions.astype(F32)[:, :, None] * frequency
    cosine, sine = jnp.cos(angles), jnp.sin(angles)
    return jnp.concatenate([cosine] * 4, axis=-1), jnp.concatenate([-sine, sine] * 2, axis=-1)


def rotate(values, cosine, sine):
    half_dim = HEAD_DIM // 2
    parts = []
    for g in range(values.shape[1] // 128):
        part = values[:, g * 128 : (g + 1) * 128]
        lane = lax.broadcasted_iota(jnp.int32, part.shape, 1)
        swapped = jnp.where(
            lane % HEAD_DIM < half_dim, pltpu.roll(part, 128 - half_dim, 1), pltpu.roll(part, half_dim, 1)
        )
        parts.append(part * cosine + swapped * sine)
    return jnp.concatenate(parts, axis=1) if len(parts) > 1 else parts[0]


def only_head(values, h):
    lane = lax.broadcasted_iota(jnp.int32, values.shape, 1)
    return jnp.where(lane // HEAD_DIM == h, values, jnp.zeros_like(values))


def masked_scores(keys, query, starts, first):
    scores = cols_dot(keys, query)
    key_index = lax.broadcasted_iota(jnp.int32, scores.shape, 0)
    query_index = lax.broadcasted_iota(jnp.int32, scores.shape, 1) + first
    return jnp.where((key_index >= starts) & (key_index <= query_index), scores, masked_value)


def attend(qkv, starts, lse, attended, h, W):
    S = qkv.shape[0]
    scale = HEAD_DIM**-0.5
    block = min(QUERIES, S)
    for i in range(S // block):
        rows = pl.ds(i * block, block)
        width = (i + 1) * block
        query = only_head(qkv[rows, 0:W], h) * jnp.asarray(scale, BF16)
        scores = masked_scores(qkv[0:width, W : 2 * W], query, starts[:, rows], i * block)
        top = jnp.max(scores, axis=0, keepdims=True)
        weights = jnp.exp(scores - top)
        total = jnp.sum(weights, axis=0, keepdims=True)
        lse[pl.ds(h, 1), rows] = top + jnp.log(total)
        probs = (weights * (1.0 / total)).astype(BF16)
        out = rows_dot(probs, qkv[0:width, 2 * W : 3 * W]).astype(BF16)
        lane = lax.broadcasted_iota(jnp.int32, out.shape, 1)
        attended[rows, :] = jnp.where(lane // HEAD_DIM == h, out, attended[rows, :])


def attend_back(qkv, starts, lse, grad, g_query, g_key, g_value, h, W):
    S = qkv.shape[0]
    scale = HEAD_DIM**-0.5
    block = min(QUERIES, S)
    for i in range(S // block):
        rows = pl.ds(i * block, block)
        width = (i + 1) * block
        query = only_head(qkv[rows, 0:W], h) * jnp.asarray(scale, BF16)
        keys = qkv[0:width, W : 2 * W]
        scores = masked_scores(keys, query, starts[:, rows], i * block)
        probs = jnp.exp(scores - lse[pl.ds(h, 1), rows])
        back = only_head(grad[rows, :], h)
        g_prob = cols_dot(qkv[0:width, 2 * W : 3 * W], back)
        delta = jnp.sum(probs * g_prob, axis=0, keepdims=True)
        g_score = (probs * (g_prob - delta)).astype(BF16)
        g_value[0:width, :] += jnp.dot(probs.astype(BF16), back, preferred_element_type=F32)
        g_key[0:width, :] += jnp.dot(g_score, query, preferred_element_type=F32)
        g_query[rows, :] += only_head(rows_dot(g_score, keys) * scale, h)


def attention_forward(attn_in, w_qkv, w_o, cosine, sine, starts):
    rows, S, D = attn_in.shape
    W = w_o.shape[1]
    heads = W // HEAD_DIM
    step = min(256, S)

    def kernel(x, wq, wo, cos, sin, st, qkv, lse, attended, terms):
        @pl.loop(0, S // step)
        def _(b):
            part = pl.ds(pl.multiple_of(b * step, step), step)
            lin = jnp.dot(x[0, part, :], wq[...], preferred_element_type=F32)
            c, s = cos[0, part, :], sin[0, part, :]
            qkv[0, part, 0:W] = rotate(lin[:, :W], c, s).astype(BF16)
            qkv[0, part, W : 2 * W] = rotate(lin[:, W : 2 * W], c, s).astype(BF16)
            qkv[0, part, 2 * W : 3 * W] = lin[:, 2 * W :].astype(BF16)

        @pl.loop(0, heads)
        def _(h):
            attend(qkv.at[0], st.at[0], lse.at[0], attended.at[0], h, W)

        @pl.loop(0, S // step)
        def _(b):
            part = pl.ds(pl.multiple_of(b * step, step), step)
            terms[0, part, :] = cols_dot(attended[0, part, :], wo[...]).astype(BF16)

    def row(*shape):
        return pl.BlockSpec((1,) + shape, lambda r: (r, 0, 0))

    return pl.pallas_call(
        kernel,
        grid=(rows,),
        out_shape=(
            jax.ShapeDtypeStruct((rows, S, 3 * W), BF16),
            jax.ShapeDtypeStruct((rows, 8, S), F32),
            jax.ShapeDtypeStruct((rows, S, W), BF16),
            jax.ShapeDtypeStruct((rows, S, D), BF16),
        ),
        in_specs=[
            row(S, D),
            pl.BlockSpec((D, 3 * W), lambda r: (0, 0)),
            pl.BlockSpec((D, W), lambda r: (0, 0)),
            row(S, 128),
            row(S, 128),
            row(1, S),
        ],
        out_specs=(row(S, 3 * W), row(8, S), row(S, W), row(S, D)),
        compiler_params=pltpu.CompilerParams(vmem_limit_bytes=VMEM_LIMIT),
        name="attention_forward",
    )(attn_in, w_qkv, w_o, cosine, sine, starts)


def attention_backward(g_att, attended, qkv, lse, attn_in, w_qkv, w_o, cosine, sine, starts):
    rows, S, D = attn_in.shape
    W = w_o.shape[1]
    heads = W // HEAD_DIM
    step = min(256, S)
    wide = min(512, D)

    def kernel(ga, att, qkv, ls, x, wq, wo, cos, sin, st, terms, grad_qkv, grad_o, gat, gq, gk, gv, gqkv, sum_qkv, sum_o):
        r = pl.program_id(0)

        @pl.when(r == 0)
        def _():
            sum_qkv[...] = jnp.zeros_like(sum_qkv)
            sum_o[...] = jnp.zeros_like(sum_o)

        gq[...] = jnp.zeros_like(gq)
        gk[...] = jnp.zeros_like(gk)
        gv[...] = jnp.zeros_like(gv)

        @pl.loop(0, S // step)
        def _(b):
            part = pl.ds(pl.multiple_of(b * step, step), step)
            gat[part, :] = jnp.dot(ga[0, part, :], wo[...], preferred_element_type=F32).astype(BF16)

        @pl.loop(0, heads)
        def _(h):
            attend_back(qkv.at[0], st.at[0], ls.at[0], gat, gq, gk, gv, h, W)

        @pl.loop(0, S // step)
        def _(b):
            part = pl.ds(pl.multiple_of(b * step, step), step)
            c, s = cos[0, part, :], -sin[0, part, :]
            gqkv[part, 0:W] = rotate(gq[part, :], c, s).astype(BF16)
            gqkv[part, W : 2 * W] = rotate(gk[part, :], c, s).astype(BF16)
            gqkv[part, 2 * W : 3 * W] = gv[part, :].astype(BF16)
            terms[0, part, :] = cols_dot(gqkv[part, :], wq[...]).astype(BF16)

        @pl.loop(0, D // wide)
        def _(j):
            cols = pl.ds(pl.multiple_of(j * wide, wide), wide)
            sum_qkv[:, cols] += rows_dot(gqkv[...], x[0, :, cols])
            sum_o[:, cols] += rows_dot(att[0], ga[0, :, cols])

        @pl.when(r == rows - 1)
        def _():
            @pl.loop(0, D // wide)
            def _(j):
                cols = pl.ds(pl.multiple_of(j * wide, wide), wide)
                grad_qkv[cols, :] = sum_qkv[:, cols].T.astype(BF16)
                grad_o[cols, :] = sum_o[:, cols].T.astype(BF16)

    def row(*shape):
        return pl.BlockSpec((1,) + shape, lambda r: (r, 0, 0))

    def whole(*shape):
        return pl.BlockSpec(shape, lambda r: (0, 0))

    return pl.pallas_call(
        kernel,
        grid=(rows,),
        out_shape=(
            jax.ShapeDtypeStruct((rows, S, D), BF16),
            jax.ShapeDtypeStruct((D, 3 * W), BF16),
            jax.ShapeDtypeStruct((D, W), BF16),
        ),
        in_specs=[
            row(S, D),
            row(S, W),
            row(S, 3 * W),
            row(8, S),
            row(S, D),
            whole(D, 3 * W),
            whole(D, W),
            row(S, 128),
            row(S, 128),
            row(1, S),
        ],
        out_specs=(row(S, D), whole(D, 3 * W), whole(D, W)),
        scratch_shapes=[
            pltpu.VMEM((S, W), BF16),
            pltpu.VMEM((S, W), F32),
            pltpu.VMEM((S, W), F32),
            pltpu.VMEM((S, W), F32),
            pltpu.VMEM((S, 3 * W), BF16),
            pltpu.VMEM((3 * W, D), F32),
            pltpu.VMEM((W, D), F32),
        ],
        compiler_params=pltpu.CompilerParams(vmem_limit_bytes=VMEM_LIMIT),
        name="attention_backward",
    )(g_att, attended, qkv, lse, attn_in, w_qkv, w_o, cosine, sine, starts)


def per_device(
    n,
    H,
    tokens,
    segment_ids,
    position_ids,
    w_query,
    w_key,
    w_value,
    w_output,
    w_gate,
    w_up,
    w_down,
    attn_gain,
    mlp_gain,
    cotangent,
):
    rows, T, D = tokens.shape
    S = T * H
    R, hw = w_query.shape
    ff = w_gate.shape[1]
    shard_gains = jnp.concatenate(
        [attn_gain.astype(F32)[None], mlp_gain.astype(F32)[None], jnp.zeros((6, R), F32)], axis=0
    )
    attn_in, ct_full, w_qkv, w_o, w_gu, w_d, gains = gather_all(
        n, H, tokens, cotangent, shard_gains, (w_query, w_key, w_value, w_output, w_gate, w_up, w_down)
    )
    w_qkv = w_qkv.reshape(D, 3 * hw)
    w_o = w_o.reshape(D, hw)
    w_gu = w_gu.reshape(D, 2 * ff)
    w_d = w_d.reshape(D, ff)

    cosine, sine = rope_tables(position_ids)
    starts = (jnp.arange(S, dtype=jnp.int32)[None, :] - position_ids)[:, None, :]
    qkv, lse, attended, terms = attention_forward(attn_in.reshape(rows, S, D), w_qkv, w_o, cosine, sine, starts)
    terms = terms.reshape(rows, H, T, D)
    _, g_att, _, _, grad_gu, grad_d, first_gu, first_d, g_mixed, layer_out, gain_sum = feed_forward(
        n, H, terms, ct_full, tokens, cotangent, gains, w_gu, w_d
    )
    in_terms, grad_qkv, grad_o = attention_backward(
        g_att.reshape(rows, S, D), attended, qkv, lse, attn_in.reshape(rows, S, D), w_qkv, w_o, cosine, sine, starts
    )
    in_terms = in_terms.reshape(rows, H, T, D)
    grad_qkv = grad_qkv.reshape(n, R, 3 * hw)
    grad_o = grad_o.reshape(n, R, hw)
    grad_input, grad_q, grad_k, grad_v, grad_out, grad_gate, grad_up, grad_down, gain_grads = last_sums(
        n, H, in_terms, tokens, g_mixed, gains, gain_sum, grad_qkv, grad_o, grad_gu, grad_d, first_gu, first_d
    )
    return (
        layer_out,
        grad_input,
        grad_q,
        grad_k,
        grad_v,
        grad_out,
        grad_gate,
        grad_up,
        grad_down,
        gain_grads[0],
        gain_grads[1],
    )


def solution(mesh):
    row = P("batch", "head", None)
    ids = P("batch", None)
    weight = P("batch", "head")
    gain = P("batch")
    return jax.shard_map(
        functools.partial(per_device, mesh.shape["batch"], mesh.shape["head"]),
        mesh=mesh,
        in_specs=(row, ids, ids) + (weight,) * 7 + (gain, gain, row),
        out_specs=(row, row) + (weight,) * 7 + (gain, gain),
        check_vma=False,
    )
```

time: 1740 us -> 674 us (0.39)
  waiting for transfers between devices: 1250 us -> 0 us
  Pallas kernels: 0 us -> 641 us
  matrix products: 281 us -> 0 us
  other arithmetic: 114 us -> 9.55 us
  blocking collectives: 53.4 us -> 0 us
    pallas_call x0 -> x5, Pallas kernels: none -> 641 us  [the longest x1 267 us: feed_forward(): pl.pallas_call(kernel, out_shape=(jax.ShapeDtypeStruct((rows, H, T, D), B...]
    psum x2 -> x0, waiting for transfers between devices: 595 us -> none  [the longest x1 322 us: per_device(): mixed_full = lax.psum(attn_terms + placed, 'head')]
    all_gather x11 -> x0, waiting for transfers between devices: 338 us -> none  [the longest x2 85.1 us: per_device(): lax.all_gather(normed(inputs, gain_one).astype(jnp.bfloat16), 'head', axi...]
    reduce_scatter x11 -> x0, waiting for transfers between devices: 308 us -> none  [the longest x2 101 us: per_device(): lax.psum_scatter(attn_in_terms.astype(jnp.bfloat16), 'head', scatter_dime...]
    dot_general x66 -> x0, matrix products: 281 us -> none  [the longest x14 69.3 us: contract_cols(): lax.dot_general(left, right, (((1,), (1,)), ((), ())), preferred_element_...]
    convert_element_type x21 -> x0, other arithmetic: 43.6 us -> none  [the longest x4 22.5 us: attend_backward(): grad_score = (probs_full * (grad_prob - row_delta)).astype(jnp.bfloat16)]
    reduce_sum x9 -> x0, other arithmetic: 30.4 us -> none  [the longest x1 14.7 us: per_device(): jnp.sum(jnp.where(own_rows[:, None], gain_terms, 0.0), axis=0)]
    psum x1 -> x0, blocking collectives: 25.9 us -> none  [reduce_grads(): gain_sums = lax.psum((grad_parts[7], grad_parts[8]), 'head')]
  transfers between devices with their start and end apart: 24 -> 0, of which waited for: 21 -> 0; matrix products, arithmetic and copies ran while one was open for 20% -> 0% of each run, Pallas kernels for 0% -> 0%
where the time goes in v1:
time: 674 us; the launch traced here: 665 us
  Pallas kernels  641 us (95%)
  local copies, waits for them, and re-layouts  13.5 us (2%)
  other arithmetic  9.55 us (1%)
    pallas_call x1, Pallas kernels, feed_forward(): pl.pallas_call(kernel, out_shape=(jax.ShapeDtypeStruct((rows, H, T, D), B...  267 us
    pallas_call x1, Pallas kernels, gather_all(): pl.pallas_call(kernel, out_shape=(jax.ShapeDtypeStruct((rows, H, T, D), B...  166 us
    pallas_call x1, Pallas kernels, last_sums(): pl.pallas_call(kernel, out_shape=(jax.ShapeDtypeStruct((rows, T, D), F32)...  116 us
    pallas_call x1, Pallas kernels, attention_backward(): pl.pallas_call(kernel, grid=(rows,), out_shape=(jax.ShapeDtypeStruct((row...  57.4 us
    pallas_call x1, Pallas kernels, attention_forward(): pl.pallas_call(kernel, grid=(rows,), out_shape=(jax.ShapeDtypeStruct((row...  34.6 us

profile of v1, /device:TPU:0, one launch (start us, length us, event | category | flops | bytes accessed | tf_op | source)
XLA Modules:
  0.0 665.1 jit_solution(2807533595276874975)
XLA Ops:
  0.7 0.1 pad.10.clone
  0.7 0.7 broadcast_in_dim.27
  1.4 0.7 broadcast_in_dim.28
  2.1 0.7 maximum_maximum_fusion.gain
  2.8 0.8 iota_subtract_fusion
  3.6 0.6 broadcast_in_dim.26.st
  4.2 3.7 fusion
  7.9 3.0 pad_maximum_fusion
  10.9 166.3 %gather_all.1 = (bf16[2,8,128,2048]{3,2,1,0:T(8,128)(2,1)}, bf16[2,8,128,2048]{3,2,1,0:T(8,128)(2,1)}, bf16[4,512,768]{2,1,0:T(8,128)(2,1)}, bf16[4,512,256]{2,1...) custom-call(bf16[2,128,2048]{2,1,0:T(8,128)(2,1)} %tok.5, ...), custom_call_target="tpu_custom_call" | custom-call | tf_op jit(solution)/shard_map/gather_all/pallas_call | solution.py:608
  177.2 34.6 %attention_forward.1 = (bf16[2,1024,768]{2,1,0:T(8,128)(2,1)}, f32[2,8,1024]{2,1,0:T(8,128)}, bf16[2,1024,256]{2,1,0:T(8,128)(2,1)}, bf16[2,1024,2048]{2,1,0:T(8,128)(2,1)}) custom-call(bf16[2,1024,2048]{2,1,0:T(8,128)(2,1)} %bitcast.14, bf16[2048,768]{1,0:T(8,128)(2,1)} %bitcast.16, bf16[2048,256]{1,0:T(8,128)(2,1)} %bitcast.23, ...), custom_call_target="tpu_custom_call" | custom-call | tf_op jit(solution)/shard_map/attention_forward/pallas_call | solution.py:1536
  211.8 266.7 %feed_forward.1 = (bf16[2,8,128,2048]{3,2,1,0:T(8,128)(2,1)}, bf16[2,8,128,2048]{3,2,1,0:T(8,128)(2,1)}, bf16[2048,1024]{1,0:T(8,128)(2,1)}, bf16[2048,2048]{1,0...) custom-call(bf16[2,8,128,2048]{3,2,1,0:T(8,128)(2,1)} %bitcast.21, ...), custom_call_target="tpu_custom_call" | custom-call | tf_op jit(solution)/shard_map/feed_forward/pallas_call | solution.py:1272
  478.5 57.4 %attention_backward.1 = (bf16[2,1024,2048]{2,1,0:T(8,128)(2,1)}, bf16[2048,768]{1,0:T(8,128)(2,1)}, bf16[2048,256]{1,0:T(8,128)(2,1)}) custom-call(bf16[2,1024,2048]{2,1,0:T(8,128)(2,1)} %bitcast.18, bf16[2,1024,256]{2,1,0:T(8,128)(2,1)} %get-tuple-element.52.att, bf16[2,1024,768]{2,1,0:T(8,128)(2,1)} %get-tuple-element.53.qkv, ...), custom_call_target="tpu_custom_call" | custom-call | tf_op jit(solution)/shard_map/attention_backward/pallas_call | solution.py:1616
  535.9 115.9 %last_sums.1 = (f32[2,128,2048]{2,1,0:T(8,128)}, f32[512,256]{1,0:T(8,128)}, f32[512,256]{1,0:T(8,128)}, f32[512,256]{1,0:T(8,128)}, f32[512,256]{1,0:T(8,128)},...) custom-call(bf16[2,8,128,2048]{3,2,1,0:T(8,128)(2,1)} %bitcast.19, ...), custom_call_target="tpu_custom_call" | custom-call | tf_op jit(solution)/shard_map/last_sums/pallas_call | solution.py:1404
  651.8 0.0 copy-start.7
  651.8 1.4 fusion.1
  653.2 1.0 copy.32
  654.2 3.3 copy.33
  657.5 0.8 copy.34
  658.3 0.8 copy.35
  659.1 0.8 copy.36
  659.9 0.8 copy.37
  660.7 1.3 copy.38
  662.0 1.3 copy.39
  663.3 1.3 copy.40
  (17 shorter events, 0.0 us)
Async XLA Ops:
  535.9 117.3 %copy-start.3 = (bf16[2,128,2048]{2,1,0:T(8,128)(2,1)S(1)}, bf16[2,128,2048]{2,1,0:T(8,128)(2,1)}, u32[]{:S(2)}) copy-start(bf16[2,128,2048]{2,1,0:T(8,128)(2,1)} %get-tuple-element.93) | copy-start | bytes 3145732
  651.8 5.7 copy-start.7
  651.8 6.5 copy-start.6
  653.2 5.9 copy-start.5
  654.2 5.7 copy-start.4
  654.2 6.5 copy-start.2
  657.5 4.5 copy-start.1
  660.7 2.6 copy-start

commit v2 on v1

--- a/solution.py
+++ b/solution.py
@@ -18,6 +18,7 @@
 ANY = pl.BlockSpec(memory_space=pl.ANY)
 VMEM = pl.BlockSpec(memory_space=pltpu.VMEM)
 VMEM_LIMIT = 60 * 2**20
+BACK_LIMIT = 63 * 2**20
 
 
 class Place:
@@ -514,114 +515,6 @@
 
 def inv_root_of(values):
     return lax.rsqrt(jnp.mean(values * values, axis=-1, keepdims=True) + epsilon)
-
-
-def gather_all(n, H, tokens, cotangent, gains, weights):
-    rows, T, D = tokens.shape
-    R = weights[0].shape[0]
-    hw, ff = weights[0].shape[1], weights[4].shape[1]
-    L = H // 2
-    names = Names()
-    normed_at = names.add([pltpu.VMEM((rows, T, D), BF16)])
-    z_at = [names.add(Gather.sems(L)) for _ in range(2 * rows)]
-    w_at = [names.add(BatchGather.sems(n)) for _ in range(7)]
-    g_at = names.add([DMA((n,)), DMA((n,)), DMA])
-
-    def kernel(tok, ct, gain, wq, wk, wv, wo, wg, wu, wd, attn_in, ct_full, w_qkv, w_o, w_gu, w_d, gains_full, *scratch):
-        at = Place(n, H)
-        (normed,) = scratch[normed_at]
-        at.greet()
-        gsend, grecv, glocal = scratch[g_at]
-
-        def gain_dst(b):
-            return gains_full.at[:, pl.ds(pl.multiple_of(b * R, R), R)]
-
-        gain_jobs = []
-        if at.square:
-            first = remote(gain, gain_dst(at.b), gsend.at[0], grecv.at[0], {"batch": at.xn})
-            own_y = remote(gain, gain_dst(at.b), gsend.at[1], grecv.at[1], {"batch": at.yn})
-            first.start()
-            own_y.start()
-        else:
-            for o in range(1, n):
-                job = remote(gain, gain_dst(at.b), gsend.at[o], grecv.at[o], {"batch": (at.b + o) % n})
-                job.start()
-                gain_jobs.append(job)
-        mine = pltpu.make_async_copy(gain, gain_dst(at.b), glocal)
-        mine.start()
-
-        ct_jobs = [Gather(at, ct.at[r], ct_full.at[r], scratch[z_at[rows + r]]) for r in range(rows)]
-        in_jobs = [Gather(at, normed.at[r], attn_in.at[r], scratch[z_at[r]]) for r in range(rows)]
-        outs = []
-        for src, dst, col, width in (
-            (wq, w_qkv, 0, hw),
-            (wk, w_qkv, hw, hw),
-            (wv, w_qkv, 2 * hw, hw),
-            (wo, w_o, 0, hw),
-            (wg, w_gu, 0, ff),
-            (wu, w_gu, ff, ff),
-            (wd, w_d, 0, ff),
-        ):
-            outs.append((src, lambda b, rr, dst=dst, col=col, width=width: dst.at[b, rr, pl.ds(col, width)]))
-        w_jobs = [BatchGather(at, src, out, scratch[w_at[i]]) for i, (src, out) in enumerate(outs)]
-        ct_jobs[0].start()
-        mine.wait()
-        if at.square:
-            got = gain_dst(at.xn)
-            remote(got, got, gsend.at[0], grecv.at[0], {"batch": at.xn}).wait_recv()
-            fwd = remote(got, got, gsend.at[2], grecv.at[2], {"batch": at.yn})
-            fwd.start()
-            got = gain_dst(at.yn)
-            remote(got, got, gsend.at[1], grecv.at[1], {"batch": at.yn}).wait_recv()
-            got = gain_dst(at.dg)
-            remote(got, got, gsend.at[2], grecv.at[2], {"batch": at.yn}).wait_recv()
-            first.wait_send()
-            own_y.wait_send()
-            fwd.wait_send()
-        else:
-            for o in range(1, n):
-                got = gain_dst((at.b + n - o) % n)
-                remote(got, got, gsend.at[o], grecv.at[o], {"batch": (at.b + o) % n}).wait_recv()
-                gain_jobs[o - 1].wait_send()
-
-        for job in w_jobs:
-            job.start()
-        for r in range(rows):
-
-            def norm(part, r=r):
-                values = tok[r, part, :].astype(F32)
-                normed[r, part, :] = (values * inv_root_of(values) * gains_full[0:1, :]).astype(BF16)
-
-            chunk_loop(T, 32, norm)
-            in_jobs[r].start()
-        for job in ct_jobs[1:]:
-            job.start()
-        order = [ct_jobs[0]] + in_jobs + ct_jobs[1:]
-        for k in range(1, L):
-            for job in order:
-                job.step(k)
-            for job in {1: w_jobs[:4], 2: w_jobs[4:]}.get(k, ()):
-                job.forward()
-        for job in order + w_jobs:
-            job.finish()
-
-    return pl.pallas_call(
-        kernel,
-        out_shape=(
-            jax.ShapeDtypeStruct((rows, H, T, D), BF16),
-            jax.ShapeDtypeStruct((rows, H, T, D), BF16),
-            jax.ShapeDtypeStruct((n, R, 3 * hw), BF16),
-            jax.ShapeDtypeStruct((n, R, hw), BF16),
-            jax.ShapeDtypeStruct((n, R, 2 * ff), BF16),
-            jax.ShapeDtypeStruct((n, R, ff), BF16),
-            jax.ShapeDtypeStruct((8, D), F32),
-        ),
-        in_specs=[VMEM, ANY, VMEM] + [ANY] * 7,
-        out_specs=(ANY,) * 6 + (VMEM,),
-        scratch_shapes=names.shapes,
-        compiler_params=pltpu.CompilerParams(collective_id=1, has_side_effects=True, vmem_limit_bytes=VMEM_LIMIT),
-        name="gather_all",
-    )(tokens, cotangent, gains, *weights)
 
 
 def far_first(L, z):
@@ -689,7 +582,7 @@
             self.sends.append(now)
             if todo and s >= free:
                 name, needs, makes, i, length = todo[0]
-                if needs is None or self.complete.get(needs, never) <= s:
+                if all(self.complete.get(j, never) <= s for j in needs):
                     self.tasks[s] = todo.pop(0)
                     free = s + length
                     for j in makes:
@@ -699,7 +592,7 @@
         close()
         self.jobs, self.reduces, self.order = jobs, reduces, order
         self.ready, self.arrive, self.own = ready, arrive, own
-        self.slots = 1 + max(list(self.final.values()) + list(self.complete.values()))
+        self.slots = 1 + max(list(self.final.values()) + list(self.complete.values()) + [s + 1 for s in self.tasks])
 
     def block(self, z, i):
         return pick(z, [self.order[q][i] for q in range(self.L)])
@@ -912,35 +805,256 @@
     return back, jnp.sum(grad * unit, axis=0, keepdims=True)
 
 
-def feed_forward(n, H, terms, ct_full, tokens, cotangent, gains, w_gu, w_d):
+def attention_in(n, H, tokens, cotangent, gains, weights, cosine, sine, starts):
+    rows, T, D = tokens.shape
+    R, W = weights[0].shape
+    ff = weights[4].shape[1]
+    L = H // 2
+    S = H * T
+    heads = W // HEAD_DIM
+    rank = [("x", r) for r in range(rows)] + [("ct", 0)]
+    tasks = []
+    for r in range(rows):
+        kinds = ("qkv", "low", "high", "terms") if r + 1 < rows else ("qkv", "heads", "terms")
+        tasks += [((kind, r), (("x", r),), (), 0, 1) for kind in kinds]
+    plan = Plan(L, rank, [], {}, {}, {j: 0 for j in rank}, tasks)
+    names = Names()
+    z_at = [names.add(SlotGather.sems(L)) for _ in range(rows + 1)]
+    w_at = [names.add(BatchGather.sems(n)) for _ in range(6)]
+    g_at = names.add([DMA((n,)), DMA((n,)), DMA])
+    rest = names.add(
+        [
+            pltpu.VMEM((rows, T, D), BF16),
+            pltpu.VMEM((2, 2, T, D), BF16),
+            pltpu.VMEM((2, 2, T, D), BF16),
+            pltpu.VMEM((D, 3 * W), BF16),
+            pltpu.VMEM((D, W), BF16),
+            DMA((2,)),
+            DMA((2,)),
+            DMA((2,)),
+        ]
+    )
+    wide = min(512, D)
+
+    def kernel(
+        tok,
+        ct,
+        gain,
+        cos,
+        sin,
+        st,
+        wq,
+        wk,
+        wv,
+        wo,
+        wg,
+        wu,
+        attn_in,
+        ct_first,
+        w_qkv,
+        w_o,
+        w_gu,
+        terms,
+        gains_full,
+        qkv,
+        lse,
+        attended,
+        *scratch,
+    ):
+        at = Place(n, H)
+        normed, xb, stage, wqkv, wout, x_sem, o_sem, w_sem = scratch[rest]
+        gsend, grecv, glocal = scratch[g_at]
+        at.greet()
+
+        def gain_dst(b):
+            return gains_full.at[:, pl.ds(pl.multiple_of(b * R, R), R)]
+
+        mine = pltpu.make_async_copy(gain, gain_dst(at.b), glocal)
+        mine.start()
+        if at.square:
+            first = remote(gain, gain_dst(at.b), gsend.at[0], grecv.at[0], {"batch": at.xn})
+            own_y = remote(gain, gain_dst(at.b), gsend.at[1], grecv.at[1], {"batch": at.yn})
+            first.start()
+            own_y.start()
+            got = gain_dst(at.xn)
+            remote(got, got, gsend.at[0], grecv.at[0], {"batch": at.xn}).wait_recv()
+            fwd = remote(got, got, gsend.at[2], grecv.at[2], {"batch": at.yn})
+            fwd.start()
+            got = gain_dst(at.yn)
+            remote(got, got, gsend.at[1], grecv.at[1], {"batch": at.yn}).wait_recv()
+            got = gain_dst(at.dg)
+            remote(got, got, gsend.at[2], grecv.at[2], {"batch": at.yn}).wait_recv()
+            for job in (first, own_y, fwd):
+                job.wait_send()
+        else:
+            for o in range(1, n):
+                remote(gain, gain_dst(at.b), gsend.at[o], grecv.at[o], {"batch": (at.b + o) % n}).start()
+            for o in range(1, n):
+                got = gain_dst((at.b + n - o) % n)
+                remote(got, got, gsend.at[o], grecv.at[o], {"batch": (at.b + o) % n}).wait()
+        mine.wait()
+
+        gathers = {("x", r): SlotGather(at, normed.at[r], attn_in.at[r], scratch[z_at[r]]) for r in range(rows)}
+        gathers[("ct", 0)] = SlotGather(at, ct.at[0], ct_first, scratch[z_at[rows]])
+
+        def norm(r):
+            def one(part):
+                values = tok[r, part, :].astype(F32)
+                normed[r, part, :] = (values * inv_root_of(values) * gains_full[0:1, :]).astype(BF16)
+
+            chunk_loop(T, 32, one)
+            gathers[("x", r)].begin()
+
+        outs = []
+        for src, dst, col, width in (
+            (wq, w_qkv, 0, W),
+            (wk, w_qkv, W, W),
+            (wv, w_qkv, 2 * W, W),
+            (wo, w_o, 0, W),
+            (wg, w_gu, 0, ff),
+            (wu, w_gu, ff, ff),
+        ):
+            outs.append((src, lambda b, part, dst=dst, col=col, width=width: dst.at[b, part, pl.ds(col, width)]))
+        shards = [BatchGather(at, src, out, scratch[w_at[i]]) for i, (src, out) in enumerate(outs)]
+        for job in shards[:4]:
+            job.start()
+        for r in range(rows):
+            norm(r)
+        gathers[("ct", 0)].begin()
+
+        def weight_loads():
+            return [
+                pltpu.make_async_copy(w_qkv.at[b], wqkv.at[pl.ds(b * R, R), :], w_sem.at[0]) for b in range(n)
+            ] + [pltpu.make_async_copy(w_o.at[b], wout.at[pl.ds(b * R, R), :], w_sem.at[1]) for b in range(n)]
+
+        def x_load(r, b):
+            return pltpu.make_async_copy(attn_in.at[r, pl.ds(2 * b, 2)], xb.at[b % 2], x_sem.at[b % 2])
+
+        def make_qkv(r):
+            gathers[("x", r)].finish()
+            x_load(r, 0).start()
+            x_load(r, 1).start()
+            if r == 0:
+                pltpu.make_async_copy(wqkv, wqkv, w_sem.at[0]).wait()
+                pltpu.make_async_copy(wout, wout, w_sem.at[1]).wait()
+            for b in range(L):
+                x_load(r, b).wait()
+                part = pl.ds(b * 2 * T, 2 * T)
+                lin = jnp.dot(xb[b % 2].reshape(2 * T, D), wqkv[...], preferred_element_type=F32)
+                if b + 2 < L:
+                    x_load(r, b + 2).start()
+                c, s = cos[r, part, :], sin[r, part, :]
+                qkv[r, part, 0:W] = rotate(lin[:, :W], c, s).astype(BF16)
+                qkv[r, part, W : 2 * W] = rotate(lin[:, W : 2 * W], c, s).astype(BF16)
+                qkv[r, part, 2 * W : 3 * W] = lin[:, 2 * W :].astype(BF16)
+
+        def head(r, h):
+            attend(qkv.at[r], st.at[r], lse.at[r], attended.at[r], h, W)
+
+        def store(r, b):
+            return pltpu.make_async_copy(stage.at[b % 2], terms.at[r, pl.ds(2 * b, 2)], o_sem.at[b % 2])
+
+        def make_terms(r):
+            for b in range(L):
+                if b >= 2:
+                    store(r, b - 2).wait()
+                for j in range(D // wide):
+                    cols = pl.ds(j * wide, wide)
+                    value = cols_dot(attended[r, pl.ds(b * 2 * T, 2 * T), :], wout[cols, :]).astype(BF16)
+                    stage[b % 2, 0, :, cols] = value[:T]
+                    stage[b % 2, 1, :, cols] = value[T:]
+                store(r, b).start()
+            for b in (L - 2, L - 1):
+                store(r, b).wait()
+
+        def task(name):
+            kind, r = name
+            if kind == "qkv":
+                make_qkv(r)
+            elif kind == "low":
+                pl.loop(0, heads // 2)(lambda h: head(r, h))
+            elif kind == "high":
+                pl.loop(heads // 2, heads)(lambda h: head(r, h))
+            elif kind == "heads":
+                pl.loop(0, heads)(lambda h: head(r, h))
+            else:
+                make_terms(r)
+
+        def after(s):
+            if s == 3:
+                for job in shards[:4]:
+                    job.forward()
+                for job in shards[4:]:
+                    job.start()
+            if s == 6:
+                for job in shards[:4]:
+                    job.finish()
+                for job in weight_loads():
+                    job.start()
+            if s == 11:
+                shards[4].forward()
+            if s == 15:
+                shards[5].forward()
+
+        run_plan(plan, at, gathers, task, after, None)
+        gathers[("ct", 0)].finish()
+        for job in shards[4:]:
+            job.finish()
+
+    return pl.pallas_call(
+        kernel,
+        out_shape=(
+            jax.ShapeDtypeStruct((rows, H, T, D), BF16),
+            jax.ShapeDtypeStruct((H, T, D), BF16),
+            jax.ShapeDtypeStruct((n, R, 3 * W), BF16),
+            jax.ShapeDtypeStruct((n, R, W), BF16),
+            jax.ShapeDtypeStruct((n, R, 2 * ff), BF16),
+            jax.ShapeDtypeStruct((rows, H, T, D), BF16),
+            jax.ShapeDtypeStruct((8, D), F32),
+            jax.ShapeDtypeStruct((rows, S, 3 * W), BF16),
+            jax.ShapeDtypeStruct((rows, 8, S), F32),
+            jax.ShapeDtypeStruct((rows, S, W), BF16),
+        ),
+        in_specs=[VMEM, ANY] + [VMEM] * 4 + [ANY] * 6,
+        out_specs=(ANY,) * 6 + (VMEM,) * 4,
+        scratch_shapes=names.shapes,
+        compiler_params=pltpu.CompilerParams(collective_id=1, has_side_effects=True, vmem_limit_bytes=VMEM_LIMIT),
+        name="attention_in",
+    )(tokens, cotangent, gains, cosine, sine, starts, *weights)
+
+
+def feed_forward(n, H, terms, ct_first, tokens, cotangent, gains, w_gu, w_d):
     rows, T, D = tokens.shape
     L = H // 2
     ff = w_d.shape[1]
     S = H * T
-    U = w_d.shape[0] // n // 2
+    R = w_d.shape[0]
+    U = R // 2
     square = n == 4
     rank = []
     for kinds in (("mix", "in"), ("sum", "att"), ("out",)):
         rank += [(kind, r) for r in range(rows) for kind in kinds]
+    rank[2:2] = [("ct", r) for r in range(1, rows)]
     tasks = []
     for r in range(rows):
         for i in range(L):
-            tasks.append((("first", r, i), ("in", r), (), i, 1))
-            tasks.append((("second", r, i), None, (("sum", r), ("out", r)), i, 1))
-    tasks += [(("grad", k, 0), None, (), 0, 1) for k in range(2 * n)]
+            tasks.append((("first", r, i), (("in", r),) + ((("ct", r),) if r else ()), (), i, 1))
+            tasks.append((("second", r, i), (), (("sum", r), ("out", r)), i, 1))
+    tasks += [(("grad", k, 0), (), (), 0, 1) for k in range(2 * n)]
     plan = Plan(
         L,
         rank,
         [j for j in rank if j[0] in ("mix", "sum", "out")],
         {("mix", r): [r * L + i for i in range(L)] for r in range(rows)},
         {(a, r): (b, r) for a, b in (("mix", "in"), ("sum", "att")) for r in range(rows)},
-        {},
+        {("ct", r): 0 for r in range(1, rows)},
         tasks,
     )
     names = Names()
     n_bufs = [names.add(SlotReduce.bufs(L, T, D)) for _ in range(2 * rows)]
     n_sems = [names.add(SlotReduce.sems(L)) for _ in range(2 * rows)]
-    n_gsem = [names.add(SlotGather.sems(L)) for _ in range(rows)]
+    n_gsem = [names.add(SlotGather.sems(L)) for _ in range(2 * rows)]
+    n_wsem = names.add(BatchGather.sems(n))
     rest = names.add(
         [
             pltpu.VMEM((rows, T, D), BF16),
@@ -956,7 +1070,7 @@
             pltpu.VMEM((2, max(2 * T, U), 2 * ff), BF16),
             pltpu.VMEM((2, rows, H, T, U), BF16),
             pltpu.VMEM((2, rows, H, T, U), BF16),
-            DMA((4,)),
+            DMA((6,)),
             DMA((2, 4)),
             DMA((2, 4)),
             DMA((2,)),
@@ -972,12 +1086,13 @@
 
     def kernel(
         src,
-        ctf,
+        ct_row,
         tok,
         ct,
         gain,
         wgu_hbm,
-        wd_hbm,
+        wd_own,
+        ctf,
         mlp_in,
         g_att,
         hid_hbm,
@@ -1017,10 +1132,13 @@
             h_sem,
             g_sem,
         ) = scratch[rest]
-        loads = [
-            pltpu.make_async_copy(wgu_hbm, wgu.at[pl.ds(0, D), :], w_sem.at[0]),
-            pltpu.make_async_copy(wd_hbm, wd.at[pl.ds(0, D), :], w_sem.at[1]),
-        ]
+        loads = [pltpu.make_async_copy(wgu_hbm, wgu.at[pl.ds(0, D), :], w_sem.at[0])]
+        down = BatchGather(
+            at,
+            wd_own,
+            lambda b, part: wd.at[pl.ds(pl.multiple_of(b * R + part.start, U), part.size), :],
+            scratch[n_wsem],
+        )
         red, gat = {}, {}
         for r in range(rows):
             for kind in ("mix", "sum"):
@@ -1028,8 +1146,11 @@
             red[("out", r)] = SlotReduce(at, *scratch[n_bufs[rows + r]], scratch[n_sems[rows + r]])
             gat[("in", r)] = SlotGather(at, normed.at[r], mlp_in.at[r], scratch[n_gsem[r]])
             gat[("att", r)] = SlotGather(at, att.at[r], g_att.at[r], scratch[n_gsem[r]])
+            if r:
+                gat[("ct", r)] = SlotGather(at, ct.at[r], ctf.at[r - 1], scratch[n_gsem[rows + r]])
         both = {**red, **gat}
-        at.greet(batch=square)
+        at.greet()
+        down.start()
 
         def mine_of(r, zd):
             return red[("out", r)].recv.at[zd]
@@ -1045,6 +1166,8 @@
                 zd = plan.block(z, i)
                 exchange(r, zd).start()
                 own_load(r, zd).start()
+        for r in range(1, rows):
+            gat[("ct", r)].begin()
         for job in loads:
             job.start()
         gain_sum[...] = jnp.zeros_like(gain_sum)
@@ -1066,7 +1189,9 @@
             blk = plan.block(z, i)
             return (
                 pltpu.make_async_copy(mlp_in.at[r, pl.ds(2 * blk, 2)], xb.at[i % 2], x_sem.at[i % 2]),
-                pltpu.make_async_copy(ctf.at[r, pl.ds(2 * blk, 2)], cb.at[i % 2], c_sem.at[i % 2]),
+                pltpu.make_async_copy(
+                    (ctf.at[r - 1] if r else ct_row).at[pl.ds(2 * blk, 2)], cb.at[i % 2], c_sem.at[i % 2]
+                ),
             )
 
         def act_store(r, i):
@@ -1080,9 +1205,12 @@
         def first_part(r, i):
             if i == 0:
                 gat[("in", r)].finish()
+                if r:
+                    gat[("ct", r)].finish()
                 for job in x_load(r, 0):
                     job.start()
                 if r == 0:
+                    down.finish()
                     for job in loads:
                         job.wait()
             for job in x_load(r, i):
@@ -1159,19 +1287,7 @@
             red[("out", r)].final(put)
             red[("out", r)].sent()
 
-        if square:
-            units = [
-                ((1 - at.y) * 2 + 1 - at.x, 0, 1 - at.y, at.xn),
-                ((1 - at.y) * 2 + 1 - at.x, 1, 3 - at.x, at.yn),
-                (at.y * 2 + 1 - at.x, 0, at.y, at.xn),
-                ((1 - at.y) * 2 + at.x, 1, 2 + at.x, at.yn),
-                ((1 - at.y) * 2 + at.x, 0, None, None),
-                (at.y * 2 + 1 - at.x, 1, None, None),
-                (at.b, 0, None, None),
-                (at.b, 1, None, None),
-            ]
-        else:
-            units = [(k // 2, k % 2, None, None) for k in range(2 * n)]
+        units = send_units(at, square, n)
         again = [
             pltpu.make_async_copy(ggu_hbm, wgu.at[pl.ds(0, rows * S), :], w_sem.at[0]),
             pltpu.make_async_copy(hid_hbm, wd.at[pl.ds(0, rows * S), :], w_sem.at[1]),
@@ -1181,7 +1297,10 @@
             cols = pl.ds(pl.multiple_of((units[k][0] * 2 + units[k][1]) * U, U), U)
             return [
                 pltpu.make_async_copy(mlp_in.at[:, :, :, cols], xt.at[k % 2], t_sem.at[k % 2]),
-                pltpu.make_async_copy(ctf.at[:, :, :, cols], ct_t.at[k % 2], t_sem.at[2 + k % 2]),
+                pltpu.make_async_copy(ct_row.at[:, :, cols], ct_t.at[k % 2, 0], t_sem.at[2 + k % 2]),
+                pltpu.make_async_copy(
+                    ctf.at[:, :, :, cols], ct_t.at[k % 2, pl.ds(1, rows - 1)], t_sem.at[4 + k % 2]
+                ),
             ]
 
         def grad_store(k):
@@ -1245,6 +1364,8 @@
                 grad(r)
 
         def after(s):
+            if s == 7:
+                down.forward()
             if s + 1 < rows * L:
                 combine_mix((s + 1) // L, (s + 1) % L)
             name = plan.tasks[s - 1][0] if s - 1 in plan.tasks else None
@@ -1272,6 +1393,7 @@
     return pl.pallas_call(
         kernel,
         out_shape=(
+            jax.ShapeDtypeStruct((rows - 1, H, T, D), BF16),
             jax.ShapeDtypeStruct((rows, H, T, D), BF16),
             jax.ShapeDtypeStruct((rows, H, T, D), BF16),
             jax.ShapeDtypeStruct((rows * S, ff), BF16),
@@ -1285,63 +1407,464 @@
             jax.ShapeDtypeStruct((8, D), F32),
         ),
         in_specs=[ANY, ANY, VMEM, VMEM, VMEM, ANY, ANY],
-        out_specs=(ANY,) * 8 + (VMEM, VMEM, VMEM),
+        out_specs=(ANY,) * 9 + (VMEM, VMEM, VMEM),
         scratch_shapes=names.shapes,
         compiler_params=pltpu.CompilerParams(collective_id=2, has_side_effects=True, vmem_limit_bytes=VMEM_LIMIT),
         name="feed_forward",
-    )(terms, ct_full, tokens, cotangent, gains, w_gu, w_d)
-
-
-def last_sums(n, H, terms, tokens, g_mixed, gains, gain_sum, g_qkv, g_o, g_gu, g_d, first_gu, first_d):
+    )(terms, ct_first, tokens, cotangent, gains, w_gu, w_d)
+
+
+class LateReduce:
+    def __init__(self, at, src, first, bufs, sems):
+        self.at, self.src, self.first = at, src, first
+        self.mine, self.came, self.second = bufs
+        self.load, self.send, self.recv = sems
+        self.U = first.shape[1]
+
+    @staticmethod
+    def bufs(U, K):
+        return [pltpu.VMEM((2, U, K), BF16)] * 3
+
+    @staticmethod
+    def sems():
+        return [DMA((4,)), DMA((2,)), DMA((2,))]
+
+    def loads(self, j, own):
+        at, U = self.at, self.U
+        if j == 0:
+            y = at.y if own else 1 - at.y
+            b, slot = y * 2 + at.x, y
+        else:
+            x = at.x if own else 1 - at.x
+            b, slot = at.y * 2 + x, 2 + x
+        return [
+            pltpu.make_async_copy(self.src.at[b, pl.ds(j * U, U), :], self.mine.at[j], self.load.at[2 * j]),
+            pltpu.make_async_copy(self.first.at[slot], self.came.at[j], self.load.at[2 * j + 1]),
+        ]
+
+    def pass_on(self, j):
+        to = {"batch": self.at.xn if j else self.at.yn}
+        return remote(self.mine.at[j], self.second.at[j], self.send.at[j], self.recv.at[j], to)
+
+    def start(self):
+        for j in (0, 1):
+            for job in self.loads(j, False):
+                job.start()
+
+    def second_step(self):
+        for j in (0, 1):
+            for job in self.loads(j, False):
+                job.wait()
+
+            def add(rows, j=j):
+                self.mine[j, rows, :] = (self.mine[j, rows, :].astype(F32) + self.came[j, rows, :].astype(F32)).astype(BF16)
+
+            chunk_loop(self.U, 16, add)
+            self.pass_on(j).start()
+
+    def reload(self):
+        for j in (0, 1):
+            self.pass_on(j).wait()
+            for job in self.loads(j, True):
+                job.start()
+
+    def final(self, j, step, put):
+        for job in self.loads(j, True):
+            job.wait()
+
+        @pl.loop(0, self.U // step)
+        def _(i):
+            rows = pl.ds(pl.multiple_of(i * step, step), step)
+            put(
+                i,
+                self.mine[j, rows, :].astype(F32) + self.came[j, rows, :].astype(F32) + self.second[j, rows, :].astype(F32),
+            )
+
+
+def send_units(at, square, n):
+    if not square:
+        return [(k // 2, k % 2, None, None) for k in range(2 * n)]
+    return [
+        ((1 - at.y) * 2 + 1 - at.x, 0, 1 - at.y, at.xn),
+        ((1 - at.y) * 2 + 1 - at.x, 1, 3 - at.x, at.yn),
+        (at.y * 2 + 1 - at.x, 0, at.y, at.xn),
+        ((1 - at.y) * 2 + at.x, 1, 2 + at.x, at.yn),
+        ((1 - at.y) * 2 + at.x, 0, None, None),
+        (at.y * 2 + 1 - at.x, 1, None, None),
+        (at.b, 0, None, None),
+        (at.b, 1, None, None),
+    ]
+
+
+def attention_back(
+    n,
+    H,
+    g_att,
+    attended,
+    qkv,
+    lse,
+    attn_in,
+    w_qkv,
+    w_o,
+    cosine,
+    sine,
+    starts,
+    tokens,
+    g_mixed,
+    gains,
+    gain_sum,
+    g_gu,
+    g_d,
+    first_gu,
+    first_d,
+):
     rows, T, D = tokens.shape
     L = H // 2
-    R, hw = g_o.shape[1], g_o.shape[2]
-    ff = g_d.shape[2]
+    S = H * T
+    R, ff = g_d.shape[1], g_d.shape[2]
+    W = w_o.shape[1]
+    heads = W // HEAD_DIM
+    U = R // 2
+    square = n == 4
+    step = min(256, S)
+    wide = min(512, D)
+    blocks = S // step
+    rank = [("in", r) for r in range(rows)]
+    tasks = []
+    for r in range(rows):
+        tasks.append((("prob", r, 0), (), (), 0, 1))
+        if r == 0:
+            tasks.append((("heads", r, 0), (), (), 0, 1))
+        else:
+            tasks += [(("head", r, h), (), (), 0, 1) for h in range(heads)]
+        tasks += [(("terms", r, i), (), (("in", r),), i, 1) for i in range(L)]
+    tasks += [(("grad", k, 0), (), (), 0, 1) for k in range(n)]
+    plan = Plan(L, rank, rank, {}, {}, {}, tasks)
     names = Names()
-    r_bufs = [names.add(Reduce.bufs(L, T, D)) for _ in range(rows)]
-    r_sems = [names.add(Reduce.sems(L)) for _ in range(rows)]
-    b_bufs = [names.add(BatchReduce.bufs(n, R, w)) for w in (ff, 2 * ff, hw, 3 * hw)]
-    b_sems = [names.add(BatchReduce.sems(n)) for _ in range(4)]
+    r_bufs = [names.add(SlotReduce.bufs(L, T, D)) for _ in range(rows)]
+    r_sems = [names.add(SlotReduce.sems(L)) for _ in range(rows)]
+    if square:
+        m_bufs = [names.add(LateReduce.bufs(U, K)) for K in (ff, 2 * ff)]
+        m_sems = [names.add(LateReduce.sems()) for _ in range(2)]
+        a_bufs = names.add([pltpu.VMEM((4, U, 4 * W), BF16), pltpu.VMEM((2, U, 4 * W), BF16)])
+        a_sems = names.add([DMA((6,)), DMA((6,))])
+    else:
+        m_bufs = [names.add(BatchReduce.bufs(n, R, K)) for K in (ff, 2 * ff)]
+        m_sems = [names.add(BatchReduce.sems(n)) for _ in range(2)]
+        a_bufs = names.add([pltpu.VMEM((n, 2, U, 4 * W), BF16)])
+        a_sems = names.add([DMA((n,)), DMA((n,))])
     s_at = names.add(
         [pltpu.VMEM((8, D), F32), pltpu.VMEM((n, 8, R), F32), pltpu.VMEM((H, 8, R), F32)]
         + [DMA((n,)), DMA((n,)), DMA((H,)), DMA((H,)), DMA]
     )
-
-    def kernel(src, tok, gmix, gain, gain_in, gqkv, go, ggu, gd, fgu, fd, grad_in, gq, gk, gv, gout, ggate, gup, gdown, gain_out, *scratch):
+    rest = names.add(
+        [
+            pltpu.VMEM((2, step, D), BF16),
+            pltpu.VMEM((S, W), BF16),
+            pltpu.VMEM((S, W), F32),
+            pltpu.VMEM((S, W), F32),
+            pltpu.VMEM((S, W), F32),
+            pltpu.VMEM((rows * S, 3 * W), BF16),
+            pltpu.VMEM((2, 2, T, D), BF16),
+            pltpu.VMEM((2, rows * S, U), BF16),
+            pltpu.VMEM((2, rows * S, U), BF16),
+            pltpu.VMEM((2 * n, U, 4 * W), BF16),
+            pltpu.VMEM((4, 32, 2 * ff), F32),
+            DMA((2,)),
+            DMA((4,)),
+            DMA((4, 2)),
+            DMA,
+        ]
+    )
+
+    def kernel(
+        ga,
+        att,
+        qkv,
+        ls,
+        x_hbm,
+        wq,
+        wo,
+        cos,
+        sin,
+        st,
+        tok,
+        gmix,
+        gain,
+        gain_in,
+        ggu,
+        gd,
+        fgu,
+        fd,
+        grad_in,
+        out_q,
+        out_k,
+        out_v,
+        out_o,
+        ggate,
+        gup,
+        gdown,
+        gain_out,
+        *scratch,
+    ):
         at = Place(n, H)
+        z = at.z
+        small, over_batch, over_head, bsend, brecv, hsend, hrecv, local = scratch[s_at]
+        gab, gat, gq, gk, gv, gqkv, stage, xt, gt, units_buf, out_buf, ga_sem, t_sem, o_sem, mix_sem = scratch[rest]
+        sums = {("in", r): SlotReduce(at, *scratch[r_bufs[r]], scratch[r_sems[r]]) for r in range(rows)}
+        asend, arecv = scratch[a_sems]
+        units = send_units(at, square, n)
+        take_mix = pltpu.make_async_copy(gmix, grad_in, mix_sem)
+        take_mix.start()
+
+        def ga_load(g):
+            return pltpu.make_async_copy(
+                ga.at[g // blocks, pl.ds(g % blocks * step, step), :], gab.at[g % 2], ga_sem.at[g % 2]
+            )
+
+        ga_load(0).start()
+        ga_load(1).start()
         at.greet(all_heads=True)
-        small, over_batch, over_head, bsend, brecv, hsend, hrecv, local = scratch[s_at]
-        sums = [Reduce(at, src.at[r], *scratch[r_bufs[r]], scratch[r_sems[r]]) for r in range(rows)]
-        weights = [
-            BatchReduce(at, s, scratch[b_bufs[i]], scratch[b_sems[i]], first if at.square else None)
-            for i, (s, first) in enumerate(((gd, fd), (ggu, fgu), (go, None), (gqkv, None)))
-        ]
-        for job in sums[:1] + weights + sums[1:]:
+        if square:
+            mlp = [
+                LateReduce(at, src, first, scratch[m_bufs[i]], scratch[m_sems[i]])
+                for i, (src, first) in enumerate(((gd, fd), (ggu, fgu)))
+            ]
+        else:
+            mlp = [BatchReduce(at, src, scratch[m_bufs[i]], scratch[m_sems[i]]) for i, src in enumerate((gd, ggu))]
+        for job in mlp:
             job.start()
-        for job in weights[:2]:
+        small[...] = gain_in[...]
+        for job in mlp:
             job.second_step()
-        small[...] = gain_in[...]
-
-        def finish_sum(r):
+
+        def prob(r):
+            gq[...] = jnp.zeros_like(gq)
+            gk[...] = jnp.zeros_like(gk)
+            gv[...] = jnp.zeros_like(gv)
+            for b in range(blocks):
+                g = r * blocks + b
+                ga_load(g).wait()
+                gat[b * step : (b + 1) * step, :] = jnp.dot(gab[g % 2], wo[...], preferred_element_type=F32).astype(BF16)
+                if g + 2 < rows * blocks:
+                    ga_load(g + 2).start()
+
+        def head(r, h):
+            attend_back(qkv.at[r], st.at[r], ls.at[r], gat, gq, gk, gv, h, W)
+
+        def terms(r, i):
+            zd = plan.block(z, i)
+            k = i % 2
+            part = pl.ds(pl.multiple_of(zd * 2 * T, 2 * T), 2 * T)
+            c, s = cos[r, part, :], -sin[r, part, :]
+            keep = pl.ds(pl.multiple_of(r * S + zd * 2 * T, 2 * T), 2 * T)
+            gqkv[keep, 0:W] = rotate(gq[part, :], c, s).astype(BF16)
+            gqkv[keep, W : 2 * W] = rotate(gk[part, :], c, s).astype(BF16)
+            gqkv[keep, 2 * W : 3 * W] = gv[part, :].astype(BF16)
+
+            @pl.loop(0, D // wide)
+            def _(j):
+                cols = pl.ds(pl.multiple_of(j * wide, wide), wide)
+                back = cols_dot(gqkv[keep, :], wq[cols, :]).astype(BF16)
+                stage[k, 0, :, cols] = back[:T]
+                stage[k, 1, :, cols] = back[T:]
+
+            sums[("in", r)].exchange(zd, stage.at[k, 1 - at.c]).start()
+
+        def combine_terms(r, i):
+            zd = plan.block(z, i)
+            job = sums[("in", r)]
+            job.exchange(zd, stage.at[i % 2, 1 - at.c]).wait()
+            job.combine(zd, stage.at[i % 2, at.c])
+
+        def columns(k):
+            cols = pl.ds(pl.multiple_of((units[k][0] * 2 + units[k][1]) * U, U), U)
+            return [pltpu.make_async_copy(x_hbm.at[:, cols], xt.at[k % 2], t_sem.at[k % 2])] + [
+                pltpu.make_async_copy(
+                    ga.at[r, :, cols], gt.at[k % 2, pl.ds(r * S, S), :], t_sem.at[2 + k % 2]
+                )
+                for r in range(rows)
+            ]
+
+        def columns_wait(k):
+            pltpu.make_async_copy(xt.at[k % 2], xt.at[k % 2], t_sem.at[k % 2]).wait()
+            pltpu.make_async_copy(gt.at[k % 2], gt.at[k % 2], t_sem.at[2 + k % 2]).wait()
+
+        def grad(k):
+            if k == 0:
+                for job in columns(0):
+                    job.start()
+            columns_wait(k)
+            if k + 1 < 2 * n:
+                for job in columns(k + 1):
+                    job.start()
+            units_buf[k, :, 0 : 3 * W] = rows_dot(xt[k % 2], gqkv[...]).astype(BF16)
+            units_buf[k, :, 3 * W : 4 * W] = rows_dot(gt[k % 2], att[...].reshape(rows * S, W)).astype(BF16)
+            if units[k][3] is not None:
+                unit_send(k).start()
+
+        if square:
+            a_first, a_second = scratch[a_bufs]
+
+            def unit_send(k):
+                _, _, slot, to = units[k]
+                return remote(units_buf.at[k], a_first.at[slot], asend.at[k], arecv.at[slot], {"batch": to})
+
+            def unit_pass(j):
+                to = at.xn if j else at.yn
+                return remote(units_buf.at[4 + j], a_second.at[j], asend.at[4 + j], arecv.at[4 + j], {"batch": to})
+
+            def unit_second():
+                for j, k, slot in ((0, 0, 1 - at.y), (1, 1, 3 - at.x)):
+                    unit_send(k).wait_recv()
+
+                    def add(part, j=j, slot=slot):
+                        units_buf[4 + j, part, :] = (
+                            units_buf[4 + j, part, :].astype(F32) + a_first[slot, part, :].astype(F32)
+                        ).astype(BF16)
+
+                    chunk_loop(U, 16, add)
+                    unit_pass(j).start()
+
+            def unit_final(put):
+                for j, k, slot in ((0, 2, at.y), (1, 3, 2 + at.x)):
+                    unit_send(k).wait_recv()
+                    unit_pass(j).wait_recv()
+
+                    @pl.loop(0, U // 16)
+                    def _(i, j=j, slot=slot):
+                        r = pl.multiple_of(i * 16, 16)
+                        part = pl.ds(r, 16)
+                        put(
+                            pl.ds(r + j * U, 16),
+                            units_buf[6 + j, part, :].astype(F32)
+                            + a_first[slot, part, :].astype(F32)
+                            + a_second[j, part, :].astype(F32),
+                        )
+
+                for k in range(4):
+                    unit_send(k).wait_send()
+                for j in (0, 1):
+                    unit_pass(j).wait_send()
+
+        else:
+            (a_slots,) = scratch[a_bufs]
+
+            def unit_direct(off):
+                to = (at.b + off) % n
+                return remote(
+                    units_buf.at[pl.ds(2 * to, 2)], a_slots.at[off], asend.at[off], arecv.at[off], {"batch": to}
+                )
+
+            def unit_second():
+                for off in range(1, n):
+                    unit_direct(off).start()
+
+            def unit_final(put):
+                for off in range(1, n):
+                    unit_direct(off).wait()
+                for j in (0, 1):
+
+                    @pl.loop(0, U // 16)
+                    def _(i, j=j):
+                        r = pl.multiple_of(i * 16, 16)
+                        part = pl.ds(r, 16)
+                        total = units_buf[2 * at.b + j, part, :].astype(F32)
+                        for off in range(1, n):
+                            total = total + a_slots[off, j, part, :].astype(F32)
+                        put(pl.ds(r + j * U, 16), total)
+
+        def finish(j):
+            r = j[1]
+
             def put(part, value):
                 back, gain_part = norm_back_part(tok[r, part, :].astype(F32), gain[0:1, :], value)
-                grad_in[r, part, :] = gmix[r, part, :] + back
+                grad_in[r, part, :] += back
                 small[0:1, :] += gain_part
 
-            sums[r].final(put)
-
-        for k in range(L - 1):
-            sums[0].hops(k)
-        for r in range(rows):
-            if r + 1 < rows:
-                for k in range(L - 1):
-                    sums[r + 1].hops(k, "first")
-            finish_sum(r)
-            if r + 1 < rows:
-                for k in range(L - 1):
-                    sums[r + 1].hops(k, "mid")
-        for job in weights[2:]:
-            job.second_step()
+            sums[j].final(put)
+            sums[j].sent()
+
+        def task(name):
+            kind, r, i = name
+            if kind == "prob":
+                prob(r)
+                if r == 0:
+                    take_mix.wait()
+            elif kind == "heads":
+                pl.loop(0, heads)(lambda h: head(r, h))
+            elif kind == "head":
+                head(r, i)
+            elif kind == "terms":
+                terms(r, i)
+            else:
+                grad(2 * r)
+                grad(2 * r + 1)
+
+        def out_copies(outs, r, ring, step):
+            return [
+                pltpu.make_async_copy(
+                    out_buf.at[ring, pl.ds(0, step), pl.ds(a * ff, ff)], dst.at[pl.ds(r, step), :], o_sem.at[ring, a]
+                )
+                for a, dst in enumerate(outs)
+            ]
+
+        mlp_outs = ((gdown,), (ggate, gup))
+
+        def mlp_half(a, j):
+            step = min(32, U)
+            count = U // step
+            outs = mlp_outs[a]
+
+            def put(i, value):
+                ring = i % 4
+
+                @pl.when(i >= 4)
+                def _():
+                    for copy in out_copies(outs, j * U, ring, step):
+                        copy.wait()
+
+                out_buf[ring, 0:step, 0 : len(outs) * ff] = value
+                for copy in out_copies(outs, pl.multiple_of(j * U + i * step, step), ring, step):
+                    copy.start()
+
+            mlp[a].final(j, step, put)
+            for ring in range(min(4, count)):
+                for copy in out_copies(outs, j * U, ring, step):
+                    copy.wait()
+
+        def mlp_whole(a):
+            outs = mlp_outs[a]
+
+            def put(part, value):
+                out_buf[0, 0:16, 0 : len(outs) * ff] = value
+                for copy in out_copies(outs, part.start, 0, 16):
+                    copy.start()
+                for copy in out_copies(outs, part.start, 0, 16):
+                    copy.wait()
+
+            mlp[a].final(put)
+            mlp[a].finish()
+
+        grads_at = min(s for s, task in plan.tasks.items() if task[0][0] == "grad")
+
+        def after(s):
+            name = plan.tasks[s - 1][0] if s - 1 in plan.tasks else None
+            if name and name[0] == "terms":
+                combine_terms(*name[1:])
+            if square:
+                if s == grads_at + 1:
+                    for job in mlp:
+                        job.reload()
+                if s == grads_at + 2:
+                    mlp_half(0, 0)
+                    mlp_half(0, 1)
+                if s == grads_at + 4:
+                    mlp_half(1, 0)
+            if s == grads_at + n - 1:
+                unit_second()
+
+        run_plan(plan, at, sums, task, after, finish)
 
         def slice_of(b):
             return small.at[:, pl.ds(pl.multiple_of(b * R, R), R)]
@@ -1354,20 +1877,11 @@
             batch_job(off).start()
         mine = pltpu.make_async_copy(slice_of(at.b), over_batch.at[0], local)
         mine.start()
-
-        def put_o(part, value):
-            gout[part, :] = value
-
-        def put_d(part, value):
-            gdown[part, :] = value
-
-        def put_gu(part, value):
-            ggate[part, :] = value[:, :ff]
-            gup[part, :] = value[:, ff:]
-
-        weights[0].final(put_d)
-        weights[1].final(put_gu)
-        weights[2].final(put_o)
+        if square:
+            mlp_half(1, 1)
+        else:
+            mlp_whole(0)
+            mlp_whole(1)
         mine.wait()
         total = over_batch[0]
         for off in range(1, n):
@@ -1382,12 +1896,13 @@
         for off in range(1, H):
             head_job(off, at.h).start()
 
-        def put_qkv(part, value):
-            gq[part, :] = value[:, :hw]
-            gk[part, :] = value[:, hw : 2 * hw]
-            gv[part, :] = value[:, 2 * hw :]
-
-        weights[3].final(put_qkv)
+        def put_units(part, value):
+            out_q[part, :] = value[:, :W]
+            out_k[part, :] = value[:, W : 2 * W]
+            out_v[part, :] = value[:, 2 * W : 3 * W]
+            out_o[part, :] = value[:, 3 * W :]
+
+        unit_final(put_units)
         for off in range(1, H):
             head_job(off, (at.h + H - off) % H).wait_recv()
         total = over_head[0]
@@ -1398,28 +1913,47 @@
             batch_job(off).wait_send()
         for off in range(1, H):
             head_job(off, at.h).wait_send()
-        for job in sums + weights:
-            job.finish()
-
+
+    weight = jax.ShapeDtypeStruct((R, W), F32)
+    wide_weight = jax.ShapeDtypeStruct((R, ff), F32)
     return pl.pallas_call(
         kernel,
         out_shape=(
             jax.ShapeDtypeStruct((rows, T, D), F32),
-            jax.ShapeDtypeStruct((R, hw), F32),
-            jax.ShapeDtypeStruct((R, hw), F32),
-            jax.ShapeDtypeStruct((R, hw), F32),
-            jax.ShapeDtypeStruct((R, hw), F32),
-            jax.ShapeDtypeStruct((R, ff), F32),
-            jax.ShapeDtypeStruct((R, ff), F32),
-            jax.ShapeDtypeStruct((R, ff), F32),
+            weight,
+            weight,
+            weight,
+            weight,
+            wide_weight,
+            wide_weight,
+            wide_weight,
             jax.ShapeDtypeStruct((8, R), F32),
         ),
-        in_specs=[ANY, VMEM, VMEM, VMEM, VMEM] + [ANY] * 6,
-        out_specs=(VMEM,) * 9,
+        in_specs=[ANY, VMEM, VMEM, VMEM, ANY] + [VMEM] * 6 + [ANY, VMEM, VMEM] + [ANY] * 4,
+        out_specs=(VMEM,) * 5 + (ANY,) * 3 + (VMEM,),
         scratch_shapes=names.shapes,
-        compiler_params=pltpu.CompilerParams(collective_id=4, has_side_effects=True, vmem_limit_bytes=VMEM_LIMIT),
-        name="last_sums",
-    )(terms, tokens, g_mixed, gains, gain_sum, g_qkv, g_o, g_gu, g_d, first_gu, first_d)
+        compiler_params=pltpu.CompilerParams(collective_id=4, has_side_effects=True, vmem_limit_bytes=BACK_LIMIT),
+        name="attention_back",
+    )(
+        g_att,
+        attended,
+        qkv,
+        lse,
+        attn_in,
+        w_qkv,
+        w_o,
+        cosine,
+        sine,
+        starts,
+        tokens,
+        g_mixed,
+        gains,
+        gain_sum,
+        g_gu,
+        g_d,
+        first_gu,
+        first_d,
+    )
 
 
 def rows_dot(left, right):
@@ -1503,149 +2037,6 @@
         g_value[0:width, :] += jnp.dot(probs.astype(BF16), back, preferred_element_type=F32)
         g_key[0:width, :] += jnp.dot(g_score, query, preferred_element_type=F32)
         g_query[rows, :] += only_head(rows_dot(g_score, keys) * scale, h)
-
-
-def attention_forward(attn_in, w_qkv, w_o, cosine, sine, starts):
-    rows, S, D = attn_in.shape
-    W = w_o.shape[1]
-    heads = W // HEAD_DIM
-    step = min(256, S)
-
-    def kernel(x, wq, wo, cos, sin, st, qkv, lse, attended, terms):
-        @pl.loop(0, S // step)
-        def _(b):
-            part = pl.ds(pl.multiple_of(b * step, step), step)
-            lin = jnp.dot(x[0, part, :], wq[...], preferred_element_type=F32)
-            c, s = cos[0, part, :], sin[0, part, :]
-            qkv[0, part, 0:W] = rotate(lin[:, :W], c, s).astype(BF16)
-            qkv[0, part, W : 2 * W] = rotate(lin[:, W : 2 * W], c, s).astype(BF16)
-            qkv[0, part, 2 * W : 3 * W] = lin[:, 2 * W :].astype(BF16)
-
-        @pl.loop(0, heads)
-        def _(h):
-            attend(qkv.at[0], st.at[0], lse.at[0], attended.at[0], h, W)
-
-        @pl.loop(0, S // step)
-        def _(b):
-            part = pl.ds(pl.multiple_of(b * step, step), step)
-            terms[0, part, :] = cols_dot(attended[0, part, :], wo[...]).astype(BF16)
-
-    def row(*shape):
-        return pl.BlockSpec((1,) + shape, lambda r: (r, 0, 0))
-
-    return pl.pallas_call(
-        kernel,
-        grid=(rows,),
-        out_shape=(
-            jax.ShapeDtypeStruct((rows, S, 3 * W), BF16),
-            jax.ShapeDtypeStruct((rows, 8, S), F32),
-            jax.ShapeDtypeStruct((rows, S, W), BF16),
-            jax.ShapeDtypeStruct((rows, S, D), BF16),
-        ),
-        in_specs=[
-            row(S, D),
-            pl.BlockSpec((D, 3 * W), lambda r: (0, 0)),
-            pl.BlockSpec((D, W), lambda r: (0, 0)),
-            row(S, 128),
-            row(S, 128),
-            row(1, S),
-        ],
-        out_specs=(row(S, 3 * W), row(8, S), row(S, W), row(S, D)),
-        compiler_params=pltpu.CompilerParams(vmem_limit_bytes=VMEM_LIMIT),
-        name="attention_forward",
-    )(attn_in, w_qkv, w_o, cosine, sine, starts)
-
-
-def attention_backward(g_att, attended, qkv, lse, attn_in, w_qkv, w_o, cosine, sine, starts):
-    rows, S, D = attn_in.shape
-    W = w_o.shape[1]
-    heads = W // HEAD_DIM
-    step = min(256, S)
-    wide = min(512, D)
-
-    def kernel(ga, att, qkv, ls, x, wq, wo, cos, sin, st, terms, grad_qkv, grad_o, gat, gq, gk, gv, gqkv, sum_qkv, sum_o):
-        r = pl.program_id(0)
-
-        @pl.when(r == 0)
-        def _():
-            sum_qkv[...] = jnp.zeros_like(sum_qkv)
-            sum_o[...] = jnp.zeros_like(sum_o)
-
-        gq[...] = jnp.zeros_like(gq)
-        gk[...] = jnp.zeros_like(gk)
-        gv[...] = jnp.zeros_like(gv)
-
-        @pl.loop(0, S // step)
-        def _(b):
-            part = pl.ds(pl.multiple_of(b * step, step), step)
-            gat[part, :] = jnp.dot(ga[0, part, :], wo[...], preferred_element_type=F32).astype(BF16)
-
-        @pl.loop(0, heads)
-        def _(h):
-            attend_back(qkv.at[0], st.at[0], ls.at[0], gat, gq, gk, gv, h, W)
-
-        @pl.loop(0, S // step)
-        def _(b):
-            part = pl.ds(pl.multiple_of(b * step, step), step)
-            c, s = cos[0, part, :], -sin[0, part, :]
-            gqkv[part, 0:W] = rotate(gq[part, :], c, s).astype(BF16)
-            gqkv[part, W : 2 * W] = rotate(gk[part, :], c, s).astype(BF16)
-            gqkv[part, 2 * W : 3 * W] = gv[part, :].astype(BF16)
-            terms[0, part, :] = cols_dot(gqkv[part, :], wq[...]).astype(BF16)
-
-        @pl.loop(0, D // wide)
-        def _(j):
-            cols = pl.ds(pl.multiple_of(j * wide, wide), wide)
-            sum_qkv[:, cols] += rows_dot(gqkv[...], x[0, :, cols])
-            sum_o[:, cols] += rows_dot(att[0], ga[0, :, cols])
-
-        @pl.when(r == rows - 1)
-        def _():
-            @pl.loop(0, D // wide)
-            def _(j):
-                cols = pl.ds(pl.multiple_of(j * wide, wide), wide)
-                grad_qkv[cols, :] = sum_qkv[:, cols].T.astype(BF16)
-                grad_o[cols, :] = sum_o[:, cols].T.astype(BF16)
-
-    def row(*shape):
-        return pl.BlockSpec((1,) + shape, lambda r: (r, 0, 0))
-
-    def whole(*shape):
-        return pl.BlockSpec(shape, lambda r: (0, 0))
-
-    return pl.pallas_call(
-        kernel,
-        grid=(rows,),
-        out_shape=(
-            jax.ShapeDtypeStruct((rows, S, D), BF16),
-            jax.ShapeDtypeStruct((D, 3 * W), BF16),
-            jax.ShapeDtypeStruct((D, W), BF16),
-        ),
-        in_specs=[
-            row(S, D),
-            row(S, W),
-            row(S, 3 * W),
-            row(8, S),
-            row(S, D),
-            whole(D, 3 * W),
-            whole(D, W),
-            row(S, 128),
-            row(S, 128),
-            row(1, S),
-        ],
-        out_specs=(row(S, D), whole(D, 3 * W), whole(D, W)),
-        scratch_shapes=[
-            pltpu.VMEM((S, W), BF16),
-            pltpu.VMEM((S, W), F32),
-            pltpu.VMEM((S, W), F32),
-            pltpu.VMEM((S, W), F32),
-            pltpu.VMEM((S, 3 * W), BF16),
-            pltpu.VMEM((3 * W, D), F32),
-            pltpu.VMEM((W, D), F32),
-        ],
-        compiler_params=pltpu.CompilerParams(vmem_limit_bytes=VMEM_LIMIT),
-        name="attention_backward",
-    )(g_att, attended, qkv, lse, attn_in, w_qkv, w_o, cosine, sine, starts)
 
 
 def per_device(
@@ -1672,29 +2063,38 @@
     shard_gains = jnp.concatenate(
         [attn_gain.astype(F32)[None], mlp_gain.astype(F32)[None], jnp.zeros((6, R), F32)], axis=0
     )
-    attn_in, ct_full, w_qkv, w_o, w_gu, w_d, gains = gather_all(
-        n, H, tokens, cotangent, shard_gains, (w_query, w_key, w_value, w_output, w_gate, w_up, w_down)
+    cosine, sine = rope_tables(position_ids)
+    starts = (jnp.arange(S, dtype=jnp.int32)[None, :] - position_ids)[:, None, :]
+    attn_in, ct_first, w_qkv, w_o, w_gu, terms, gains, qkv, lse, attended = attention_in(
+        n, H, tokens, cotangent, shard_gains, (w_query, w_key, w_value, w_output, w_gate, w_up), cosine, sine, starts
     )
     w_qkv = w_qkv.reshape(D, 3 * hw)
     w_o = w_o.reshape(D, hw)
     w_gu = w_gu.reshape(D, 2 * ff)
-    w_d = w_d.reshape(D, ff)
-
-    cosine, sine = rope_tables(position_ids)
-    starts = (jnp.arange(S, dtype=jnp.int32)[None, :] - position_ids)[:, None, :]
-    qkv, lse, attended, terms = attention_forward(attn_in.reshape(rows, S, D), w_qkv, w_o, cosine, sine, starts)
-    terms = terms.reshape(rows, H, T, D)
-    _, g_att, _, _, grad_gu, grad_d, first_gu, first_d, g_mixed, layer_out, gain_sum = feed_forward(
-        n, H, terms, ct_full, tokens, cotangent, gains, w_gu, w_d
+    _, _, g_att, _, _, grad_gu, grad_d, first_gu, first_d, g_mixed, layer_out, gain_sum = feed_forward(
+        n, H, terms, ct_first, tokens, cotangent, gains, w_gu, w_down
     )
-    in_terms, grad_qkv, grad_o = attention_backward(
-        g_att.reshape(rows, S, D), attended, qkv, lse, attn_in.reshape(rows, S, D), w_qkv, w_o, cosine, sine, starts
-    )
-    in_terms = in_terms.reshape(rows, H, T, D)
-    grad_qkv = grad_qkv.reshape(n, R, 3 * hw)
-    grad_o = grad_o.reshape(n, R, hw)
-    grad_input, grad_q, grad_k, grad_v, grad_out, grad_gate, grad_up, grad_down, gain_grads = last_sums(
-        n, H, in_terms, tokens, g_mixed, gains, gain_sum, grad_qkv, grad_o, grad_gu, grad_d, first_gu, first_d
+    grad_input, grad_q, grad_k, grad_v, grad_out, grad_gate, grad_up, grad_down, gain_grads = attention_back(
+        n,
+        H,
+        g_att.reshape(rows, S, D),
+        attended,
+        qkv,
+        lse,
+        attn_in.reshape(rows * S, D),
+        w_qkv,
+        w_o,
+        cosine,
+        sine,
+        starts,
+        tokens,
+        g_mixed,
+        gains,
+        gain_sum,
+        grad_gu,
+        grad_d,
+        first_gu,
+        first_d,
     )
     return (
         layer_out,

time: 674 us -> 558 us (0.83)
  Pallas kernels: 641 us -> 528 us
    pallas_call x5 -> x3, Pallas kernels: 641 us -> 528 us  [the longest x1 276 us: feed_forward(): pl.pallas_call(kernel, out_shape=(jax.ShapeDtypeStruct((rows - 1, H, T, D...]
where the time goes in v2:
time: 558 us; the launch traced here: 553 us
  Pallas kernels  528 us (95%)
  local copies, waits for them, and re-layouts  14.9 us (3%)
  other arithmetic  9.55 us (2%)
    pallas_call x1, Pallas kernels, feed_forward(): pl.pallas_call(kernel, out_shape=(jax.ShapeDtypeStruct((rows - 1, H, T, D...  276 us
    pallas_call x1, Pallas kernels, attention_in(): pl.pallas_call(kernel, out_shape=(jax.ShapeDtypeStruct((rows, H, T, D), B...  128 us
    pallas_call x1, Pallas kernels, attention_back(): pl.pallas_call(kernel, out_shape=(jax.ShapeDtypeStruct((rows, T, D), F32)...  124 us
    unnamed x23, local copies, waits for them, and re-layouts  12.8 us

profile of v2, /device:TPU:0, one launch (start us, length us, event | category | flops | bytes accessed | tf_op | source)
XLA Modules:
  0.0 553.2 jit_solution(2055653117188669782)
XLA Ops:
  0.7 0.1 pad.10.clone
  0.7 0.7 broadcast_in_dim.27
  1.4 0.7 broadcast_in_dim.28
  2.1 0.7 maximum_maximum_fusion.gain
  2.8 0.8 iota_subtract_fusion
  3.6 0.6 broadcast_in_dim.26.st
  4.2 3.7 fusion
  7.9 3.0 pad_maximum_fusion
  10.9 127.5 %attention_in.1 = (bf16[2,8,128,2048]{3,2,1,0:T(8,128)(2,1)}, bf16[8,128,2048]{2,1,0:T(8,128)(2,1)}, bf16[4,512,768]{2,1,0:T(8,128)(2,1)}, bf16[4,512,256]{2,1,0...) custom-call(bf16[2,128,2048]{2,1,0:T(8,128)(2,1)} %tok.5, ...), custom_call_target="tpu_custom_call" | custom-call | tf_op jit(solution)/shard_map/attention_in/pallas_call | solution.py:1004
  138.4 276.2 %feed_forward.1 = (bf16[1,8,128,2048]{3,2,1,0:T(8,128)(2,1)}, bf16[2,8,128,2048]{3,2,1,0:T(8,128)(2,1)}, bf16[2,8,128,2048]{3,2,1,0:T(8,128)(2,1)}, bf16[2048,10...) custom-call(bf16[2,8,128,2048]{3,2,1,0:T(8,128)(2,1)} %get-tuple-ele, ...), custom_call_target="tpu_custom_call" | custom-call | tf_op jit(solution)/shard_map/feed_forward/pallas_call | solution.py:1393
  414.7 123.9 %attention_back.1 = (f32[2,128,2048]{2,1,0:T(8,128)}, f32[512,256]{1,0:T(8,128)}, f32[512,256]{1,0:T(8,128)}, f32[512,256]{1,0:T(8,128)}, f32[512,256]{1,0:T(8,1...) custom-call(bf16[2,1024,2048]{2,1,0:T(8,128)(2,1)} %bitcast.10, ...), custom_call_target="tpu_custom_call" | custom-call | tf_op jit(solution)/shard_map/attention_back/pallas_call | solution.py:1919
  538.5 0.0 copy-start.6
  538.5 0.0 copy-start.5
  538.6 1.4 fusion.1
  540.0 2.4 copy.32
  542.3 3.3 copy.33
  545.6 0.8 copy.34
  546.4 0.8 copy.35
  547.2 0.8 copy.36
  548.0 0.8 copy.37
  548.8 0.0 copy-done.2
  548.8 1.3 copy.38
  550.1 1.3 copy.39
  551.5 1.3 copy.40
  (13 shorter events, 0.0 us)
Async XLA Ops:
  538.5 7.1 %copy-start.6 = (f32[512,256]{1,0:T(8,128)S(1)}, f32[512,256]{1,0:T(8,128)}, u32[]{:S(2)}) copy-start(f32[512,256]{1,0:T(8,128)} %get-tuple-element.87) | copy-start | bytes 1572868
  538.5 7.9 %copy-start.5 = (f32[512,256]{1,0:T(8,128)S(1)}, f32[512,256]{1,0:T(8,128)}, u32[]{:S(2)}) copy-start(f32[512,256]{1,0:T(8,128)} %get-tuple-element.88) | copy-start | bytes 1572868
  540.0 7.3 %copy-start.4 = (f32[512,256]{1,0:T(8,128)S(1)}, f32[512,256]{1,0:T(8,128)}, u32[]{:S(2)}) copy-start(f32[512,256]{1,0:T(8,128)} %get-tuple-element.89) | copy-start | bytes 1572868
  542.3 5.7 %copy-start.3 = (f32[512,256]{1,0:T(8,128)S(1)}, f32[512,256]{1,0:T(8,128)}, u32[]{:S(2)}) copy-start(f32[512,256]{1,0:T(8,128)} %get-tuple-element.90) | copy-start | bytes 1572868
  542.3 6.5 %copy-start.2 = (f32[512,1024]{1,0:T(8,128)S(1)}, f32[512,1024]{1,0:T(8,128)}, u32[]{:S(2)}) copy-start(f32[512,1024]{1,0:T(8,128)} %get-tuple-element.91) | copy-start | bytes 6291460
  545.6 4.5 copy-start.1
  548.8 2.6 copy-start

commit v3 on v2

--- a/solution.py
+++ b/solution.py
@@ -812,16 +812,22 @@
     L = H // 2
     S = H * T
     heads = W // HEAD_DIM
-    rank = [("x", r) for r in range(rows)] + [("ct", 0)]
+    mix = ("mix", 0)
+    rank = [("x", r) for r in range(rows)] + [("ct", 0), mix]
     tasks = []
     for r in range(rows):
-        kinds = ("qkv", "low", "high", "terms") if r + 1 < rows else ("qkv", "heads", "terms")
-        tasks += [((kind, r), (("x", r),), (), 0, 1) for kind in kinds]
-    plan = Plan(L, rank, [], {}, {}, {j: 0 for j in rank}, tasks)
+        tasks += [((kind, r, 0), (("x", r),), (), 0, 1) for kind in ("qkv", "low", "high")]
+        if r == 0:
+            tasks += [(("send", 0, i), (), (mix,), i, 1) for i in range(L)]
+        else:
+            tasks.append((("terms", r, 0), (), (), 0, 1))
+    plan = Plan(L, rank, [mix], {}, {}, {j: 0 for j in rank if j != mix}, tasks)
     names = Names()
     z_at = [names.add(SlotGather.sems(L)) for _ in range(rows + 1)]
     w_at = [names.add(BatchGather.sems(n)) for _ in range(6)]
     g_at = names.add([DMA((n,)), DMA((n,)), DMA])
+    m_at = names.add(SlotReduce.bufs(L, T, D))
+    ms_at = names.add(SlotReduce.sems(L))
     rest = names.add(
         [
             pltpu.VMEM((rows, T, D), BF16),
@@ -859,6 +865,8 @@
         qkv,
         lse,
         attended,
+        mixed,
+        mid,
         *scratch,
     ):
         at = Place(n, H)
@@ -896,6 +904,7 @@
 
         gathers = {("x", r): SlotGather(at, normed.at[r], attn_in.at[r], scratch[z_at[r]]) for r in range(rows)}
         gathers[("ct", 0)] = SlotGather(at, ct.at[0], ct_first, scratch[z_at[rows]])
+        total = SlotReduce(at, *scratch[m_at], scratch[ms_at])
 
         def norm(r):
             def one(part):
@@ -952,7 +961,7 @@
             attend(qkv.at[r], st.at[r], lse.at[r], attended.at[r], h, W)
 
         def store(r, b):
-            return pltpu.make_async_copy(stage.at[b % 2], terms.at[r, pl.ds(2 * b, 2)], o_sem.at[b % 2])
+            return pltpu.make_async_copy(stage.at[b % 2], terms.at[r - 1, pl.ds(2 * b, 2)], o_sem.at[b % 2])
 
         def make_terms(r):
             for b in range(L):
@@ -967,20 +976,47 @@
             for b in (L - 2, L - 1):
                 store(r, b).wait()
 
+        def make_send(i):
+            zd = plan.block(at.z, i)
+            part = pl.ds(pl.multiple_of(zd * 2 * T, 2 * T), 2 * T)
+            for j in range(D // wide):
+                cols = pl.ds(j * wide, wide)
+                value = cols_dot(attended[0, part, :], wout[cols, :]).astype(BF16)
+                stage[i % 2, 0, :, cols] = value[:T]
+                stage[i % 2, 1, :, cols] = value[T:]
+            total.exchange(zd, stage.at[i % 2, 1 - at.c]).start()
+
+        def combine(i):
+            zd = plan.block(at.z, i)
+            total.exchange(zd, stage.at[i % 2, 1 - at.c]).wait()
+            total.combine(zd, stage.at[i % 2, at.c])
+
+        def finish(j):
+            def put(part, value):
+                value = value + tok[0, part, :].astype(F32)
+                mixed[part, :] = value
+                mid[part, :] = (value * inv_root_of(value) * gains_full[1:2, :]).astype(BF16)
+
+            total.final(put)
+            total.sent()
+
         def task(name):
-            kind, r = name
+            kind, r, i = name
             if kind == "qkv":
                 make_qkv(r)
             elif kind == "low":
                 pl.loop(0, heads // 2)(lambda h: head(r, h))
             elif kind == "high":
                 pl.loop(heads // 2, heads)(lambda h: head(r, h))
-            elif kind == "heads":
-                pl.loop(0, heads)(lambda h: head(r, h))
+            elif kind == "send":
+                make_send(i)
             else:
                 make_terms(r)
 
         def after(s):
+            name = plan.tasks[s - 1][0] if s - 1 in plan.tasks else None
+            if name and name[0] == "send":
+                combine(name[2])
             if s == 3:
                 for job in shards[:4]:
                     job.forward()
@@ -996,7 +1032,7 @@
             if s == 15:
                 shards[5].forward()
 
-        run_plan(plan, at, gathers, task, after, None)
+        run_plan(plan, at, {**gathers, mix: total}, task, after, finish)
         gathers[("ct", 0)].finish()
         for job in shards[4:]:
             job.finish()
@@ -1009,21 +1045,23 @@
             jax.ShapeDtypeStruct((n, R, 3 * W), BF16),
             jax.ShapeDtypeStruct((n, R, W), BF16),
             jax.ShapeDtypeStruct((n, R, 2 * ff), BF16),
-            jax.ShapeDtypeStruct((rows, H, T, D), BF16),
+            jax.ShapeDtypeStruct((rows - 1, H, T, D), BF16),
             jax.ShapeDtypeStruct((8, D), F32),
             jax.ShapeDtypeStruct((rows, S, 3 * W), BF16),
             jax.ShapeDtypeStruct((rows, 8, S), F32),
             jax.ShapeDtypeStruct((rows, S, W), BF16),
+            jax.ShapeDtypeStruct((T, D), F32),
+            jax.ShapeDtypeStruct((T, D), BF16),
         ),
         in_specs=[VMEM, ANY] + [VMEM] * 4 + [ANY] * 6,
-        out_specs=(ANY,) * 6 + (VMEM,) * 4,
+        out_specs=(ANY,) * 6 + (VMEM,) * 6,
         scratch_shapes=names.shapes,
         compiler_params=pltpu.CompilerParams(collective_id=1, has_side_effects=True, vmem_limit_bytes=VMEM_LIMIT),
         name="attention_in",
     )(tokens, cotangent, gains, cosine, sine, starts, *weights)
 
 
-def feed_forward(n, H, terms, ct_first, tokens, cotangent, gains, w_gu, w_d):
+def feed_forward(n, H, terms, ct_first, mixed_first, mid_first, tokens, cotangent, gains, w_gu, w_d):
     rows, T, D = tokens.shape
     L = H // 2
     ff = w_d.shape[1]
@@ -1033,21 +1071,27 @@
     square = n == 4
     rank = []
     for kinds in (("mix", "in"), ("sum", "att"), ("out",)):
-        rank += [(kind, r) for r in range(rows) for kind in kinds]
-    rank[2:2] = [("ct", r) for r in range(1, rows)]
+        rank += [(kind, r) for r in range(rows) for kind in kinds if (kind, r) != ("mix", 0)]
+        if kinds[0] == "mix":
+            rank[2:2] = [("ct", r) for r in range(1, rows)]
     tasks = []
     for r in range(rows):
         for i in range(L):
-            tasks.append((("first", r, i), (("in", r),) + ((("ct", r),) if r else ()), (), i, 1))
-            tasks.append((("second", r, i), (), (("sum", r), ("out", r)), i, 1))
+            needs = (("in", r),) + ((("ct", r),) if r else ())
+            made = (("sum", r), ("out", r))
+            if r and i < L // 2:
+                tasks.append((("both", r, i), needs, made, i, 1))
+            else:
+                tasks.append((("first", r, i), needs, (), i, 1))
+                tasks.append((("second", r, i), (), made, i, 1))
     tasks += [(("grad", k, 0), (), (), 0, 1) for k in range(2 * n)]
     plan = Plan(
         L,
         rank,
         [j for j in rank if j[0] in ("mix", "sum", "out")],
-        {("mix", r): [r * L + i for i in range(L)] for r in range(rows)},
+        {("mix", r): [(r - 1) * L + i for i in range(L)] for r in range(1, rows)},
         {(a, r): (b, r) for a, b in (("mix", "in"), ("sum", "att")) for r in range(rows)},
-        {("ct", r): 0 for r in range(1, rows)},
+        {("in", 0): 0, **{("ct", r): 0 for r in range(1, rows)}},
         tasks,
     )
     names = Names()
@@ -1074,6 +1118,7 @@
             DMA((2, 4)),
             DMA((2, 4)),
             DMA((2,)),
+            DMA((2,)),
             DMA((rows, L)),
             DMA((2,)),
             DMA((2,)),
@@ -1081,12 +1126,14 @@
             DMA((2,)),
         ]
     )
-    tile = min(256, ff)
+    tile = min(512, ff)
     wide = min(512, D)
 
     def kernel(
         src,
         ct_row,
+        mixed_row,
+        mid_row,
         tok,
         ct,
         gain,
@@ -1126,6 +1173,7 @@
             gsend,
             grecv,
             w_sem,
+            row_sem,
             own_sem,
             x_sem,
             c_sem,
@@ -1139,6 +1187,12 @@
             lambda b, part: wd.at[pl.ds(pl.multiple_of(b * R + part.start, U), part.size), :],
             scratch[n_wsem],
         )
+        row_loads = [
+            pltpu.make_async_copy(mixed_row, mixed.at[0], row_sem.at[0]),
+            pltpu.make_async_copy(mid_row, normed.at[0], row_sem.at[1]),
+        ]
+        for job in row_loads:
+            job.start()
         red, gat = {}, {}
         for r in range(rows):
             for kind in ("mix", "sum"):
@@ -1156,12 +1210,15 @@
             return red[("out", r)].recv.at[zd]
 
         def own_load(r, zd):
-            return pltpu.make_async_copy(src.at[r, zd * 2 + at.c], mine_of(r, zd), own_sem.at[r, zd])
+            return pltpu.make_async_copy(src.at[r - 1, zd * 2 + at.c], mine_of(r, zd), own_sem.at[r, zd])
 
         def exchange(r, zd):
-            return red[("mix", r)].exchange(zd, src.at[r, zd * 2 + 1 - at.c])
-
-        for r in range(rows):
+            return red[("mix", r)].exchange(zd, src.at[r - 1, zd * 2 + 1 - at.c])
+
+        for job in row_loads:
+            job.wait()
+        gat[("in", 0)].begin()
+        for r in range(1, rows):
             for i in range(L):
                 zd = plan.block(z, i)
                 exchange(r, zd).start()
@@ -1356,7 +1413,9 @@
             kind, r, i = name
             if kind == "first":
                 first_part(r, i)
-            elif kind == "second":
+            elif kind in ("second", "both"):
+                if kind == "both":
+                    first_part(r, i)
                 second_part(r, i)
                 if (r, i) == (rows - 1, L - 1):
                     prepare_grads()
@@ -1364,12 +1423,12 @@
                 grad(r)
 
         def after(s):
-            if s == 7:
+            if s == 4:
                 down.forward()
-            if s + 1 < rows * L:
-                combine_mix((s + 1) // L, (s + 1) % L)
+            if s + 1 < (rows - 1) * L:
+                combine_mix(1 + (s + 1) // L, (s + 1) % L)
             name = plan.tasks[s - 1][0] if s - 1 in plan.tasks else None
-            if name and name[0] == "second":
+            if name and name[0] in ("second", "both"):
                 combine_terms(*name[1:])
             if name and name[0] == "grad":
                 for job in grad_store(name[1]):
@@ -1381,7 +1440,7 @@
         def finish(j):
             {"mix": finish_mix, "sum": finish_sum, "out": finish_out}[j[0]](j[1])
 
-        combine_mix(0, 0)
+        combine_mix(1, 0)
         run_plan(plan, at, both, task, after, finish)
         if square:
             for k in range(4):
@@ -1406,12 +1465,12 @@
             jax.ShapeDtypeStruct((rows, T, D), BF16),
             jax.ShapeDtypeStruct((8, D), F32),
         ),
-        in_specs=[ANY, ANY, VMEM, VMEM, VMEM, ANY, ANY],
+        in_specs=[ANY, ANY, ANY, ANY, VMEM, VMEM, VMEM, ANY, ANY],
         out_specs=(ANY,) * 9 + (VMEM, VMEM, VMEM),
         scratch_shapes=names.shapes,
         compiler_params=pltpu.CompilerParams(collective_id=2, has_side_effects=True, vmem_limit_bytes=VMEM_LIMIT),
         name="feed_forward",
-    )(terms, ct_first, tokens, cotangent, gains, w_gu, w_d)
+    )(terms, ct_first, mixed_first, mid_first, tokens, cotangent, gains, w_gu, w_d)
 
 
 class LateReduce:
@@ -2039,6 +2098,27 @@
         g_query[rows, :] += only_head(rows_dot(g_score, keys) * scale, h)
 
 
+def hand_out(arrays):
+    count = len(arrays)
+
+    def kernel(*refs):
+        sem = refs[-1]
+        jobs = [pltpu.make_async_copy(refs[i], refs[count + i], sem.at[i]) for i in range(count)]
+        for job in jobs:
+            job.start()
+        for job in jobs:
+            job.wait()
+
+    return pl.pallas_call(
+        kernel,
+        out_shape=tuple(jax.ShapeDtypeStruct(a.shape, a.dtype) for a in arrays),
+        in_specs=[ANY] * count,
+        out_specs=(ANY,) * count,
+        scratch_shapes=[DMA((count,))],
+        name="hand_out",
+    )(*arrays)
+
+
 def per_device(
     n,
     H,
@@ -2065,14 +2145,14 @@
     )
     cosine, sine = rope_tables(position_ids)
     starts = (jnp.arange(S, dtype=jnp.int32)[None, :] - position_ids)[:, None, :]
-    attn_in, ct_first, w_qkv, w_o, w_gu, terms, gains, qkv, lse, attended = attention_in(
+    attn_in, ct_first, w_qkv, w_o, w_gu, terms, gains, qkv, lse, attended, mixed_first, mid_first = attention_in(
         n, H, tokens, cotangent, shard_gains, (w_query, w_key, w_value, w_output, w_gate, w_up), cosine, sine, starts
     )
     w_qkv = w_qkv.reshape(D, 3 * hw)
     w_o = w_o.reshape(D, hw)
     w_gu = w_gu.reshape(D, 2 * ff)
     _, _, g_att, _, _, grad_gu, grad_d, first_gu, first_d, g_mixed, layer_out, gain_sum = feed_forward(
-        n, H, terms, ct_first, tokens, cotangent, gains, w_gu, w_down
+        n, H, terms, ct_first, mixed_first, mid_first, tokens, cotangent, gains, w_gu, w_down
     )
     grad_input, grad_q, grad_k, grad_v, grad_out, grad_gate, grad_up, grad_down, gain_grads = attention_back(
         n,
@@ -2096,19 +2176,10 @@
         first_gu,
         first_d,
     )
-    return (
-        layer_out,
-        grad_input,
-        grad_q,
-        grad_k,
-        grad_v,
-        grad_out,
-        grad_gate,
-        grad_up,
-        grad_down,
-        gain_grads[0],
-        gain_grads[1],
+    results = hand_out(
+        (layer_out, grad_input, grad_q, grad_k, grad_v, grad_out, grad_gate, grad_up, grad_down)
     )
+    return (*results, gain_grads[0], gain_grads[1])
 
 
 def solution(mesh):

time: 558 us -> 872 us (1.56)
  Pallas kernels: 528 us -> 854 us
  local copies, waits for them, and re-layouts: 14.9 us -> 2.06 us
    pallas_call x0 -> x1, Pallas kernels: none -> 351 us  [hand_out(): pl.pallas_call(kernel, out_shape=tuple((jax.ShapeDtypeStruct(a.shape, a.d...]
    pallas_call x1, Pallas kernels: 276 us -> 251 us  [feed_forward(): pl.pallas_call(kernel, out_shape=(jax.ShapeDtypeStruct((rows - 1, H, T, D...]
    unnamed x23 -> x0, local copies, waits for them, and re-layouts: 12.8 us -> none
where the time goes in v3:
time: 872 us; the launch traced here: 867 us
  Pallas kernels  854 us (98%)
  other arithmetic  9.55 us (1%)
    pallas_call x1, Pallas kernels, hand_out(): pl.pallas_call(kernel, out_shape=tuple((jax.ShapeDtypeStruct(a.shape, a.d...  351 us
    pallas_call x1, Pallas kernels, feed_forward(): pl.pallas_call(kernel, out_shape=(jax.ShapeDtypeStruct((rows - 1, H, T, D...  251 us
    pallas_call x1, Pallas kernels, attention_in(): pl.pallas_call(kernel, out_shape=(jax.ShapeDtypeStruct((rows, H, T, D), B...  130 us
    pallas_call x1, Pallas kernels, attention_back(): pl.pallas_call(kernel, out_shape=(jax.ShapeDtypeStruct((rows, T, D), F32)...  122 us

profile of v3, /device:TPU:0, one launch (start us, length us, event | category | flops | bytes accessed | tf_op | source)
XLA Modules:
  0.0 866.7 jit_solution(9094121348490845690)
XLA Ops:
  0.7 0.1 pad.10.clone
  0.7 0.7 broadcast_in_dim.27
  1.4 0.7 broadcast_in_dim.28
  2.1 0.7 maximum_maximum_fusion.gain
  2.8 0.8 iota_subtract_fusion
  3.6 0.6 broadcast_in_dim.26.st
  4.2 3.7 fusion
  7.9 3.0 pad_maximum_fusion
  10.9 130.3 %attention_in.1 = (bf16[2,8,128,2048]{3,2,1,0:T(8,128)(2,1)}, bf16[8,128,2048]{2,1,0:T(8,128)(2,1)}, bf16[4,512,768]{2,1,0:T(8,128)(2,1)}, bf16[4,512,256]{2,1,0...) custom-call(bf16[2,128,2048]{2,1,0:T(8,128)(2,1)} %tok.5, ...), custom_call_target="tpu_custom_call" | custom-call | tf_op jit(solution)/shard_map/attention_in/pallas_call | solution.py:1040
  141.2 251.3 %feed_forward.1 = (bf16[1,8,128,2048]{3,2,1,0:T(8,128)(2,1)}, bf16[2,8,128,2048]{3,2,1,0:T(8,128)(2,1)}, bf16[2,8,128,2048]{3,2,1,0:T(8,128)(2,1)}, bf16[2048,10...) custom-call(bf16[1,8,128,2048]{3,2,1,0:T(8,128)(2,1)} %get-tuple-ele, ...), custom_call_target="tpu_custom_call" | custom-call | tf_op jit(solution)/shard_map/feed_forward/pallas_call | solution.py:1452
  392.4 121.8 %attention_back.1 = (f32[2,128,2048]{2,1,0:T(8,128)}, f32[512,256]{1,0:T(8,128)}, f32[512,256]{1,0:T(8,128)}, f32[512,256]{1,0:T(8,128)}, f32[512,256]{1,0:T(8,1...) custom-call(bf16[2,1024,2048]{2,1,0:T(8,128)(2,1)} %bitcast.10, ...), custom_call_target="tpu_custom_call" | custom-call | tf_op jit(solution)/shard_map/attention_back/pallas_call | solution.py:1978
  514.3 350.6 %hand_out.1 = (bf16[2,128,2048]{2,1,0:T(8,128)(2,1)}, f32[2,128,2048]{2,1,0:T(8,128)}, f32[512,256]{1,0:T(8,128)}, f32[512,256]{1,0:T(8,128)}, f32[512,256]{1,0:...) custom-call(bf16[2,128,2048]{2,1,0:T(8,128)(2,1)} %get-tuple-element.55.refs_0_,, ...), custom_call_target="tpu_custom_call" | custom-call | tf_op jit(solution)/shard_map/hand_out/pallas_call | solution.py:2112
  864.9 1.4 fusion.1
  (2 shorter events, 0.0 us)

commit v4 on v3

--- a/solution.py
+++ b/solution.py
@@ -2,6 +2,7 @@
 
 import jax
 import jax.numpy as jnp
+import numpy as np
 from jax import lax
 from jax.experimental import pallas as pl
 from jax.experimental.pallas import tpu as pltpu
@@ -38,7 +39,7 @@
         self.dg = (1 - self.y) * 2 + (1 - self.x)
         self.square = batch == 4
 
-    def greet(self, line=True, batch=True, all_heads=False):
+    def greet(self, line=True, batch=True, all_heads=False, all_batch=False):
         barrier = pltpu.get_barrier_semaphore()
         me, L = self, self.L
 
@@ -63,7 +64,7 @@
                 hello({"head": me.up})
 
         if batch:
-            if self.square and not all_heads:
+            if self.square and not all_heads and not all_batch:
                 hello({"batch": me.xn})
                 hello({"batch": me.yn})
                 count += 2
@@ -805,7 +806,7 @@
     return back, jnp.sum(grad * unit, axis=0, keepdims=True)
 
 
-def attention_in(n, H, tokens, cotangent, gains, weights, cosine, sine, starts):
+def attention_in(n, H, tokens, cotangent, gains, weights, positions, frequencies):
     rows, T, D = tokens.shape
     R, W = weights[0].shape
     ff = weights[4].shape[1]
@@ -821,7 +822,7 @@
             tasks += [(("send", 0, i), (), (mix,), i, 1) for i in range(L)]
         else:
             tasks.append((("terms", r, 0), (), (), 0, 1))
-    plan = Plan(L, rank, [mix], {}, {}, {j: 0 for j in rank if j != mix}, tasks)
+    plan = Plan(L, rank, [mix], {}, {}, {j: 0 if j[0] == "ct" else 2 for j in rank if j != mix}, tasks)
     names = Names()
     z_at = [names.add(SlotGather.sems(L)) for _ in range(rows + 1)]
     w_at = [names.add(BatchGather.sems(n)) for _ in range(6)]
@@ -846,9 +847,8 @@
         tok,
         ct,
         gain,
-        cos,
-        sin,
-        st,
+        pos,
+        freq,
         wq,
         wk,
         wv,
@@ -867,40 +867,26 @@
         attended,
         mixed,
         mid,
+        cos,
+        sin,
+        st,
         *scratch,
     ):
         at = Place(n, H)
         normed, xb, stage, wqkv, wout, x_sem, o_sem, w_sem = scratch[rest]
         gsend, grecv, glocal = scratch[g_at]
-        at.greet()
+        at.greet(all_batch=True)
 
         def gain_dst(b):
             return gains_full.at[:, pl.ds(pl.multiple_of(b * R, R), R)]
 
-        mine = pltpu.make_async_copy(gain, gain_dst(at.b), glocal)
-        mine.start()
-        if at.square:
-            first = remote(gain, gain_dst(at.b), gsend.at[0], grecv.at[0], {"batch": at.xn})
-            own_y = remote(gain, gain_dst(at.b), gsend.at[1], grecv.at[1], {"batch": at.yn})
-            first.start()
-            own_y.start()
-            got = gain_dst(at.xn)
-            remote(got, got, gsend.at[0], grecv.at[0], {"batch": at.xn}).wait_recv()
-            fwd = remote(got, got, gsend.at[2], grecv.at[2], {"batch": at.yn})
-            fwd.start()
-            got = gain_dst(at.yn)
-            remote(got, got, gsend.at[1], grecv.at[1], {"batch": at.yn}).wait_recv()
-            got = gain_dst(at.dg)
-            remote(got, got, gsend.at[2], grecv.at[2], {"batch": at.yn}).wait_recv()
-            for job in (first, own_y, fwd):
-                job.wait_send()
-        else:
-            for o in range(1, n):
-                remote(gain, gain_dst(at.b), gsend.at[o], grecv.at[o], {"batch": (at.b + o) % n}).start()
-            for o in range(1, n):
-                got = gain_dst((at.b + n - o) % n)
-                remote(got, got, gsend.at[o], grecv.at[o], {"batch": (at.b + o) % n}).wait()
-        mine.wait()
+        def gain_send(off):
+            return remote(gain, gain_dst(at.b), gsend.at[off], grecv.at[off], {"batch": (at.b + off) % n})
+
+        own_gain = pltpu.make_async_copy(gain, gain_dst(at.b), glocal)
+        own_gain.start()
+        for off in range(1, n):
+            gain_send(off).start()
 
         gathers = {("x", r): SlotGather(at, normed.at[r], attn_in.at[r], scratch[z_at[r]]) for r in range(rows)}
         gathers[("ct", 0)] = SlotGather(at, ct.at[0], ct_first, scratch[z_at[rows]])
@@ -925,11 +911,34 @@
         ):
             outs.append((src, lambda b, part, dst=dst, col=col, width=width: dst.at[b, part, pl.ds(col, width)]))
         shards = [BatchGather(at, src, out, scratch[w_at[i]]) for i, (src, out) in enumerate(outs)]
+        gathers[("ct", 0)].begin()
         for job in shards[:4]:
             job.start()
-        for r in range(rows):
-            norm(r)
-        gathers[("ct", 0)].begin()
+
+        def norms():
+            own_gain.wait()
+            for off in range(1, n):
+                got = gain_dst((at.b + n - off) % n)
+                remote(got, got, gsend.at[off], grecv.at[off], {"batch": (at.b + off) % n}).wait()
+            for r in range(rows):
+                norm(r)
+
+        def tables(r):
+            step = 128
+            for i in range(S // step):
+                places = pos[r : r + 1, i * step : (i + 1) * step]
+                index = lax.broadcasted_iota(jnp.int32, places.shape, 1) + i * step
+                st[r, 0:1, i * step : (i + 1) * step] = index - places
+
+            @pl.loop(0, S // step)
+            def _(i):
+                part = pl.ds(pl.multiple_of(i * step, step), step)
+                down = jnp.broadcast_to(pos[r : r + 1, part].astype(F32), (step, step)).T
+                angles = down * freq[...]
+                lane = lax.broadcasted_iota(jnp.int32, angles.shape, 1)
+                cos[r, part, :] = jnp.cos(angles)
+                sine = jnp.sin(angles)
+                sin[r, part, :] = jnp.where(lane % HEAD_DIM < HEAD_DIM // 2, -sine, sine)
 
         def weight_loads():
             return [
@@ -1017,6 +1026,10 @@
             name = plan.tasks[s - 1][0] if s - 1 in plan.tasks else None
             if name and name[0] == "send":
                 combine(name[2])
+            if s == 1:
+                norms()
+            if s - 4 in range(rows):
+                tables(s - 4)
             if s == 3:
                 for job in shards[:4]:
                     job.forward()
@@ -1052,13 +1065,16 @@
             jax.ShapeDtypeStruct((rows, S, W), BF16),
             jax.ShapeDtypeStruct((T, D), F32),
             jax.ShapeDtypeStruct((T, D), BF16),
+            jax.ShapeDtypeStruct((rows, S, 128), F32),
+            jax.ShapeDtypeStruct((rows, S, 128), F32),
+            jax.ShapeDtypeStruct((rows, 1, S), jnp.int32),
         ),
-        in_specs=[VMEM, ANY] + [VMEM] * 4 + [ANY] * 6,
-        out_specs=(ANY,) * 6 + (VMEM,) * 6,
+        in_specs=[VMEM, VMEM] + [VMEM] * 3 + [ANY] * 6,
+        out_specs=(ANY,) * 6 + (VMEM,) * 9,
         scratch_shapes=names.shapes,
         compiler_params=pltpu.CompilerParams(collective_id=1, has_side_effects=True, vmem_limit_bytes=VMEM_LIMIT),
         name="attention_in",
-    )(tokens, cotangent, gains, cosine, sine, starts, *weights)
+    )(tokens, cotangent, gains, positions, frequencies, *weights)
 
 
 def feed_forward(n, H, terms, ct_first, mixed_first, mid_first, tokens, cotangent, gains, w_gu, w_d):
@@ -2026,14 +2042,6 @@
 QUERIES = 256
 
 
-def rope_tables(positions):
-    half_dim = HEAD_DIM // 2
-    frequency = rope_base ** (-(jnp.arange(half_dim).astype(F32) * 2.0) / HEAD_DIM)
-    angles = positions.astype(F32)[:, :, None] * frequency
-    cosine, sine = jnp.cos(angles), jnp.sin(angles)
-    return jnp.concatenate([cosine] * 4, axis=-1), jnp.concatenate([-sine, sine] * 2, axis=-1)
-
-
 def rotate(values, cosine, sine):
     half_dim = HEAD_DIM // 2
     parts = []
@@ -2102,11 +2110,15 @@
     count = len(arrays)
 
     def kernel(*refs):
-        sem = refs[-1]
-        jobs = [pltpu.make_async_copy(refs[i], refs[count + i], sem.at[i]) for i in range(count)]
-        for job in jobs:
+        held, sem_in, sem_out = refs[2 * count : 3 * count], refs[-2], refs[-1]
+        take = [pltpu.make_async_copy(refs[i], held[i], sem_in.at[i]) for i in range(count)]
+        give = [pltpu.make_async_copy(held[i], refs[count + i], sem_out.at[i]) for i in range(count)]
+        for job in take:
             job.start()
-        for job in jobs:
+        for i in range(count):
+            take[i].wait()
+            give[i].start()
+        for job in give:
             job.wait()
 
     return pl.pallas_call(
@@ -2114,7 +2126,8 @@
         out_shape=tuple(jax.ShapeDtypeStruct(a.shape, a.dtype) for a in arrays),
         in_specs=[ANY] * count,
         out_specs=(ANY,) * count,
-        scratch_shapes=[DMA((count,))],
+        scratch_shapes=[pltpu.VMEM(a.shape, a.dtype) for a in arrays] + [DMA((count,))] * 2,
+        compiler_params=pltpu.CompilerParams(vmem_limit_bytes=VMEM_LIMIT),
         name="hand_out",
     )(*arrays)
 
@@ -2143,10 +2156,35 @@
     shard_gains = jnp.concatenate(
         [attn_gain.astype(F32)[None], mlp_gain.astype(F32)[None], jnp.zeros((6, R), F32)], axis=0
     )
-    cosine, sine = rope_tables(position_ids)
-    starts = (jnp.arange(S, dtype=jnp.int32)[None, :] - position_ids)[:, None, :]
-    attn_in, ct_first, w_qkv, w_o, w_gu, terms, gains, qkv, lse, attended, mixed_first, mid_first = attention_in(
-        n, H, tokens, cotangent, shard_gains, (w_query, w_key, w_value, w_output, w_gate, w_up), cosine, sine, starts
+    half_dim = HEAD_DIM // 2
+    frequencies = jnp.asarray(
+        np.tile(rope_base ** (-(np.arange(half_dim) * 2.0) / HEAD_DIM), 4).astype(np.float32)[None]
+    )
+    (
+        attn_in,
+        ct_first,
+        w_qkv,
+        w_o,
+        w_gu,
+        terms,
+        gains,
+        qkv,
+        lse,
+        attended,
+        mixed_first,
+        mid_first,
+        cosine,
+        sine,
+        starts,
+    ) = attention_in(
+        n,
+        H,
+        tokens,
+        cotangent,
+        shard_gains,
+        (w_query, w_key, w_value, w_output, w_gate, w_up),
+        position_ids,
+        frequencies,
     )
     w_qkv = w_qkv.reshape(D, 3 * hw)
     w_o = w_o.reshape(D, hw)

time: 872 us -> 522 us (0.60)
  Pallas kernels: 854 us -> 509 us
    pallas_call x1, Pallas kernels: 351 us -> 8.13 us  [hand_out(): pl.pallas_call(kernel, out_shape=tuple((jax.ShapeDtypeStruct(a.shape, a.d...]
where the time goes in v4:
time: 522 us; the launch traced here: 513 us
  Pallas kernels  509 us (98%)
    pallas_call x1, Pallas kernels, feed_forward(): pl.pallas_call(kernel, out_shape=(jax.ShapeDtypeStruct((rows - 1, H, T, D...  252 us
    pallas_call x1, Pallas kernels, attention_in(): pl.pallas_call(kernel, out_shape=(jax.ShapeDtypeStruct((rows, H, T, D), B...  127 us
    pallas_call x1, Pallas kernels, attention_back(): pl.pallas_call(kernel, out_shape=(jax.ShapeDtypeStruct((rows, T, D), F32)...  121 us

profile of v4, /device:TPU:0, one launch (start us, length us, event | category | flops | bytes accessed | tf_op | source)
XLA Modules:
  0.0 513.3 jit_solution(11375250846701981100)
XLA Ops:
  0.7 0.1 pad.2.clone
  0.7 0.7 broadcast_in_dim.20
  1.4 0.7 broadcast_in_dim.21
  2.1 0.7 maximum_maximum_fusion.gain
  2.8 127.4 %attention_in.1 = (bf16[2,8,128,2048]{3,2,1,0:T(8,128)(2,1)}, bf16[8,128,2048]{2,1,0:T(8,128)(2,1)}, bf16[4,512,768]{2,1,0:T(8,128)(2,1)}, bf16[4,512,256]{2,1,0...) custom-call(bf16[2,128,2048]{2,1,0:T(8,128)(2,1)} %tok.5, ...), custom_call_target="tpu_custom_call" | custom-call | tf_op jit(solution)/shard_map/attention_in/pallas_call | solution.py:1053
  130.2 251.9 %feed_forward.1 = (bf16[1,8,128,2048]{3,2,1,0:T(8,128)(2,1)}, bf16[2,8,128,2048]{3,2,1,0:T(8,128)(2,1)}, bf16[2,8,128,2048]{3,2,1,0:T(8,128)(2,1)}, bf16[2048,10...) custom-call(bf16[1,8,128,2048]{3,2,1,0:T(8,128)(2,1)} %get-tuple-ele, ...), custom_call_target="tpu_custom_call" | custom-call | tf_op jit(solution)/shard_map/feed_forward/pallas_call | solution.py:1468
  382.1 121.2 %attention_back.1 = (f32[2,128,2048]{2,1,0:T(8,128)}, f32[512,256]{1,0:T(8,128)}, f32[512,256]{1,0:T(8,128)}, f32[512,256]{1,0:T(8,128)}, f32[512,256]{1,0:T(8,1...) custom-call(bf16[2,1024,2048]{2,1,0:T(8,128)(2,1)} %bitcast.10, ...), custom_call_target="tpu_custom_call" | custom-call | tf_op jit(solution)/shard_map/attention_back/pallas_call | solution.py:1994
  503.3 8.1 %hand_out.1 = (bf16[2,128,2048]{2,1,0:T(8,128)(2,1)}, f32[2,128,2048]{2,1,0:T(8,128)}, f32[512,256]{1,0:T(8,128)}, f32[512,256]{1,0:T(8,128)}, f32[512,256]{1,0:...) custom-call(bf16[2,128,2048]{2,1,0:T(8,128)(2,1)} %get-tuple-element.58.refs_0_,, ...), custom_call_target="tpu_custom_call" | custom-call | tf_op jit(solution)/shard_map/hand_out/pallas_call | solution.py:2124
  511.5 1.4 fusion
  (1 shorter events, 0.0 us)

commit v5 on v4

--- a/solution.py
+++ b/solution.py
@@ -1087,14 +1087,19 @@
     square = n == 4
     rank = []
     for kinds in (("mix", "in"), ("sum", "att"), ("out",)):
-        rank += [(kind, r) for r in range(rows) for kind in kinds if (kind, r) != ("mix", 0)]
+        rank += [
+            (kind, r)
+            for r in range(rows)
+            for kind in kinds
+            if (kind, r) not in (("mix", 0), ("att", rows - 1), ("out", rows - 1))
+        ]
         if kinds[0] == "mix":
             rank[2:2] = [("ct", r) for r in range(1, rows)]
     tasks = []
     for r in range(rows):
         for i in range(L):
             needs = (("in", r),) + ((("ct", r),) if r else ())
-            made = (("sum", r), ("out", r))
+            made = (("sum", r), ("out", r)) if r + 1 < rows else (("sum", r),)
             if r and i < L // 2:
                 tasks.append((("both", r, i), needs, made, i, 1))
             else:
@@ -1106,19 +1111,20 @@
         rank,
         [j for j in rank if j[0] in ("mix", "sum", "out")],
         {("mix", r): [(r - 1) * L + i for i in range(L)] for r in range(1, rows)},
-        {(a, r): (b, r) for a, b in (("mix", "in"), ("sum", "att")) for r in range(rows)},
+        {**{("mix", r): ("in", r) for r in range(1, rows)}, **{("sum", r): ("att", r) for r in range(rows - 1)}},
         {("in", 0): 0, **{("ct", r): 0 for r in range(1, rows)}},
         tasks,
     )
     names = Names()
-    n_bufs = [names.add(SlotReduce.bufs(L, T, D)) for _ in range(2 * rows)]
-    n_sems = [names.add(SlotReduce.sems(L)) for _ in range(2 * rows)]
+    n_bufs = [names.add(SlotReduce.bufs(L, T, D)) for _ in range(2 * rows - 1)]
+    n_sems = [names.add(SlotReduce.sems(L)) for _ in range(2 * rows - 1)]
     n_gsem = [names.add(SlotGather.sems(L)) for _ in range(2 * rows)]
     n_wsem = names.add(BatchGather.sems(n))
     rest = names.add(
         [
             pltpu.VMEM((rows, T, D), BF16),
-            pltpu.VMEM((rows, T, D), BF16),
+            pltpu.VMEM((rows - 1, T, D), BF16),
+            pltpu.VMEM((rows - 1, L, T, D), BF16),
             pltpu.VMEM((rows, T, D), F32),
             pltpu.VMEM((2, 2, T, D), BF16),
             pltpu.VMEM((2, 2, T, D), BF16),
@@ -1131,8 +1137,9 @@
             pltpu.VMEM((2, rows, H, T, U), BF16),
             pltpu.VMEM((2, rows, H, T, U), BF16),
             DMA((6,)),
-            DMA((2, 4)),
-            DMA((2, 4)),
+            DMA((2, 2)),
+            DMA((2, 2)),
+            DMA((2,)),
             DMA((2,)),
             DMA((2,)),
             DMA((rows, L)),
@@ -1164,8 +1171,11 @@
         grad_d,
         first_gu,
         first_d,
+        out_terms,
         g_mixed,
         layer_out,
+        mixed_last,
+        att_last,
         gain_sum,
         *scratch,
     ):
@@ -1174,6 +1184,7 @@
         (
             normed,
             att,
+            own_terms,
             mixed,
             stage_g,
             stage_o,
@@ -1188,6 +1199,7 @@
             t_sem,
             gsend,
             grecv,
+            last_sem,
             w_sem,
             row_sem,
             own_sem,
@@ -1213,9 +1225,11 @@
         for r in range(rows):
             for kind in ("mix", "sum"):
                 red[(kind, r)] = SlotReduce(at, *scratch[n_bufs[r]], scratch[n_sems[r]])
-            red[("out", r)] = SlotReduce(at, *scratch[n_bufs[rows + r]], scratch[n_sems[rows + r]])
+            if r + 1 < rows:
+                red[("out", r)] = SlotReduce(at, *scratch[n_bufs[rows + r]], scratch[n_sems[rows + r]])
             gat[("in", r)] = SlotGather(at, normed.at[r], mlp_in.at[r], scratch[n_gsem[r]])
-            gat[("att", r)] = SlotGather(at, att.at[r], g_att.at[r], scratch[n_gsem[r]])
+            if r + 1 < rows:
+                gat[("att", r)] = SlotGather(at, att.at[r], g_att.at[r], scratch[n_gsem[r]])
             if r:
                 gat[("ct", r)] = SlotGather(at, ct.at[r], ctf.at[r - 1], scratch[n_gsem[rows + r]])
         both = {**red, **gat}
@@ -1223,7 +1237,7 @@
         down.start()
 
         def mine_of(r, zd):
-            return red[("out", r)].recv.at[zd]
+            return own_terms.at[r - 1, zd]
 
         def own_load(r, zd):
             return pltpu.make_async_copy(src.at[r - 1, zd * 2 + at.c], mine_of(r, zd), own_sem.at[r, zd])
@@ -1251,9 +1265,18 @@
             exchange(r, zd).wait()
             red[("mix", r)].combine(zd, mine_of(r, zd))
 
+        def kinds_of(r):
+            return (("sum", stage_g), ("out", stage_o)) if r + 1 < rows else (("sum", stage_g),)
+
+        def last_store(i):
+            zd = plan.block(z, i)
+            return pltpu.make_async_copy(stage_o.at[i % 2], out_terms.at[pl.ds(2 * zd, 2)], last_sem.at[i % 2])
+
         def combine_terms(r, i):
             zd = plan.block(z, i)
-            for kind, stage in (("sum", stage_g), ("out", stage_o)):
+            if r + 1 == rows:
+                last_store(i).wait()
+            for kind, stage in kinds_of(r):
                 job = red[(kind, r)]
                 job.exchange(zd, stage.at[i % 2, 1 - at.c]).wait()
                 job.combine(zd, stage.at[i % 2, at.c])
@@ -1328,13 +1351,17 @@
                 stage_o[k, 1, :, cols] = out[T:]
 
             zd = plan.block(z, i)
-            for kind, stage in (("sum", stage_g), ("out", stage_o)):
+            if r + 1 == rows:
+                last_store(i).start()
+            for kind, stage in kinds_of(r):
                 red[(kind, r)].exchange(zd, stage.at[k, 1 - at.c]).start()
 
         def finish_mix(r):
             def put(part, value):
                 value = value + tok[r, part, :].astype(F32)
                 mixed[r, part, :] = value
+                if r + 1 == rows:
+                    mixed_last[part, :] = value
                 normed[r, part, :] = (value * inv_root_of(value) * gain[1:2, :]).astype(BF16)
 
             red[("mix", r)].final(put)
@@ -1346,12 +1373,16 @@
                 back, gain_part = norm_back_part(mixed[r, part, :], gain[1:2, :], value)
                 total = ct[r, part, :].astype(F32) + back
                 g_mixed[r, part, :] = total
-                att[r, part, :] = total.astype(BF16)
+                if r + 1 < rows:
+                    att[r, part, :] = total.astype(BF16)
+                else:
+                    att_last[part, :] = total.astype(BF16)
                 gain_sum[1:2, :] += gain_part
 
             red[("sum", r)].final(put)
             red[("sum", r)].sent()
-            gat[("att", r)].begin()
+            if r + 1 < rows:
+                gat[("att", r)].begin()
 
         def finish_out(r):
             def put(part, value):
@@ -1385,10 +1416,10 @@
             ]
 
         def grad_sends(k):
-            b, half, slot, to = units[k]
+            b, half, _, to = units[k]
             part = pl.ds(half * U, U)
             return [
-                remote(src.at[b, part, :], dst.at[slot], gsend.at[a, k], grecv.at[a, slot], {"batch": to})
+                remote(src.at[b, part, :], dst.at[k], gsend.at[a, k], grecv.at[a, k], {"batch": to})
                 for a, (src, dst) in enumerate(((grad_d, first_d), (grad_gu, first_gu)))
             ]
 
@@ -1449,7 +1480,7 @@
             if name and name[0] == "grad":
                 for job in grad_store(name[1]):
                     job.wait()
-                if units[name[1]][3] is not None:
+                if square and name[1] < 2:
                     for job in grad_sends(name[1]):
                         job.start()
 
@@ -1459,10 +1490,10 @@
         combine_mix(1, 0)
         run_plan(plan, at, both, task, after, finish)
         if square:
-            for k in range(4):
+            for k in range(2):
                 for job in grad_sends(k):
                     job.wait()
-        for r in range(rows):
+        for r in range(rows - 1):
             gat[("att", r)].finish()
 
     return pl.pallas_call(
@@ -1470,19 +1501,22 @@
         out_shape=(
             jax.ShapeDtypeStruct((rows - 1, H, T, D), BF16),
             jax.ShapeDtypeStruct((rows, H, T, D), BF16),
-            jax.ShapeDtypeStruct((rows, H, T, D), BF16),
+            jax.ShapeDtypeStruct((rows - 1, H, T, D), BF16),
             jax.ShapeDtypeStruct((rows * S, ff), BF16),
             jax.ShapeDtypeStruct((rows * S, 2 * ff), BF16),
             jax.ShapeDtypeStruct((n, 2 * U, 2 * ff), BF16),
             jax.ShapeDtypeStruct((n, 2 * U, ff), BF16),
-            jax.ShapeDtypeStruct((4, U, 2 * ff), BF16),
-            jax.ShapeDtypeStruct((4, U, ff), BF16),
+            jax.ShapeDtypeStruct((2, U, 2 * ff), BF16),
+            jax.ShapeDtypeStruct((2, U, ff), BF16),
+            jax.ShapeDtypeStruct((H, T, D), BF16),
             jax.ShapeDtypeStruct((rows, T, D), F32),
-            jax.ShapeDtypeStruct((rows, T, D), BF16),
+            jax.ShapeDtypeStruct((rows - 1, T, D), BF16),
+            jax.ShapeDtypeStruct((T, D), F32),
+            jax.ShapeDtypeStruct((T, D), BF16),
             jax.ShapeDtypeStruct((8, D), F32),
         ),
         in_specs=[ANY, ANY, ANY, ANY, VMEM, VMEM, VMEM, ANY, ANY],
-        out_specs=(ANY,) * 9 + (VMEM, VMEM, VMEM),
+        out_specs=(ANY,) * 10 + (VMEM,) * 5,
         scratch_shapes=names.shapes,
         compiler_params=pltpu.CompilerParams(collective_id=2, has_side_effects=True, vmem_limit_bytes=VMEM_LIMIT),
         name="feed_forward",
@@ -1490,45 +1524,59 @@
 
 
 class LateReduce:
-    def __init__(self, at, src, first, bufs, sems):
-        self.at, self.src, self.first = at, src, first
-        self.mine, self.came, self.second = bufs
+    def __init__(self, at, src, first, parts, bufs, sems):
+        self.at, self.src, self.first, self.parts = at, src, first, parts
+        if at.square:
+            self.mine, self.came = bufs
         self.load, self.send, self.recv = sems
-        self.U = first.shape[1]
+        self.U = src.shape[1] // 2
 
     @staticmethod
-    def bufs(U, K):
-        return [pltpu.VMEM((2, U, K), BF16)] * 3
+    def bufs(n, U, K):
+        return [pltpu.VMEM((2, U, K), BF16)] * 2 if n == 4 else []
 
     @staticmethod
-    def sems():
-        return [DMA((4,)), DMA((2,)), DMA((2,))]
-
-    def loads(self, j, own):
+    def sems(n):
+        m = 4 if n == 4 else n
+        return [DMA((4,)), DMA((m,)), DMA((m,))]
+
+    def loads(self, j):
         at, U = self.at, self.U
-        if j == 0:
-            y = at.y if own else 1 - at.y
-            b, slot = y * 2 + at.x, y
-        else:
-            x = at.x if own else 1 - at.x
-            b, slot = at.y * 2 + x, 2 + x
+        b = at.y * 2 + 1 - at.x if j else (1 - at.y) * 2 + at.x
         return [
             pltpu.make_async_copy(self.src.at[b, pl.ds(j * U, U), :], self.mine.at[j], self.load.at[2 * j]),
-            pltpu.make_async_copy(self.first.at[slot], self.came.at[j], self.load.at[2 * j + 1]),
+            pltpu.make_async_copy(self.first.at[j], self.came.at[j], self.load.at[2 * j + 1]),
         ]
 
     def pass_on(self, j):
         to = {"batch": self.at.xn if j else self.at.yn}
-        return remote(self.mine.at[j], self.second.at[j], self.send.at[j], self.recv.at[j], to)
+        dst = self.parts.at[1, pl.ds(j * self.U, self.U), :]
+        return remote(self.mine.at[j], dst, self.send.at[j], self.recv.at[j], to)
+
+    def rest(self, j):
+        at, rows = self.at, pl.ds(j * self.U, self.U)
+        b = (1 - at.y) * 2 + at.x if j else at.y * 2 + 1 - at.x
+        to = {"batch": at.yn if j else at.xn}
+        return remote(self.src.at[b, rows, :], self.parts.at[0, rows, :], self.send.at[2 + j], self.recv.at[2 + j], to)
+
+    def direct(self, off):
+        to = (self.at.b + off) % self.at.n
+        return remote(self.src.at[to], self.parts.at[off - 1], self.send.at[off], self.recv.at[off], {"batch": to})
 
     def start(self):
+        if self.at.square:
+            for j in (0, 1):
+                for job in self.loads(j):
+                    job.start()
+        else:
+            for off in range(1, self.at.n):
+                self.direct(off).start()
+
+    def second_step(self):
+        if not self.at.square:
+            return
         for j in (0, 1):
-            for job in self.loads(j, False):
-                job.start()
-
-    def second_step(self):
-        for j in (0, 1):
-            for job in self.loads(j, False):
+            for job in self.loads(j):
                 job.wait()
 
             def add(rows, j=j):
@@ -1536,24 +1584,17 @@
 
             chunk_loop(self.U, 16, add)
             self.pass_on(j).start()
-
-    def reload(self):
         for j in (0, 1):
-            self.pass_on(j).wait()
-            for job in self.loads(j, True):
-                job.start()
-
-    def final(self, j, step, put):
-        for job in self.loads(j, True):
-            job.wait()
-
-        @pl.loop(0, self.U // step)
-        def _(i):
-            rows = pl.ds(pl.multiple_of(i * step, step), step)
-            put(
-                i,
-                self.mine[j, rows, :].astype(F32) + self.came[j, rows, :].astype(F32) + self.second[j, rows, :].astype(F32),
-            )
+            self.rest(j).start()
+
+    def finish(self):
+        if self.at.square:
+            for j in (0, 1):
+                self.pass_on(j).wait()
+                self.rest(j).wait()
+        else:
+            for off in range(1, self.at.n):
+                self.direct(off).wait()
 
 
 def send_units(at, square, n):
@@ -1571,10 +1612,17 @@
     ]
 
 
+def BACK_RANK(last):
+    return [("att", last), ("out", last)] + [("in", r) for r in range(last + 1)]
+
+
 def attention_back(
     n,
     H,
     g_att,
+    att_last,
+    out_terms,
+    mixed_last,
     attended,
     qkv,
     lse,
@@ -1601,31 +1649,34 @@
     heads = W // HEAD_DIM
     U = R // 2
     square = n == 4
-    step = min(256, S)
+    step = 2 * T
     wide = min(512, D)
-    blocks = S // step
-    rank = [("in", r) for r in range(rows)]
+    blocks = L
+    last = rows - 1
+    gather, out = ("att", last), ("out", last)
+    rank = BACK_RANK(last)
     tasks = []
     for r in range(rows):
-        tasks.append((("prob", r, 0), (), (), 0, 1))
+        tasks.append((("prob", r, 0), (gather,) if r == last else (), (), 0, 1))
         if r == 0:
             tasks.append((("heads", r, 0), (), (), 0, 1))
         else:
             tasks += [(("head", r, h), (), (), 0, 1) for h in range(heads)]
         tasks += [(("terms", r, i), (), (("in", r),), i, 1) for i in range(L)]
     tasks += [(("grad", k, 0), (), (), 0, 1) for k in range(n)]
-    plan = Plan(L, rank, rank, {}, {}, {}, tasks)
+    plan = Plan(L, rank, [j for j in rank if j != gather], {out: list(range(L))}, {}, {gather: 0}, tasks)
+    P = 2 if square else n - 1
     names = Names()
     r_bufs = [names.add(SlotReduce.bufs(L, T, D)) for _ in range(rows)]
     r_sems = [names.add(SlotReduce.sems(L)) for _ in range(rows)]
+    o_sems = names.add(SlotReduce.sems(L))
+    l_sems = names.add(SlotGather.sems(L))
+    m_bufs = [names.add(LateReduce.bufs(n, U, K)) for K in (ff, 2 * ff)]
+    m_sems = [names.add(LateReduce.sems(n)) for _ in range(2)]
     if square:
-        m_bufs = [names.add(LateReduce.bufs(U, K)) for K in (ff, 2 * ff)]
-        m_sems = [names.add(LateReduce.sems()) for _ in range(2)]
         a_bufs = names.add([pltpu.VMEM((4, U, 4 * W), BF16), pltpu.VMEM((2, U, 4 * W), BF16)])
         a_sems = names.add([DMA((6,)), DMA((6,))])
     else:
-        m_bufs = [names.add(BatchReduce.bufs(n, R, K)) for K in (ff, 2 * ff)]
-        m_sems = [names.add(BatchReduce.sems(n)) for _ in range(2)]
         a_bufs = names.add([pltpu.VMEM((n, 2, U, 4 * W), BF16)])
         a_sems = names.add([DMA((n,)), DMA((n,))])
     s_at = names.add(
@@ -1634,7 +1685,8 @@
     )
     rest = names.add(
         [
-            pltpu.VMEM((2, step, D), BF16),
+            pltpu.VMEM((2, 2, T, D), BF16),
+            pltpu.VMEM((2, T, D), BF16),
             pltpu.VMEM((S, W), BF16),
             pltpu.VMEM((S, W), F32),
             pltpu.VMEM((S, W), F32),
@@ -1642,18 +1694,21 @@
             pltpu.VMEM((rows * S, 3 * W), BF16),
             pltpu.VMEM((2, 2, T, D), BF16),
             pltpu.VMEM((2, rows * S, U), BF16),
-            pltpu.VMEM((2, rows * S, U), BF16),
+            pltpu.VMEM((2, rows, H, T, U), BF16),
             pltpu.VMEM((2 * n, U, 4 * W), BF16),
-            pltpu.VMEM((4, 32, 2 * ff), F32),
             DMA((2,)),
-            DMA((4,)),
-            DMA((4, 2)),
+            DMA((6,)),
+            DMA((L,)),
             DMA,
+            pltpu.SemaphoreType.REGULAR,
         ]
     )
 
     def kernel(
-        ga,
+        ga_first,
+        att_own,
+        oterms,
+        mix_last,
         att,
         qkv,
         ls,
@@ -1676,37 +1731,62 @@
         out_k,
         out_v,
         out_o,
-        ggate,
-        gup,
-        gdown,
+        layer_last,
+        ga_last,
+        parts_d,
+        parts_gu,
         gain_out,
         *scratch,
     ):
         at = Place(n, H)
         z = at.z
         small, over_batch, over_head, bsend, brecv, hsend, hrecv, local = scratch[s_at]
-        gab, gat, gq, gk, gv, gqkv, stage, xt, gt, units_buf, out_buf, ga_sem, t_sem, o_sem, mix_sem = scratch[rest]
+        gab, land, gat, gq, gk, gv, gqkv, stage, xt, gt, units_buf, ga_sem, t_sem, own_sem, mix_sem, free = scratch[rest]
         sums = {("in", r): SlotReduce(at, *scratch[r_bufs[r]], scratch[r_sems[r]]) for r in range(rows)}
+        sums[out] = SlotReduce(at, *scratch[r_bufs[last]], scratch[o_sems])
+        late = SlotGather(at, att_own, ga_last, scratch[l_sems])
         asend, arecv = scratch[a_sems]
         units = send_units(at, square, n)
         take_mix = pltpu.make_async_copy(gmix, grad_in, mix_sem)
         take_mix.start()
 
+        def rows_of(r):
+            return ga_last if r == last else ga_first.at[r]
+
         def ga_load(g):
             return pltpu.make_async_copy(
-                ga.at[g // blocks, pl.ds(g % blocks * step, step), :], gab.at[g % 2], ga_sem.at[g % 2]
+                rows_of(g // blocks).at[pl.ds(g % blocks * 2, 2)], gab.at[g % 2], ga_sem.at[g % 2]
             )
+
+        def own_load(i):
+            zd = plan.block(z, i)
+            return pltpu.make_async_copy(oterms.at[zd * 2 + at.c], land.at[i % 2], own_sem.at[i])
+
+        def out_exchange(i):
+            zd = plan.block(z, i)
+            return sums[out].exchange(zd, oterms.at[zd * 2 + 1 - at.c])
 
         ga_load(0).start()
         ga_load(1).start()
+        own_load(0).start()
+        own_load(1).start()
         at.greet(all_heads=True)
-        if square:
-            mlp = [
-                LateReduce(at, src, first, scratch[m_bufs[i]], scratch[m_sems[i]])
-                for i, (src, first) in enumerate(((gd, fd), (ggu, fgu)))
-            ]
-        else:
-            mlp = [BatchReduce(at, src, scratch[m_bufs[i]], scratch[m_sems[i]]) for i, src in enumerate((gd, ggu))]
+        late.begin()
+        for i in range(L):
+            out_exchange(i).start()
+
+        def combine_out(i):
+            zd = plan.block(z, i)
+            own_load(i).wait()
+            out_exchange(i).wait()
+            sums[out].combine(zd, land.at[i % 2])
+            if i + 2 < L:
+                own_load(i + 2).start()
+
+        mlp = [
+            LateReduce(at, src, first, parts, scratch[m_bufs[i]], scratch[m_sems[i]])
+            for i, (src, first, parts) in enumerate(((gd, fd, parts_d), (ggu, fgu, parts_gu)))
+        ]
         for job in mlp:
             job.start()
         small[...] = gain_in[...]
@@ -1717,11 +1797,17 @@
             gq[...] = jnp.zeros_like(gq)
             gk[...] = jnp.zeros_like(gk)
             gv[...] = jnp.zeros_like(gv)
+            if r == last:
+                late.finish()
+                ga_load(r * blocks).start()
+                ga_load(r * blocks + 1).start()
             for b in range(blocks):
                 g = r * blocks + b
                 ga_load(g).wait()
-                gat[b * step : (b + 1) * step, :] = jnp.dot(gab[g % 2], wo[...], preferred_element_type=F32).astype(BF16)
-                if g + 2 < rows * blocks:
+                gat[b * step : (b + 1) * step, :] = jnp.dot(
+                    gab[g % 2].reshape(step, D), wo[...], preferred_element_type=F32
+                ).astype(BF16)
+                if b + 2 < blocks or (r + 1 < last and g + 2 < rows * blocks):
                     ga_load(g + 2).start()
 
         def head(r, h):
@@ -1730,6 +1816,8 @@
         def terms(r, i):
             zd = plan.block(z, i)
             k = i % 2
+            if r == last and i == 0:
+                pl.semaphore_wait(free, 1 + jnp.minimum(z, 1) + jnp.minimum(L - 1 - z, 1))
             part = pl.ds(pl.multiple_of(zd * 2 * T, 2 * T), 2 * T)
             c, s = cos[r, part, :], -sin[r, part, :]
             keep = pl.ds(pl.multiple_of(r * S + zd * 2 * T, 2 * T), 2 * T)
@@ -1755,9 +1843,7 @@
         def columns(k):
             cols = pl.ds(pl.multiple_of((units[k][0] * 2 + units[k][1]) * U, U), U)
             return [pltpu.make_async_copy(x_hbm.at[:, cols], xt.at[k % 2], t_sem.at[k % 2])] + [
-                pltpu.make_async_copy(
-                    ga.at[r, :, cols], gt.at[k % 2, pl.ds(r * S, S), :], t_sem.at[2 + k % 2]
-                )
+                pltpu.make_async_copy(rows_of(r).at[:, :, cols], gt.at[k % 2, r], t_sem.at[2 + k % 2])
                 for r in range(rows)
             ]
 
@@ -1774,7 +1860,7 @@
                 for job in columns(k + 1):
                     job.start()
             units_buf[k, :, 0 : 3 * W] = rows_dot(xt[k % 2], gqkv[...]).astype(BF16)
-            units_buf[k, :, 3 * W : 4 * W] = rows_dot(gt[k % 2], att[...].reshape(rows * S, W)).astype(BF16)
+            units_buf[k, :, 3 * W : 4 * W] = rows_dot(gt[k % 2].reshape(rows * S, U), att[...].reshape(rows * S, W)).astype(BF16)
             if units[k][3] is not None:
                 unit_send(k).start()
 
@@ -1851,6 +1937,24 @@
 
         def finish(j):
             r = j[1]
+            if j == out:
+
+                def put_layer(part, value):
+                    layer_last[part, :] = (mix_last[part, :] + value).astype(BF16)
+
+                sums[j].final(put_layer)
+                sums[j].sent()
+                pl.semaphore_signal(free, inc=1, device_id={"head": at.sib}, device_id_type=MESH)
+
+                @pl.when(z > 0)
+                def _():
+                    pl.semaphore_signal(free, inc=1, device_id={"head": at.down}, device_id_type=MESH)
+
+                @pl.when(z < L - 1)
+                def _():
+                    pl.semaphore_signal(free, inc=1, device_id={"head": at.up}, device_id_type=MESH)
+
+                return
 
             def put(part, value):
                 back, gain_part = norm_back_part(tok[r, part, :].astype(F32), gain[0:1, :], value)
@@ -1876,70 +1980,19 @@
                 grad(2 * r)
                 grad(2 * r + 1)
 
-        def out_copies(outs, r, ring, step):
-            return [
-                pltpu.make_async_copy(
-                    out_buf.at[ring, pl.ds(0, step), pl.ds(a * ff, ff)], dst.at[pl.ds(r, step), :], o_sem.at[ring, a]
-                )
-                for a, dst in enumerate(outs)
-            ]
-
-        mlp_outs = ((gdown,), (ggate, gup))
-
-        def mlp_half(a, j):
-            step = min(32, U)
-            count = U // step
-            outs = mlp_outs[a]
-
-            def put(i, value):
-                ring = i % 4
-
-                @pl.when(i >= 4)
-                def _():
-                    for copy in out_copies(outs, j * U, ring, step):
-                        copy.wait()
-
-                out_buf[ring, 0:step, 0 : len(outs) * ff] = value
-                for copy in out_copies(outs, pl.multiple_of(j * U + i * step, step), ring, step):
-                    copy.start()
-
-            mlp[a].final(j, step, put)
-            for ring in range(min(4, count)):
-                for copy in out_copies(outs, j * U, ring, step):
-                    copy.wait()
-
-        def mlp_whole(a):
-            outs = mlp_outs[a]
-
-            def put(part, value):
-                out_buf[0, 0:16, 0 : len(outs) * ff] = value
-                for copy in out_copies(outs, part.start, 0, 16):
-                    copy.start()
-                for copy in out_copies(outs, part.start, 0, 16):
-                    copy.wait()
-
-            mlp[a].final(put)
-            mlp[a].finish()
-
         grads_at = min(s for s, task in plan.tasks.items() if task[0][0] == "grad")
 
         def after(s):
             name = plan.tasks[s - 1][0] if s - 1 in plan.tasks else None
+            if s + 1 < L:
+                combine_out(s + 1)
             if name and name[0] == "terms":
                 combine_terms(*name[1:])
-            if square:
-                if s == grads_at + 1:
-                    for job in mlp:
-                        job.reload()
-                if s == grads_at + 2:
-                    mlp_half(0, 0)
-                    mlp_half(0, 1)
-                if s == grads_at + 4:
-                    mlp_half(1, 0)
             if s == grads_at + n - 1:
                 unit_second()
 
-        run_plan(plan, at, sums, task, after, finish)
+        combine_out(0)
+        run_plan(plan, at, {**sums, gather: late}, task, after, finish)
 
         def slice_of(b):
             return small.at[:, pl.ds(pl.multiple_of(b * R, R), R)]
@@ -1952,11 +2005,6 @@
             batch_job(off).start()
         mine = pltpu.make_async_copy(slice_of(at.b), over_batch.at[0], local)
         mine.start()
-        if square:
-            mlp_half(1, 1)
-        else:
-            mlp_whole(0)
-            mlp_whole(1)
         mine.wait()
         total = over_batch[0]
         for off in range(1, n):
@@ -1988,9 +2036,10 @@
             batch_job(off).wait_send()
         for off in range(1, H):
             head_job(off, at.h).wait_send()
+        for job in mlp:
+            job.finish()
 
     weight = jax.ShapeDtypeStruct((R, W), F32)
-    wide_weight = jax.ShapeDtypeStruct((R, ff), F32)
     return pl.pallas_call(
         kernel,
         out_shape=(
@@ -1999,18 +2048,22 @@
             weight,
             weight,
             weight,
-            wide_weight,
-            wide_weight,
-            wide_weight,
+            jax.ShapeDtypeStruct((T, D), BF16),
+            jax.ShapeDtypeStruct((H, T, D), BF16),
+            jax.ShapeDtypeStruct((P, R, ff), BF16),
+            jax.ShapeDtypeStruct((P, R, 2 * ff), BF16),
             jax.ShapeDtypeStruct((8, R), F32),
         ),
-        in_specs=[ANY, VMEM, VMEM, VMEM, ANY] + [VMEM] * 6 + [ANY, VMEM, VMEM] + [ANY] * 4,
-        out_specs=(VMEM,) * 5 + (ANY,) * 3 + (VMEM,),
+        in_specs=[ANY, VMEM, ANY, VMEM] + [VMEM] * 3 + [ANY] + [VMEM] * 6 + [ANY, VMEM, VMEM] + [ANY] * 4,
+        out_specs=(VMEM,) * 6 + (ANY,) * 3 + (VMEM,),
         scratch_shapes=names.shapes,
         compiler_params=pltpu.CompilerParams(collective_id=4, has_side_effects=True, vmem_limit_bytes=BACK_LIMIT),
         name="attention_back",
     )(
         g_att,
+        att_last,
+        out_terms,
+        mixed_last,
         attended,
         qkv,
         lse,
@@ -2106,30 +2159,95 @@
         g_query[rows, :] += only_head(rows_dot(g_score, keys) * scale, h)
 
 
-def hand_out(arrays):
+def hand_out(layer_first, layer_last, arrays, grad_d, grad_gu, parts_d, parts_gu):
+    _, R, ff = grad_d.shape
+    P = parts_d.shape[0]
+    lead, T, D = layer_first.shape
     count = len(arrays)
 
     def kernel(*refs):
-        held, sem_in, sem_out = refs[2 * count : 3 * count], refs[-2], refs[-1]
-        take = [pltpu.make_async_copy(refs[i], held[i], sem_in.at[i]) for i in range(count)]
-        give = [pltpu.make_async_copy(held[i], refs[count + i], sem_out.at[i]) for i in range(count)]
+        first_in, last_in = refs[:2]
+        plain = refs[2 : 2 + count]
+        gd, ggu, pd, pgu = refs[2 + count : 6 + count]
+        outs = refs[6 + count : 10 + 2 * count]
+        held = refs[10 + 2 * count : 10 + 3 * count]
+        layer, own_d, own_gu, more_d, more_gu, sum_d, sum_g, sum_u, sem, out_sem = refs[10 + 3 * count :]
+        b = lax.axis_index("batch")
+        take = [
+            pltpu.make_async_copy(gd.at[b], own_d, sem.at[0]),
+            pltpu.make_async_copy(pd, more_d, sem.at[1]),
+            pltpu.make_async_copy(ggu.at[b], own_gu, sem.at[2]),
+            pltpu.make_async_copy(pgu, more_gu, sem.at[3]),
+            pltpu.make_async_copy(first_in, layer.at[pl.ds(0, lead)], sem.at[4]),
+            pltpu.make_async_copy(last_in, layer.at[lead], sem.at[5]),
+        ] + [pltpu.make_async_copy(plain[i], held[i], sem.at[6 + i]) for i in range(count)]
+        sources = [layer, *held, sum_g, sum_u, sum_d]
+        give = [pltpu.make_async_copy(src, dst, out_sem.at[i]) for i, (src, dst) in enumerate(zip(sources, outs))]
         for job in take:
             job.start()
+
+        def total(own, more, rows):
+            value = own[rows, :].astype(F32)
+            for p in range(P):
+                value = value + more[p, rows, :].astype(F32)
+            return value
+
+        take[0].wait()
+        take[1].wait()
+
+        def down(rows):
+            sum_d[rows, :] = total(own_d, more_d, rows)
+
+        chunk_loop(R, 16, down)
+        give[3 + count].start()
+        take[2].wait()
+        take[3].wait()
+
+        def gate_up(rows):
+            value = total(own_gu, more_gu, rows)
+            sum_g[rows, :] = value[:, :ff]
+            sum_u[rows, :] = value[:, ff:]
+
+        chunk_loop(R, 16, gate_up)
+        give[1 + count].start()
+        give[2 + count].start()
+        take[4].wait()
+        take[5].wait()
+        give[0].start()
         for i in range(count):
-            take[i].wait()
-            give[i].start()
+            take[6 + i].wait()
+            give[1 + i].start()
         for job in give:
             job.wait()
 
+    wide = jax.ShapeDtypeStruct((R, ff), F32)
     return pl.pallas_call(
         kernel,
-        out_shape=tuple(jax.ShapeDtypeStruct(a.shape, a.dtype) for a in arrays),
-        in_specs=[ANY] * count,
-        out_specs=(ANY,) * count,
-        scratch_shapes=[pltpu.VMEM(a.shape, a.dtype) for a in arrays] + [DMA((count,))] * 2,
+        out_shape=(
+            jax.ShapeDtypeStruct((lead + 1, T, D), BF16),
+            *(jax.ShapeDtypeStruct(a.shape, a.dtype) for a in arrays),
+            wide,
+            wide,
+            wide,
+        ),
+        in_specs=[ANY] * (6 + count),
+        out_specs=(ANY,) * (4 + count),
+        scratch_shapes=[pltpu.VMEM(a.shape, a.dtype) for a in arrays]
+        + [
+            pltpu.VMEM((lead + 1, T, D), BF16),
+            pltpu.VMEM((R, ff), BF16),
+            pltpu.VMEM((R, 2 * ff), BF16),
+            pltpu.VMEM((P, R, ff), BF16),
+            pltpu.VMEM((P, R, 2 * ff), BF16),
+            pltpu.VMEM((R, ff), F32),
+            pltpu.VMEM((R, ff), F32),
+            pltpu.VMEM((R, ff), F32),
+            DMA((6 + count,)),
+            DMA((4 + count,)),
+        ],
         compiler_params=pltpu.CompilerParams(vmem_limit_bytes=VMEM_LIMIT),
         name="hand_out",
-    )(*arrays)
+    )(layer_first, layer_last, *arrays, grad_d, grad_gu, parts_d, parts_gu)
 
 
 def per_device(
@@ -2189,13 +2307,30 @@
     w_qkv = w_qkv.reshape(D, 3 * hw)
     w_o = w_o.reshape(D, hw)
     w_gu = w_gu.reshape(D, 2 * ff)
-    _, _, g_att, _, _, grad_gu, grad_d, first_gu, first_d, g_mixed, layer_out, gain_sum = feed_forward(
-        n, H, terms, ct_first, mixed_first, mid_first, tokens, cotangent, gains, w_gu, w_down
-    )
-    grad_input, grad_q, grad_k, grad_v, grad_out, grad_gate, grad_up, grad_down, gain_grads = attention_back(
+    (
+        _,
+        _,
+        g_att,
+        _,
+        _,
+        grad_gu,
+        grad_d,
+        first_gu,
+        first_d,
+        out_terms,
+        g_mixed,
+        layer_first,
+        mixed_last,
+        att_last,
+        gain_sum,
+    ) = feed_forward(n, H, terms, ct_first, mixed_first, mid_first, tokens, cotangent, gains, w_gu, w_down)
+    grad_input, grad_q, grad_k, grad_v, grad_o, layer_last, _, parts_d, parts_gu, gain_grads = attention_back(
         n,
         H,
-        g_att.reshape(rows, S, D),
+        g_att,
+        att_last,
+        out_terms,
+        mixed_last,
         attended,
         qkv,
         lse,
@@ -2215,7 +2350,7 @@
         first_d,
     )
     results = hand_out(
-        (layer_out, grad_input, grad_q, grad_k, grad_v, grad_out, grad_gate, grad_up, grad_down)
+        layer_first, layer_last, (grad_input, grad_q, grad_k, grad_v, grad_o), grad_d, grad_gu, parts_d, parts_gu
     )
     return (*results, gain_grads[0], gain_grads[1])
 

time: 522 us -> 516 us (0.989)
  Pallas kernels: 509 us -> 503 us
    pallas_call x1, Pallas kernels: 252 us -> 218 us  [feed_forward(): pl.pallas_call(kernel, out_shape=(jax.ShapeDtypeStruct((rows - 1, H, T, D...]
    pallas_call x1, Pallas kernels: 121 us -> 149 us  [attention_back(): pl.pallas_call(kernel, out_shape=(jax.ShapeDtypeStruct((rows, T, D), F32)...]
where the time goes in v5:
time: 516 us; the launch traced here: 508 us
  Pallas kernels  503 us (97%)
    pallas_call x1, Pallas kernels, feed_forward(): pl.pallas_call(kernel, out_shape=(jax.ShapeDtypeStruct((rows - 1, H, T, D...  218 us
    pallas_call x1, Pallas kernels, attention_back(): pl.pallas_call(kernel, out_shape=(jax.ShapeDtypeStruct((rows, T, D), F32)...  149 us
    pallas_call x1, Pallas kernels, attention_in(): pl.pallas_call(kernel, out_shape=(jax.ShapeDtypeStruct((rows, H, T, D), B...  127 us

profile of v5, /device:TPU:0, one launch (start us, length us, event | category | flops | bytes accessed | tf_op | source)
XLA Modules:
  0.0 507.8 jit_solution(11320662919049406180)
XLA Ops:
  0.7 0.1 pad.2.clone
  0.7 0.7 broadcast_in_dim.20
  1.4 0.7 broadcast_in_dim.21
  2.1 0.7 maximum_maximum_fusion.gain
  2.8 127.3 %attention_in.1 = (bf16[2,8,128,2048]{3,2,1,0:T(8,128)(2,1)}, bf16[8,128,2048]{2,1,0:T(8,128)(2,1)}, bf16[4,512,768]{2,1,0:T(8,128)(2,1)}, bf16[4,512,256]{2,1,0...) custom-call(bf16[2,128,2048]{2,1,0:T(8,128)(2,1)} %tok.5, ...), custom_call_target="tpu_custom_call" | custom-call | tf_op jit(solution)/shard_map/attention_in/pallas_call | solution.py:1053
  130.1 218.0 %feed_forward.1 = (bf16[1,8,128,2048]{3,2,1,0:T(8,128)(2,1)}, bf16[2,8,128,2048]{3,2,1,0:T(8,128)(2,1)}, bf16[1,8,128,2048]{3,2,1,0:T(8,128)(2,1)}, bf16[2048,10...) custom-call(bf16[1,8,128,2048]{3,2,1,0:T(8,128)(2,1)} %get-tuple-ele, ...), custom_call_target="tpu_custom_call" | custom-call | tf_op jit(solution)/shard_map/feed_forward/pallas_call | solution.py:1499
  348.1 148.8 %attention_back.1 = (f32[2,128,2048]{2,1,0:T(8,128)}, f32[512,256]{1,0:T(8,128)}, f32[512,256]{1,0:T(8,128)}, f32[512,256]{1,0:T(8,128)}, f32[512,256]{1,0:T(8,1...) custom-call(bf16[1,8,128,2048]{3,2,1,0:T(8,128)(2,1)} %get-tuple-ele, ...), custom_call_target="tpu_custom_call" | custom-call | tf_op jit(solution)/shard_map/attention_back/pallas_call | solution.py:2043
  496.9 9.2 %hand_out.1 = (bf16[2,128,2048]{2,1,0:T(8,128)(2,1)}, f32[2,128,2048]{2,1,0:T(8,128)}, f32[512,256]{1,0:T(8,128)}, f32[512,256]{1,0:T(8,128)}, f32[512,256]{1,0:...) custom-call(bf16[1,128,2048]{2,1,0:T(8,128)(2,1)} %get-tuple-element.61.refs_0_,, ...), custom_call_target="tpu_custom_call" | custom-call | tf_op jit(solution)/shard_map/hand_out/pallas_call | solution.py:2224
  506.1 1.4 fusion
  (1 shorter events, 0.0 us)
